TPU v7x, 32 devices: a whole 2x2x4 slice. The times are simulated.
32 devices in a mesh: cells: 8 (over z, y), genes: 4 (over x, core).
Axes of the slice: x: 2, y: 2, z: 4, core: 2. Of those that a mesh axis runs over, the one named last changes fastest.
Arguments:
- counts: bfloat16 [1024, 16384], P('cells', 'genes'), may hold values from 0 to 254
- occupancy: int32 [8, 128], P('cells', 'genes'), may hold values 0 or 1
- start_basis: bfloat16 [64, 16384], P(None, 'genes'), may hold values from -0.046875 to 0.046875
Outputs:
- new_basis: float32 [64, 16384], P(None, ('genes', 'cells'))
All inputs are finite; a program needn't handle non-finite values. No bound on the sum of `occupancy` on one device may be relied on, other than what follows from the above.
Results may differ from a plain program's by a relative error of at most 0.01.
Values sent between devices are 32-bit elements; how exact they have to be, the bound alone decides.
No kernel may reach another device: no remote copies, remote signals or barrier semaphores. Data moves between devices by JAX's collectives and lax.ppermute only.
A program may use at most 64 MiB of HBM per device.

v0:
```python
import functools
import math

import jax
import jax.numpy as jnp
from jax import lax
from jax.experimental import pallas as pl
from jax.experimental.pallas import tpu as pltpu
from jax.sharding import PartitionSpec as P

F32 = jnp.float32
BF16 = jnp.bfloat16
NN = (((1,), (0,)), ((), ()))
NT = (((1,), (1,)), ((), ()))
WHOLE = pl.BlockSpec(memory_space=pltpu.VMEM)
SCALARS = pl.BlockSpec(memory_space=pltpu.SMEM)
LANES = 128
PARAMS = pltpu.CompilerParams(vmem_limit_bytes=16 * 2**20)
LOG_PARAMS = pltpu.CompilerParams(vmem_limit_bytes=205 * 2**18)


def dot(a, b, dims):
    return lax.dot_general(a, b, dims, preferred_element_type=F32)


def split_terms(x, count):
    terms = []
    for _ in range(count):
        term = x.astype(BF16)
        terms.append(term)
        x = x - term.astype(F32)
    return terms


def tree_sum(parts):
    while len(parts) > 1:
        parts = [sum(parts[at + 1:at + 2], parts[at]) for at in range(0, len(parts), 2)]
    return parts[0]


def log_kernel(width, counts_hbm, high_ref, low_ref, sum_ref, counts_ref, counts_sem):
    cells, genes = high_ref.shape
    fetches = [
        pltpu.make_async_copy(
            counts_hbm.at[:, pl.ds(at * width, width)], counts_ref.at[:, pl.ds(at * width, width)], counts_sem.at[at]
        )
        for at in range(genes // width)
    ]
    for fetch in fetches:
        fetch.start()
    for at, fetch in enumerate(fetches):
        fetch.wait()
        for begin in range(at * width, (at + 1) * width, LANES):
            lanes = pl.ds(begin, LANES)
            logged = jnp.log(1.0 + counts_ref[:, lanes].astype(F32))
            high = logged.astype(BF16)
            high_ref[:, lanes] = high
            low_ref[:, lanes] = (logged - high.astype(F32)).astype(BF16)
            sum_ref[:, lanes] = jnp.sum(logged, axis=0, keepdims=True)


def log_terms(counts):
    cells, genes = counts.shape
    width = genes // 8
    return pl.pallas_call(
        functools.partial(log_kernel, width),
        out_shape=(
            jax.ShapeDtypeStruct((cells, genes), BF16),
            jax.ShapeDtypeStruct((cells, genes), BF16),
            jax.ShapeDtypeStruct((1, genes), F32),
        ),
        in_specs=[pl.BlockSpec(memory_space=pltpu.HBM)],
        out_specs=(WHOLE, WHOLE, WHOLE),
        scratch_shapes=[pltpu.VMEM(counts.shape, BF16), pltpu.SemaphoreType.DMA((genes // width,))],
        compiler_params=LOG_PARAMS,
        cost_estimate=pl.CostEstimate(flops=20 * cells * genes, bytes_accessed=8 * cells * genes, transcendentals=0),
        name="log_terms",
    )(counts)


def score_kernel(width, occ_ref, basis_ref, high_ref, low_ref, score_ref, lane_ref):
    comps, genes = basis_ref.shape
    edge = genes // occ_ref.shape[1]
    occupancy = occ_ref[...].astype(F32)
    scores = None
    for begin in range(0, genes, width):
        basis = []
        for at in range(begin, begin + width, edge):
            occ = jnp.broadcast_to(occupancy[:, at // edge:at // edge + 1], (1, edge))
            lane_ref[:, pl.ds(at, edge)] = occ
            basis.append(basis_ref[:, pl.ds(at, edge)] * occ.astype(BF16))
        basis = jnp.concatenate(basis, axis=1)
        lanes = pl.ds(begin, width)
        part = dot(basis, high_ref[:, lanes], NT) + dot(basis, low_ref[:, lanes], NT)
        scores = part if scores is None else scores + part
    score_ref[...] = scores


def score_part(occupancy, basis, high, low):
    comps, genes = basis.shape
    cells = high.shape[0]
    return pl.pallas_call(
        functools.partial(score_kernel, genes // 4),
        out_shape=(jax.ShapeDtypeStruct((comps, cells), F32), jax.ShapeDtypeStruct((1, genes), F32)),
        in_specs=[WHOLE] * 4,
        out_specs=(WHOLE, WHOLE),
        compiler_params=PARAMS,
        name="scores",
    )(occupancy, basis, high, low)


def spread_piece(terms, high, low):
    comps = terms[0].shape[0]
    on_low = dot(jnp.concatenate(terms[:2], axis=0), low, NN)
    on_high = dot(jnp.concatenate(terms, axis=0), high, NN)
    small = on_low[comps:] + on_high[2 * comps:]
    middle = on_low[:comps] + on_high[comps:2 * comps]
    return (small + middle) + on_high[:comps]


def spread_kernel(count, picks, me_ref, *refs):
    score_refs, outs = refs[:count], refs[count + 4:]
    high_ref, low_ref, sum_ref, occ_ref = refs[count:count + 4]
    scores = tree_sum([ref[...] for ref in score_refs])
    comps = scores.shape[0]
    terms = split_terms(scores, 3)
    eye = lax.broadcasted_iota(jnp.int32, (comps, LANES), 0) == lax.broadcasted_iota(jnp.int32, (comps, LANES), 1)
    row_sums = jnp.sum(jnp.where(eye, jnp.sum(scores, axis=1, keepdims=True), 0.0), axis=0, keepdims=True)
    chunks = high_ref.shape[1] // (LANES * lax.axis_size("cells"))
    width = chunks * LANES
    for pick, out in zip(picks, outs):
        start = pl.multiple_of((me_ref[0] ^ pick) * width, width)
        lanes = pl.ds(start, width)
        piece = spread_piece(terms, high_ref[:, lanes], low_ref[:, lanes]) * occ_ref[:, lanes]
        sums = sum_ref[:, lanes] * occ_ref[:, lanes]
        extra = [row_sums]
        for at in range(chunks):
            out[at * comps:(at + 1) * comps] = piece[:, at * LANES:(at + 1) * LANES]
            extra.append(sums[:, at * LANES:(at + 1) * LANES])
        extra.append(jnp.zeros((out.shape[0] - chunks * comps - chunks - 1, LANES), F32))
        out[chunks * comps:] = jnp.concatenate(extra, axis=0)


def block_rows(comps, chunks):
    return comps * chunks + -(-(chunks + 1) // 8) * 8


def spread_pieces(me, scores, high, low, sums, occ, picks):
    comps = scores[0].shape[0]
    chunks = high.shape[1] // (LANES * lax.axis_size("cells"))
    block = jax.ShapeDtypeStruct((block_rows(comps, chunks), LANES), F32)
    return pl.pallas_call(
        functools.partial(spread_kernel, len(scores), picks),
        out_shape=[block] * len(picks),
        in_specs=[SCALARS] + [WHOLE] * (len(scores) + 4),
        out_specs=[WHOLE] * len(picks),
        compiler_params=PARAMS,
        cost_estimate=pl.CostEstimate(
            flops=10 * comps * len(picks) * chunks * LANES * high.shape[0], bytes_accessed=2**21, transcendentals=0
        ),
        name="spread",
    )(me, *scores, high, low, sums, occ)


def gram_kernel(scale, chunks, *refs):
    pieces, (spread_ref, gram_ref) = refs[:-2], refs[-2:]
    comps = spread_ref.shape[0]
    total = tree_sum([ref[...] for ref in pieces])
    extra = total[chunks * comps:chunks * comps + chunks + 1]
    eye = lax.broadcasted_iota(jnp.int32, (comps, LANES), 0) == lax.broadcasted_iota(jnp.int32, (comps, LANES), 1)
    row_sums = jnp.sum(jnp.where(eye, extra[:1], 0.0), axis=1, keepdims=True) * scale
    parts = [total[at * comps:(at + 1) * comps] - row_sums * extra[at + 1:at + 2] for at in range(chunks)]
    spread = jnp.concatenate(parts, axis=1)
    spread_ref[...] = spread
    gram_ref[...] = packed_gram(spread)


def packed_gram(spread):
    gram = lax.dot_general(spread, spread, NT, precision=lax.Precision.HIGHEST, preferred_element_type=F32)
    half = spread.shape[0] // 2
    return jnp.concatenate([gram[:half], gram[half:]], axis=1)


def centered_gram(pieces, comps, cell_total):
    chunks = pieces[0].shape[0] // comps
    return pl.pallas_call(
        functools.partial(gram_kernel, 1.0 / cell_total, chunks),
        out_shape=(
            jax.ShapeDtypeStruct((comps, chunks * LANES), F32),
            jax.ShapeDtypeStruct((comps // 2, comps * 2), F32),
        ),
        in_specs=[WHOLE] * len(pieces),
        out_specs=(WHOLE, WHOLE),
        compiler_params=PARAMS,
        name="gram",
    )(*pieces)


def plain_gram_kernel(scale, spread_ref, row_ref, sum_ref, out_ref, gram_ref):
    spread = spread_ref[...] - row_ref[...] * scale * sum_ref[...]
    out_ref[...] = spread
    gram_ref[...] = packed_gram(spread)


def plain_gram(spread, rows, sums, cell_total):
    comps, width = spread.shape
    return pl.pallas_call(
        functools.partial(plain_gram_kernel, 1.0 / cell_total),
        out_shape=(
            jax.ShapeDtypeStruct((comps, width), F32),
            jax.ShapeDtypeStruct((comps // 2, comps * 2), F32),
        ),
        in_specs=[WHOLE] * 3,
        out_specs=(WHOLE, WHOLE),
        compiler_params=PARAMS,
        name="plain_gram",
    )(spread, rows, sums)


def row_of(x, at):
    return jnp.broadcast_to(x[at:at + 1, :], x.shape)


def eliminate(groups, edge):
    groups = list(groups)
    below = lax.broadcasted_iota(jnp.int32, groups[0].shape, 0)
    for at in range(len(groups)):
        spread = [
            [jnp.broadcast_to(rows[:, c:c + 1], rows.shape) for c in range(at * edge, (at + 1) * edge)]
            for rows in groups[at:]
        ]
        for i in range(0, edge, 2):
            cols = spread[0]
            first, second = cols[i], cols[i + 1]
            a, b, c = row_of(first, i), row_of(second, i), row_of(second, i + 1)
            inv_a = pl.reciprocal(a, approx=True)
            inv_c = a * pl.reciprocal(a * c - b * b, approx=True)
            ratio = b * inv_a
            factors = []
            for k in range(i + 2, edge):
                top = row_of(cols[k], i)
                factors.append((k, top * inv_a, (row_of(cols[k], i + 1) - ratio * top) * inv_c))
            rows = groups[at]
            upper = row_of(rows, i) * inv_a
            rows = rows - jnp.where(below > i, first, 0.0) * upper
            lower = row_of(rows, i + 1) * inv_c
            groups[at] = rows - jnp.where(below > i + 1, second - ratio * first, 0.0) * lower
            for ahead, cols in enumerate(spread):
                first = cols[i]
                second = cols[i + 1] - ratio * first
                for k, on_first, on_second in factors:
                    cols[k] = cols[k] - first * on_first - second * on_second
                if ahead:
                    groups[at + ahead] = groups[at + ahead] - first * upper - second * lower
    return groups


def basis_kernel(scale, *refs):
    grams, (spread_ref, out_ref) = refs[:-2], refs[-2:]
    gram = tree_sum([ref[...] for ref in grams])
    comps = spread_ref.shape[0]
    gram = jnp.concatenate([gram[:, :comps], gram[:, comps:]], axis=0)
    row_at = lax.broadcasted_iota(jnp.int32, (comps, comps), 0)
    col_at = lax.broadcasted_iota(jnp.int32, (comps, comps), 1)
    eye = row_at == col_at
    diagonal = jnp.where(eye, gram, 0.0)
    row_scale = lax.rsqrt(jnp.sum(diagonal, axis=1, keepdims=True))
    col_scale = lax.rsqrt(jnp.sum(diagonal, axis=0, keepdims=True))
    both = jnp.concatenate([gram * row_scale * col_scale, jnp.where(eye, col_scale, 0.0)], axis=1)
    groups = eliminate([both[at:at + 8] for at in range(0, comps, 8)], 8)
    both = jnp.concatenate(groups, axis=0)
    pivots = jnp.sum(jnp.where(eye, both[:, :comps], 0.0), axis=1, keepdims=True)
    inverse = both[:, comps:] * (scale * lax.rsqrt(pivots))
    out_ref[...] = lax.dot_general(
        inverse, spread_ref[...], NN, precision=lax.Precision.HIGHEST, preferred_element_type=F32
    )


def orthonormal(grams, spread, scale):
    return pl.pallas_call(
        functools.partial(basis_kernel, scale),
        out_shape=jax.ShapeDtypeStruct(spread.shape, F32),
        in_specs=[WHOLE] * (len(grams) + 1),
        out_specs=WHOLE,
        compiler_params=PARAMS,
        name="orthonormal",
    )(*grams, spread)


def send(x, offset_cells, offset_genes):
    cells, genes = lax.axis_size("cells"), lax.axis_size("genes")
    pairs = []
    for c in range(cells):
        for g in range(genes):
            pairs.append((c * genes + g, (c ^ offset_cells) * genes + (g ^ offset_genes)))
    return lax.ppermute(x, ("cells", "genes"), pairs)


def gene_terms(x):
    terms = [x, send(x, 0, 1)]
    for at in range(1, lax.axis_size("genes").bit_length() - 1):
        x = tree_sum(terms)
        terms = [x, send(x, 0, 1 << at | 1)]
    return terms


def cell_terms(x):
    terms = [x]
    for at in range(lax.axis_size("cells").bit_length() - 1):
        x = tree_sum(terms)
        terms = [x, send(x, 1 << at, 1)]
    return terms


def scattered_spread(scores, high, low, sums, occ, cell_total):
    comps = scores[0].shape[0]
    me = lax.axis_index("cells").astype(jnp.int32).reshape(1)
    make = functools.partial(spread_pieces, scores=scores, high=high, low=low, sums=sums, occ=occ)
    blocks = list(make(me, picks=[7, 6, 5]))
    blocks[0], me = lax.optimization_barrier((blocks[0], me))
    came = [send(x, k - 4, 0) for k, x in zip((7, 6, 5), blocks)]
    far, own, near, *blocks = make(me, picks=[4, 0, 2, 3, 1])
    also = [send(x, 1, 0) for x in blocks]
    near = send(near + also[0], 2, 0)
    far = send(tree_sum([far] + came), 4, 0)
    return centered_gram([near, own + also[1] + far], comps, cell_total)


def all_alike(counts, occupancy, start_basis):
    tile_rows, tile_cols = occupancy.shape
    edge = counts.shape[0] // tile_rows
    logged = jnp.log(1.0 + counts.astype(F32)).reshape(tile_rows, edge, tile_cols, -1)
    logged = (logged * occupancy.astype(F32)[:, None, :, None]).reshape(counts.shape)
    high, low = split_terms(logged, 2)
    scores = lax.psum(dot(start_basis, high, NT) + dot(start_basis, low, NT), "genes")
    spread = spread_piece(split_terms(scores, 3), high, low)
    spread = lax.psum_scatter(spread, "cells", scatter_dimension=1, tiled=True)
    rows = lax.psum(jnp.sum(scores, axis=1, keepdims=True), "cells")
    sums = lax.psum_scatter(jnp.sum(logged, axis=0, keepdims=True), "cells", scatter_dimension=1, tiled=True)
    spread, gram = plain_gram(spread, rows, sums, counts.shape[0] * lax.axis_size("cells"))
    return [lax.psum(gram, ("cells", "genes"))], spread


def in_steps(counts, occupancy, start_basis):
    high, low, sums = log_terms(counts)
    scores, occ = score_part(occupancy, start_basis, high, low)
    cell_total = counts.shape[0] * lax.axis_size("cells")
    spread, gram = scattered_spread(gene_terms(scores), high, low, sums, occ, cell_total)
    return cell_terms(tree_sum(gene_terms(gram))), spread


def on_device(counts, occupancy, start_basis):
    gene_count = counts.shape[1]
    cells, genes = lax.axis_size("cells"), lax.axis_size("genes")
    halvings = cells == 1 << 3 and genes == 1 << 2
    tiles = occupancy.shape[0] == 1 and gene_count == occupancy.shape[1] * LANES
    work = in_steps if halvings and tiles and gene_count % (cells * LANES) == 0 else all_alike
    grams, spread = work(counts, occupancy, start_basis)
    return orthonormal(grams, spread, math.sqrt(gene_count * genes))


def solution(mesh):
    in_specs = (P("cells", "genes"), P("cells", "genes"), P(None, "genes"))
    out_specs = P(None, ("genes", "cells"))
    return jax.shard_map(
        on_device, mesh=mesh, in_specs=in_specs, out_specs=out_specs, check_vma=False
    )
```

profile of v0, /device:TPU:0, one launch (start us, length us, event | category | flops | bytes accessed | tf_op | source)
XLA Modules:
  0.0 48.0 jit_solution(2768259119019888133)
XLA Ops:
  0.0 1.9 %log_terms.1 = (bf16[128,4096]{1,0:T(8,128)(2,1)S(1)}, bf16[128,4096]{1,0:T(8,128)(2,1)S(1)}, f32[1,4096]{1,0:T(1,128)S(1)}) custom-call(bf16[128,4096]{1,0:T(8,128)(2,1)} %counts_hbm.1), custom_call_target="tpu_custom_call" | custom-call | flops 10485760 | bytes 4194304 | tf_op jit(solution)/shard_map/log_terms/pallas_call | solution.py:65
  2.6 0.9 %scores.1 = (f32[64,128]{1,0:T(8,128)S(1)}, f32[1,4096]{1,0:T(1,128)S(1)}) custom-call(s32[1,32]{1,0:T(1,128)S(1)} %copy-done.1, bf16[64,4096]{1,0:T(8,128)(2,1)S(1)} %copy-done, bf16[128,4096]{1,0:T(8,128)(2,1)S(1)} %get-tuple-element.22.high_ref.refs_2_, bf16[128,4096]{1,0:T(8,128)(2,1)S(1)} %get-tuple-element.23.low_ref.refs_3_), custom_call_target="tpu_custom_call" | custom-call | tf_op jit(solution)/shard_map/scores/pallas_call | solution.py:102
  4.0 0.9 %collective-permute-done = f32[64,128]{1,0:T(8,128)S(1)} collective-permute-done((f32[64,128]{1,0:T(8,128)S(1)}, f32[64,128]{1,0:T(8,128)S(1)}, u32[]{:S(2)}, u32[]{:S(2)}) %collective-permute-start) | collective-permute-done | bytes 32800 | tf_op jit(solution)/shard_map/ppermute | solution.py:296
  4.8 2.6 %collective-permute-start.1 = (f32[64,128]{1,0:T(8,128)S(1)}, f32[64,128]{1,0:T(8,128)S(1)}, u32[]{:S(2)}, u32[]{:S(2)}) collective-permute-start(f32[64,128]{1,0:T(8,128)S(1)} %add.33.refs_0_), channel_id=1, source_target_pairs={{0,3},{1,2},{2,1},{3,0},{4,7},{5,6},{6,5},{7,4},{8,11},{9,10},{10,... | collective-permute-start | bytes 98312 | tf_op jit(solution)/shard_map/ppermute | solution.py:296
  7.5 1.6 %collective-permute-done.1.refs_1_ = f32[64,128]{1,0:T(8,128)S(1)} collective-permute-done((f32[64,128]{1,0:T(8,128)S(1)}, f32[64,128]{1,0:T(8,128)S(1)}, u32[]{:S(2)}, u32[]{:S(2)}) %collective-permute-start.1) | collective-permute-done | bytes 32800 | tf_op jit(solution)/shard_map/ppermute | solution.py:296
  9.5 3.1 %collective-permute-start.5 = (f32[264,128]{1,0:T(8,128)S(1)}, f32[264,128]{1,0:T(8,128)S(1)}, u32[]{:S(2)}, u32[]{:S(2)}) collective-permute-start(f32[264,128]{1,0:T(8,128)S(1)} %get-tuple-element.34), channel_id=1, source_target_pairs={{0,12},{1,13},{2,14},{3,15},{4,8},{5,9},{6,10},{7,11},{8,4},{9,5},... | collective-permute-start | bytes 405512 | tf_op jit(solution)/shard_map/ppermute | solution.py:296
  13.8 1.9 %collective-permute-start.2 = (f32[264,128]{1,0:T(8,128)S(1)}, f32[264,128]{1,0:T(8,128)S(1)}, u32[]{:S(2)}, u32[]{:S(2)}) collective-permute-start(f32[264,128]{1,0:T(8,128)S(1)} %get-tuple-element.30), channel_id=1, source_target_pairs={{0,4},{1,5},{2,6},{3,7},{4,0},{5,1},{6,2},{7,3},{8,12},{9,13},{10,... | collective-permute-start | bytes 405512 | tf_op jit(solution)/shard_map/ppermute | solution.py:296
  15.9 1.0 %collective-permute-done.5 = f32[264,128]{1,0:T(8,128)S(1)} collective-permute-done((f32[264,128]{1,0:T(8,128)S(1)}, f32[264,128]{1,0:T(8,128)S(1)}, u32[]{:S(2)}, u32[]{:S(2)}) %collective-permute-start.5) | collective-permute-done | bytes 135200 | tf_op jit(solution)/shard_map/ppermute | solution.py:296
  16.9 2.6 %collective-permute-done.6 = f32[264,128]{1,0:T(8,128)S(1)} collective-permute-done((f32[264,128]{1,0:T(8,128)S(1)}, f32[264,128]{1,0:T(8,128)S(1)}, u32[]{:S(2)}, u32[]{:S(2)}) %collective-permute-start.6) | collective-permute-done | bytes 135200 | tf_op jit(solution)/shard_map/ppermute | solution.py:296
  19.7 2.9 %collective-permute-start.8 = (f32[264,128]{1,0:T(8,128)S(1)}, f32[264,128]{1,0:T(8,128)S(1)}, u32[]{:S(2)}, u32[]{:S(2)}) collective-permute-start(f32[264,128]{1,0:T(8,128)S(1)} %add_add_fusion), channel_id=1, source_target_pairs={{0,16},{1,17},{2,18},{3,19},{4,20},{5,21},{6,22},{7,23},{8,24},{9,... | collective-permute-start | bytes 405512 | tf_op jit(solution)/shard_map/ppermute | solution.py:296
  22.6 1.8 %collective-permute-start.3 = (f32[264,128]{1,0:T(8,128)S(1)}, f32[264,128]{1,0:T(8,128)S(1)}, u32[]{:S(2)}, u32[]{:S(2)}) collective-permute-start(f32[264,128]{1,0:T(8,128)S(1)} %add.34), channel_id=1, source_target_pairs={{0,8},{1,9},{2,10},{3,11},{4,12},{5,13},{6,14},{7,15},{8,0},{9,1},... | collective-permute-start | bytes 405512 | tf_op jit(solution)/shard_map/ppermute | solution.py:296
  24.4 0.7 %collective-permute-done.4 = f32[264,128]{1,0:T(8,128)S(1)} collective-permute-done((f32[264,128]{1,0:T(8,128)S(1)}, f32[264,128]{1,0:T(8,128)S(1)}, u32[]{:S(2)}, u32[]{:S(2)}) %collective-permute-start.4) | collective-permute-done | bytes 135200 | tf_op jit(solution)/shard_map/ppermute | solution.py:296
  25.1 3.5 %collective-permute-done.8 = f32[264,128]{1,0:T(8,128)S(1)} collective-permute-done((f32[264,128]{1,0:T(8,128)S(1)}, f32[264,128]{1,0:T(8,128)S(1)}, u32[]{:S(2)}, u32[]{:S(2)}) %collective-permute-start.8) | collective-permute-done | bytes 135200 | tf_op jit(solution)/shard_map/ppermute | solution.py:296
  28.7 0.8 %collective-permute-done.3.refs_0_ = f32[264,128]{1,0:T(8,128)S(1)} collective-permute-done((f32[264,128]{1,0:T(8,128)S(1)}, f32[264,128]{1,0:T(8,128)S(1)}, u32[]{:S(2)}, u32[]{:S(2)}) %collective-permute-start.3) | collective-permute-done | bytes 135200 | tf_op jit(solution)/shard_map/ppermute | solution.py:296
  29.9 1.2 %collective-permute-done.9 = f32[32,128]{1,0:T(8,128)S(1)} collective-permute-done((f32[32,128]{1,0:T(8,128)S(1)}, f32[32,128]{1,0:T(8,128)S(1)}, u32[]{:S(2)}, u32[]{:S(2)}) %collective-permute-start.9) | collective-permute-done | bytes 16416 | tf_op jit(solution)/shard_map/ppermute | solution.py:296
  31.1 1.3 %collective-permute-start.10 = (f32[32,128]{1,0:T(8,128)S(1)}, f32[32,128]{1,0:T(8,128)S(1)}, u32[]{:S(2)}, u32[]{:S(2)}) collective-permute-start(f32[32,128]{1,0:T(8,128)S(1)} %add.40), channel_id=1, source_target_pairs={{0,3},{1,2},{2,1},{3,0},{4,7},{5,6},{6,5},{7,4},{8,11},{9,10},{10,... | collective-permute-start | bytes 49160 | tf_op jit(solution)/shard_map/ppermute | solution.py:296
  32.4 1.9 %collective-permute-done.10 = f32[32,128]{1,0:T(8,128)S(1)} collective-permute-done((f32[32,128]{1,0:T(8,128)S(1)}, f32[32,128]{1,0:T(8,128)S(1)}, u32[]{:S(2)}, u32[]{:S(2)}) %collective-permute-start.10) | collective-permute-done | bytes 16416 | tf_op jit(solution)/shard_map/ppermute | solution.py:296
  34.3 1.5 %collective-permute-start.11 = (f32[32,128]{1,0:T(8,128)S(1)}, f32[32,128]{1,0:T(8,128)S(1)}, u32[]{:S(2)}, u32[]{:S(2)}) collective-permute-start(f32[32,128]{1,0:T(8,128)S(1)} %add.41), channel_id=1, source_target_pairs={{0,5},{1,4},{2,7},{3,6},{4,1},{5,0},{6,3},{7,2},{8,13},{9,12},{10,... | collective-permute-start | bytes 49160 | tf_op jit(solution)/shard_map/ppermute | solution.py:296
  35.8 1.6 %collective-permute-done.11 = f32[32,128]{1,0:T(8,128)S(1)} collective-permute-done((f32[32,128]{1,0:T(8,128)S(1)}, f32[32,128]{1,0:T(8,128)S(1)}, u32[]{:S(2)}, u32[]{:S(2)}) %collective-permute-start.11) | collective-permute-done | bytes 16416 | tf_op jit(solution)/shard_map/ppermute | solution.py:296
  37.4 0.8 %collective-permute-start.12 = (f32[32,128]{1,0:T(8,128)S(1)}, f32[32,128]{1,0:T(8,128)S(1)}, u32[]{:S(2)}, u32[]{:S(2)}) collective-permute-start(f32[32,128]{1,0:T(8,128)S(1)} %add.42), channel_id=1, source_target_pairs={{0,9},{1,8},{2,11},{3,10},{4,13},{5,12},{6,15},{7,14},{8,1},{9,0},... | collective-permute-start | bytes 49160 | tf_op jit(solution)/shard_map/ppermute | solution.py:296
  38.2 2.4 %collective-permute-done.12 = f32[32,128]{1,0:T(8,128)S(1)} collective-permute-done((f32[32,128]{1,0:T(8,128)S(1)}, f32[32,128]{1,0:T(8,128)S(1)}, u32[]{:S(2)}, u32[]{:S(2)}) %collective-permute-start.12) | collective-permute-done | bytes 16416 | tf_op jit(solution)/shard_map/ppermute | solution.py:296
  40.6 2.9 %collective-permute-start.13 = (f32[32,128]{1,0:T(8,128)S(1)}, f32[32,128]{1,0:T(8,128)S(1)}, u32[]{:S(2)}, u32[]{:S(2)}) collective-permute-start(f32[32,128]{1,0:T(8,128)S(1)} %add.43.refs_0_), channel_id=1, source_target_pairs={{0,17},{1,16},{2,19},{3,18},{4,21},{5,20},{6,23},{7,22},{8,25},{9,... | collective-permute-start | bytes 49160 | tf_op jit(solution)/shard_map/ppermute | solution.py:296
  43.6 1.4 %collective-permute-done.13.refs_1_ = f32[32,128]{1,0:T(8,128)S(1)} collective-permute-done((f32[32,128]{1,0:T(8,128)S(1)}, f32[32,128]{1,0:T(8,128)S(1)}, u32[]{:S(2)}, u32[]{:S(2)}) %collective-permute-start.13) | collective-permute-done | bytes 16416 | tf_op jit(solution)/shard_map/ppermute | solution.py:296
  45.0 3.0 %orthonormal.1 = f32[64,512]{1,0:T(8,128)} custom-call(f32[32,128]{1,0:T(8,128)S(1)} %add.43.refs_0_, f32[32,128]{1,0:T(8,128)S(1)} %collective-permute-done.13.refs_1_, f32[64,512]{1,0:T(8,128)S(1)} %get-tuple-element.38.refs_2_), custom_call_target="tpu_custom_call" | custom-call | tf_op jit(solution)/shard_map/orthonormal/pallas_call | solution.py:280
  (22 shorter events, 3.6 us)
Async XLA Ops:
  0.0 1.9 %copy-start = (bf16[64,4096]{1,0:T(8,128)(2,1)S(1)}, bf16[64,4096]{1,0:T(8,128)(2,1)}, u32[]{:S(2)}) copy-start(bf16[64,4096]{1,0:T(8,128)(2,1)} %basis_ref.1) | copy-start | bytes 1572868
  1.9 0.7 %copy-start.1 = (s32[1,32]{1,0:T(1,128)S(1)}, s32[1,32]{1,0:T(1,128)}, u32[]{:S(2)}) copy-start(s32[1,32]{1,0:T(1,128)} %occ_ref.1) | copy-start | bytes 388
  3.5 1.4 %collective-permute-start = (f32[64,128]{1,0:T(8,128)S(1)}, f32[64,128]{1,0:T(8,128)S(1)}, u32[]{:S(2)}, u32[]{:S(2)}) collective-permute-start(f32[64,128]{1,0:T(8,128)S(1)} %get-tuple-element.24), channel_id=1, source_target_pairs={{0,1},{1,0},{2,3},{3,2},{4,5},{5,4},{6,7},{7,6},{8,9},{9,8},{10,11... | collective-permute-start | bytes 98312 | tf_op jit(solution)/shard_map/ppermute | solution.py:296
  4.8 4.2 %collective-permute-start.1 = (f32[64,128]{1,0:T(8,128)S(1)}, f32[64,128]{1,0:T(8,128)S(1)}, u32[]{:S(2)}, u32[]{:S(2)}) collective-permute-start(f32[64,128]{1,0:T(8,128)S(1)} %add.33.refs_0_), channel_id=1, source_target_pairs={{0,3},{1,2},{2,1},{3,0},{4,7},{5,6},{6,5},{7,4},{8,11},{9,10},{10,... | collective-permute-start | bytes 98312 | tf_op jit(solution)/shard_map/ppermute | solution.py:296
  9.5 7.5 %collective-permute-start.5 = (f32[264,128]{1,0:T(8,128)S(1)}, f32[264,128]{1,0:T(8,128)S(1)}, u32[]{:S(2)}, u32[]{:S(2)}) collective-permute-start(f32[264,128]{1,0:T(8,128)S(1)} %get-tuple-element.34), channel_id=1, source_target_pairs={{0,12},{1,13},{2,14},{3,15},{4,8},{5,9},{6,10},{7,11},{8,4},{9,5},... | collective-permute-start | bytes 405512 | tf_op jit(solution)/shard_map/ppermute | solution.py:296
  12.5 7.0 %collective-permute-start.6 = (f32[264,128]{1,0:T(8,128)S(1)}, f32[264,128]{1,0:T(8,128)S(1)}, u32[]{:S(2)}, u32[]{:S(2)}) collective-permute-start(f32[264,128]{1,0:T(8,128)S(1)} %get-tuple-element.35), channel_id=1, source_target_pairs={{0,8},{1,9},{2,10},{3,11},{4,12},{5,13},{6,14},{7,15},{8,0},{9,1},... | collective-permute-start | bytes 405512 | tf_op jit(solution)/shard_map/ppermute | solution.py:296
  13.0 6.6 %collective-permute-start.7 = (f32[264,128]{1,0:T(8,128)S(1)}, f32[264,128]{1,0:T(8,128)S(1)}, u32[]{:S(2)}, u32[]{:S(2)}) collective-permute-start(f32[264,128]{1,0:T(8,128)S(1)} %get-tuple-element.36), channel_id=1, source_target_pairs={{0,4},{1,5},{2,6},{3,7},{4,0},{5,1},{6,2},{7,3},{8,12},{9,13},{10,... | collective-permute-start | bytes 405512 | tf_op jit(solution)/shard_map/ppermute | solution.py:296
  13.8 8.8 %collective-permute-start.2 = (f32[264,128]{1,0:T(8,128)S(1)}, f32[264,128]{1,0:T(8,128)S(1)}, u32[]{:S(2)}, u32[]{:S(2)}) collective-permute-start(f32[264,128]{1,0:T(8,128)S(1)} %get-tuple-element.30), channel_id=1, source_target_pairs={{0,4},{1,5},{2,6},{3,7},{4,0},{5,1},{6,2},{7,3},{8,12},{9,13},{10,... | collective-permute-start | bytes 405512 | tf_op jit(solution)/shard_map/ppermute | solution.py:296
  15.7 9.5 %collective-permute-start.4 = (f32[264,128]{1,0:T(8,128)S(1)}, f32[264,128]{1,0:T(8,128)S(1)}, u32[]{:S(2)}, u32[]{:S(2)}) collective-permute-start(f32[264,128]{1,0:T(8,128)S(1)} %get-tuple-element.32), channel_id=1, source_target_pairs={{0,4},{1,5},{2,6},{3,7},{4,0},{5,1},{6,2},{7,3},{8,12},{9,13},{10,... | collective-permute-start | bytes 405512 | tf_op jit(solution)/shard_map/ppermute | solution.py:296
  19.7 9.0 %collective-permute-start.8 = (f32[264,128]{1,0:T(8,128)S(1)}, f32[264,128]{1,0:T(8,128)S(1)}, u32[]{:S(2)}, u32[]{:S(2)}) collective-permute-start(f32[264,128]{1,0:T(8,128)S(1)} %add_add_fusion), channel_id=1, source_target_pairs={{0,16},{1,17},{2,18},{3,19},{4,20},{5,21},{6,22},{7,23},{8,24},{9,... | collective-permute-start | bytes 405512 | tf_op jit(solution)/shard_map/ppermute | solution.py:296
  22.6 6.9 %collective-permute-start.3 = (f32[264,128]{1,0:T(8,128)S(1)}, f32[264,128]{1,0:T(8,128)S(1)}, u32[]{:S(2)}, u32[]{:S(2)}) collective-permute-start(f32[264,128]{1,0:T(8,128)S(1)} %add.34), channel_id=1, source_target_pairs={{0,8},{1,9},{2,10},{3,11},{4,12},{5,13},{6,14},{7,15},{8,0},{9,1},... | collective-permute-start | bytes 405512 | tf_op jit(solution)/shard_map/ppermute | solution.py:296
  29.9 1.2 %collective-permute-start.9 = (f32[32,128]{1,0:T(8,128)S(1)}, f32[32,128]{1,0:T(8,128)S(1)}, u32[]{:S(2)}, u32[]{:S(2)}) collective-permute-start(f32[32,128]{1,0:T(8,128)S(1)} %get-tuple-element.37), channel_id=1, source_target_pairs={{0,1},{1,0},{2,3},{3,2},{4,5},{5,4},{6,7},{7,6},{8,9},{9,8},{10,11... | collective-permute-start | bytes 49160 | tf_op jit(solution)/shard_map/ppermute | solution.py:296
  31.1 3.2 %collective-permute-start.10 = (f32[32,128]{1,0:T(8,128)S(1)}, f32[32,128]{1,0:T(8,128)S(1)}, u32[]{:S(2)}, u32[]{:S(2)}) collective-permute-start(f32[32,128]{1,0:T(8,128)S(1)} %add.40), channel_id=1, source_target_pairs={{0,3},{1,2},{2,1},{3,0},{4,7},{5,6},{6,5},{7,4},{8,11},{9,10},{10,... | collective-permute-start | bytes 49160 | tf_op jit(solution)/shard_map/ppermute | solution.py:296
  34.3 3.2 %collective-permute-start.11 = (f32[32,128]{1,0:T(8,128)S(1)}, f32[32,128]{1,0:T(8,128)S(1)}, u32[]{:S(2)}, u32[]{:S(2)}) collective-permute-start(f32[32,128]{1,0:T(8,128)S(1)} %add.41), channel_id=1, source_target_pairs={{0,5},{1,4},{2,7},{3,6},{4,1},{5,0},{6,3},{7,2},{8,13},{9,12},{10,... | collective-permute-start | bytes 49160 | tf_op jit(solution)/shard_map/ppermute | solution.py:296
  37.4 3.2 %collective-permute-start.12 = (f32[32,128]{1,0:T(8,128)S(1)}, f32[32,128]{1,0:T(8,128)S(1)}, u32[]{:S(2)}, u32[]{:S(2)}) collective-permute-start(f32[32,128]{1,0:T(8,128)S(1)} %add.42), channel_id=1, source_target_pairs={{0,9},{1,8},{2,11},{3,10},{4,13},{5,12},{6,15},{7,14},{8,1},{9,0},... | collective-permute-start | bytes 49160 | tf_op jit(solution)/shard_map/ppermute | solution.py:296
  40.6 4.4 %collective-permute-start.13 = (f32[32,128]{1,0:T(8,128)S(1)}, f32[32,128]{1,0:T(8,128)S(1)}, u32[]{:S(2)}, u32[]{:S(2)}) collective-permute-start(f32[32,128]{1,0:T(8,128)S(1)} %add.43.refs_0_), channel_id=1, source_target_pairs={{0,17},{1,16},{2,19},{3,18},{4,21},{5,20},{6,23},{7,22},{8,25},{9,... | collective-permute-start | bytes 49160 | tf_op jit(solution)/shard_map/ppermute | solution.py:296
where the time goes:
time: 48.1 us; the launch traced here: 48 us
  starting transfers between devices  20.2 us (42%)
  waiting for transfers between devices  19.8 us (41%)
  Pallas kernels  7.15 us (15%)
  local copies, waits for them, and re-layouts  0.64 us (1%)
    ppermute x14, starting transfers between devices, send(): return lax.ppermute(x, ('cells', 'genes'), pairs)  20.2 us
    ppermute x14, waiting for transfers between devices, send(): return lax.ppermute(x, ('cells', 'genes'), pairs)  19.8 us
    pallas_call x1, Pallas kernels, orthonormal(): pl.pallas_call(functools.partial(basis_kernel, scale), out_shape=jax.Shap...  2.96 us
    pallas_call x1, Pallas kernels, log_terms(): pl.pallas_call(functools.partial(log_kernel, width), out_shape=(jax.Shape...  1.92 us
    pallas_call x2, Pallas kernels, spread_pieces(): pl.pallas_call(functools.partial(spread_kernel, len(scores), picks), out_...  0.98 us
  transfers between devices with their start and end apart: 14, of which 13 were waited for; matrix products, arithmetic and copies ran while one was open for 0% of the time, Pallas kernels for 1%

commit v1 on v0

--- a/solution.py
+++ b/solution.py
@@ -316,14 +316,16 @@
     comps = scores[0].shape[0]
     me = lax.axis_index("cells").astype(jnp.int32).reshape(1)
     make = functools.partial(spread_pieces, scores=scores, high=high, low=low, sums=sums, occ=occ)
-    blocks = list(make(me, picks=[7, 6, 5]))
-    blocks[0], me = lax.optimization_barrier((blocks[0], me))
-    came = [send(x, k - 4, 0) for k, x in zip((7, 6, 5), blocks)]
-    far, own, near, *blocks = make(me, picks=[4, 0, 2, 3, 1])
-    also = [send(x, 1, 0) for x in blocks]
-    near = send(near + also[0], 2, 0)
-    far = send(tree_sum([far] + came), 4, 0)
-    return centered_gram([near, own + also[1] + far], comps, cell_total)
+    first = list(make(me, picks=[6, 5, 7]))
+    first[0], me = lax.optimization_barrier((first[0], me))
+    came = [send(x, k - 4, 0) for k, x in zip((6, 5), first)]
+    straight = [send(first[2], 7, 0)]
+    far, own, *second = make(me, picks=[4, 0, 3, 2, 1])
+    came[0], second[0] = lax.optimization_barrier((came[0], second[0]))
+    far = tree_sum([far] + came)
+    far, second[1], second[2] = lax.optimization_barrier((far, second[1], second[2]))
+    straight += [send(x, k, 0) for k, x in zip((3, 2, 1), second)]
+    return centered_gram([own, send(far, 4, 0)] + straight, comps, cell_total)
 
 
 def all_alike(counts, occupancy, start_basis):

time: 48.1 us -> 47.6 us (0.990)
  starting transfers between devices: 20.2 us -> 18.5 us
  waiting for transfers between devices: 19.8 us -> 21 us
    ppermute x14, starting transfers between devices: 20.2 us -> 18.5 us  [send(): return lax.ppermute(x, ('cells', 'genes'), pairs)]
    ppermute x14, waiting for transfers between devices: 19.8 us -> 21 us  [send(): return lax.ppermute(x, ('cells', 'genes'), pairs)]
  transfers between devices with their start and end apart: 14 -> 14, of which waited for: 13 -> 9; matrix products, arithmetic and copies ran while one was open for 0% -> 0% of each run, Pallas kernels for 1% -> 1%
where the time goes in v1:
time: 47.6 us; the launch traced here: 47.4 us
  waiting for transfers between devices  21 us (44%)
  starting transfers between devices  18.5 us (39%)
  Pallas kernels  7.15 us (15%)
  local copies, waits for them, and re-layouts  0.64 us (1%)
    ppermute x14, waiting for transfers between devices, send(): return lax.ppermute(x, ('cells', 'genes'), pairs)  21 us
    ppermute x14, starting transfers between devices, send(): return lax.ppermute(x, ('cells', 'genes'), pairs)  18.5 us
    pallas_call x1, Pallas kernels, orthonormal(): pl.pallas_call(functools.partial(basis_kernel, scale), out_shape=jax.Shap...  2.97 us
    pallas_call x1, Pallas kernels, log_terms(): pl.pallas_call(functools.partial(log_kernel, width), out_shape=(jax.Shape...  1.92 us
    pallas_call x2, Pallas kernels, spread_pieces(): pl.pallas_call(functools.partial(spread_kernel, len(scores), picks), out_...  0.98 us
  transfers between devices with their start and end apart: 14, of which 9 were waited for; matrix products, arithmetic and copies ran while one was open for 0% of the time, Pallas kernels for 1%

profile of v1, /device:TPU:0, one launch (start us, length us, event | category | flops | bytes accessed | tf_op | source)
XLA Modules:
  0.0 47.4 jit_solution(16199159360465334451)
XLA Ops:
  0.0 1.9 %log_terms.1 = (bf16[128,4096]{1,0:T(8,128)(2,1)S(1)}, bf16[128,4096]{1,0:T(8,128)(2,1)S(1)}, f32[1,4096]{1,0:T(1,128)S(1)}) custom-call(bf16[128,4096]{1,0:T(8,128)(2,1)} %counts_hbm.1), custom_call_target="tpu_custom_call" | custom-call | flops 10485760 | bytes 4194304 | tf_op jit(solution)/shard_map/log_terms/pallas_call | solution.py:65
  1.9 0.6 %copy-done.1 = s32[1,32]{1,0:T(1,128)S(1)} copy-done((s32[1,32]{1,0:T(1,128)S(1)}, s32[1,32]{1,0:T(1,128)}, u32[]{:S(2)}) %copy-start.1) | copy-done | bytes 152
  2.6 0.9 %scores.1 = (f32[64,128]{1,0:T(8,128)S(1)}, f32[1,4096]{1,0:T(1,128)S(1)}) custom-call(s32[1,32]{1,0:T(1,128)S(1)} %copy-done.1, bf16[64,4096]{1,0:T(8,128)(2,1)S(1)} %copy-done, bf16[128,4096]{1,0:T(8,128)(2,1)S(1)} %get-tuple-element.27.high_ref.refs_2_, bf16[128,4096]{1,0:T(8,128)(2,1)S(1)} %get-tuple-element.28.low_ref.refs_3_), custom_call_target="tpu_custom_call" | custom-call | tf_op jit(solution)/shard_map/scores/pallas_call | solution.py:102
  4.0 0.9 %collective-permute-done = f32[64,128]{1,0:T(8,128)S(1)} collective-permute-done((f32[64,128]{1,0:T(8,128)S(1)}, f32[64,128]{1,0:T(8,128)S(1)}, u32[]{:S(2)}, u32[]{:S(2)}) %collective-permute-start) | collective-permute-done | bytes 32800 | tf_op jit(solution)/shard_map/ppermute | solution.py:296
  4.8 2.6 %collective-permute-start.1 = (f32[64,128]{1,0:T(8,128)S(1)}, f32[64,128]{1,0:T(8,128)S(1)}, u32[]{:S(2)}, u32[]{:S(2)}) collective-permute-start(f32[64,128]{1,0:T(8,128)S(1)} %add.21.refs_0_), channel_id=1, source_target_pairs={{0,3},{1,2},{2,1},{3,0},{4,7},{5,6},{6,5},{7,4},{8,11},{9,10},{10,... | collective-permute-start | bytes 98312 | tf_op jit(solution)/shard_map/ppermute | solution.py:296
  7.5 1.6 %collective-permute-done.1.refs_1_ = f32[64,128]{1,0:T(8,128)S(1)} collective-permute-done((f32[64,128]{1,0:T(8,128)S(1)}, f32[64,128]{1,0:T(8,128)S(1)}, u32[]{:S(2)}, u32[]{:S(2)}) %collective-permute-start.1) | collective-permute-done | bytes 32800 | tf_op jit(solution)/shard_map/ppermute | solution.py:296
  9.5 2.1 %collective-permute-start.2 = (f32[264,128]{1,0:T(8,128)S(1)}, f32[264,128]{1,0:T(8,128)S(1)}, u32[]{:S(2)}, u32[]{:S(2)}) collective-permute-start(f32[264,128]{1,0:T(8,128)S(1)} %get-tuple-element.36), channel_id=1, source_target_pairs={{0,8},{1,9},{2,10},{3,11},{4,12},{5,13},{6,14},{7,15},{8,0},{9,1},... | collective-permute-start | bytes 405512 | tf_op jit(solution)/shard_map/ppermute | solution.py:296
  11.6 1.5 %collective-permute-start.3 = (f32[264,128]{1,0:T(8,128)S(1)}, f32[264,128]{1,0:T(8,128)S(1)}, u32[]{:S(2)}, u32[]{:S(2)}) collective-permute-start(f32[264,128]{1,0:T(8,128)S(1)} %get-tuple-element.39), channel_id=1, source_target_pairs={{0,4},{1,5},{2,6},{3,7},{4,0},{5,1},{6,2},{7,3},{8,12},{9,13},{10,... | collective-permute-start | bytes 405512 | tf_op jit(solution)/shard_map/ppermute | solution.py:296
  13.1 2.4 %collective-permute-start.5 = (f32[264,128]{1,0:T(8,128)S(1)}, f32[264,128]{1,0:T(8,128)S(1)}, u32[]{:S(2)}, u32[]{:S(2)}) collective-permute-start(f32[264,128]{1,0:T(8,128)S(1)} %get-tuple-element.43), channel_id=1, source_target_pairs={{0,28},{1,29},{2,30},{3,31},{4,24},{5,25},{6,26},{7,27},{8,20},{9,... | collective-permute-start | bytes 405512 | tf_op jit(solution)/shard_map/ppermute | solution.py:296
  15.5 0.6 %spread.3 = (f32[264,128]{1,0:T(8,128)S(1)}, f32[264,128]{1,0:T(8,128)S(1)}, f32[264,128]{1,0:T(8,128)S(1)}, f32[264,128]{1,0:T(8,128)S(1)}, f32[264,128]{1,0:T(8,128)S(1)}) custom-call(s32[1]{0:T(128)} %bitcast.me_ref, f32[64,128]{1,0:T(8,128)S(1)} %add.21.refs_0_, f32[64,128]{1,0:T(8,128)S(1)} %collective-permute-done.1.refs_1_, ...), custom_call_target="tpu_custom_call" | custom-call | flops 209715200 | bytes 2097152 | tf_op jit(solution)/shard_map/spread/pallas_call | solution.py:152
  16.1 2.1 %collective-permute-start.6 = (f32[264,128]{1,0:T(8,128)S(1)}, f32[264,128]{1,0:T(8,128)S(1)}, u32[]{:S(2)}, u32[]{:S(2)}) collective-permute-start(f32[264,128]{1,0:T(8,128)S(1)} %get-tuple-element.44), channel_id=1, source_target_pairs={{0,12},{1,13},{2,14},{3,15},{4,8},{5,9},{6,10},{7,11},{8,4},{9,5},... | collective-permute-start | bytes 405512 | tf_op jit(solution)/shard_map/ppermute | solution.py:296
  18.2 2.7 %collective-permute-start.4 = (f32[264,128]{1,0:T(8,128)S(1)}, f32[264,128]{1,0:T(8,128)S(1)}, u32[]{:S(2)}, u32[]{:S(2)}) collective-permute-start(f32[264,128]{1,0:T(8,128)S(1)} %add_add_fusion), channel_id=1, source_target_pairs={{0,16},{1,17},{2,18},{3,19},{4,20},{5,21},{6,22},{7,23},{8,24},{9,... | collective-permute-start | bytes 405512 | tf_op jit(solution)/shard_map/ppermute | solution.py:296
  20.9 1.0 %collective-permute-start.7 = (f32[264,128]{1,0:T(8,128)S(1)}, f32[264,128]{1,0:T(8,128)S(1)}, u32[]{:S(2)}, u32[]{:S(2)}) collective-permute-start(f32[264,128]{1,0:T(8,128)S(1)} %get-tuple-element.45), channel_id=1, source_target_pairs={{0,8},{1,9},{2,10},{3,11},{4,12},{5,13},{6,14},{7,15},{8,0},{9,1},... | collective-permute-start | bytes 405512 | tf_op jit(solution)/shard_map/ppermute | solution.py:296
  22.4 5.0 %collective-permute-done.6.refs_3_ = f32[264,128]{1,0:T(8,128)S(1)} collective-permute-done((f32[264,128]{1,0:T(8,128)S(1)}, f32[264,128]{1,0:T(8,128)S(1)}, u32[]{:S(2)}, u32[]{:S(2)}) %collective-permute-start.6) | collective-permute-done | bytes 135200 | tf_op jit(solution)/shard_map/ppermute | solution.py:296
  27.4 1.8 %collective-permute-done.7.refs_4_ = f32[264,128]{1,0:T(8,128)S(1)} collective-permute-done((f32[264,128]{1,0:T(8,128)S(1)}, f32[264,128]{1,0:T(8,128)S(1)}, u32[]{:S(2)}, u32[]{:S(2)}) %collective-permute-start.7) | collective-permute-done | bytes 135200 | tf_op jit(solution)/shard_map/ppermute | solution.py:296
  29.7 1.2 %collective-permute-done.9 = f32[32,128]{1,0:T(8,128)S(1)} collective-permute-done((f32[32,128]{1,0:T(8,128)S(1)}, f32[32,128]{1,0:T(8,128)S(1)}, u32[]{:S(2)}, u32[]{:S(2)}) %collective-permute-start.9) | collective-permute-done | bytes 16416 | tf_op jit(solution)/shard_map/ppermute | solution.py:296
  30.9 1.3 %collective-permute-start.10 = (f32[32,128]{1,0:T(8,128)S(1)}, f32[32,128]{1,0:T(8,128)S(1)}, u32[]{:S(2)}, u32[]{:S(2)}) collective-permute-start(f32[32,128]{1,0:T(8,128)S(1)} %add.24), channel_id=1, source_target_pairs={{0,3},{1,2},{2,1},{3,0},{4,7},{5,6},{6,5},{7,4},{8,11},{9,10},{10,... | collective-permute-start | bytes 49160 | tf_op jit(solution)/shard_map/ppermute | solution.py:296
  32.2 1.9 %collective-permute-done.10 = f32[32,128]{1,0:T(8,128)S(1)} collective-permute-done((f32[32,128]{1,0:T(8,128)S(1)}, f32[32,128]{1,0:T(8,128)S(1)}, u32[]{:S(2)}, u32[]{:S(2)}) %collective-permute-start.10) | collective-permute-done | bytes 16416 | tf_op jit(solution)/shard_map/ppermute | solution.py:296
  34.1 1.2 %collective-permute-start.11 = (f32[32,128]{1,0:T(8,128)S(1)}, f32[32,128]{1,0:T(8,128)S(1)}, u32[]{:S(2)}, u32[]{:S(2)}) collective-permute-start(f32[32,128]{1,0:T(8,128)S(1)} %add.25), channel_id=1, source_target_pairs={{0,5},{1,4},{2,7},{3,6},{4,1},{5,0},{6,3},{7,2},{8,13},{9,12},{10,... | collective-permute-start | bytes 49160 | tf_op jit(solution)/shard_map/ppermute | solution.py:296
  35.3 2.0 %collective-permute-done.11 = f32[32,128]{1,0:T(8,128)S(1)} collective-permute-done((f32[32,128]{1,0:T(8,128)S(1)}, f32[32,128]{1,0:T(8,128)S(1)}, u32[]{:S(2)}, u32[]{:S(2)}) %collective-permute-start.11) | collective-permute-done | bytes 16416 | tf_op jit(solution)/shard_map/ppermute | solution.py:296
  37.3 3.1 %collective-permute-done.12 = f32[32,128]{1,0:T(8,128)S(1)} collective-permute-done((f32[32,128]{1,0:T(8,128)S(1)}, f32[32,128]{1,0:T(8,128)S(1)}, u32[]{:S(2)}, u32[]{:S(2)}) %collective-permute-start.12) | collective-permute-done | bytes 16416 | tf_op jit(solution)/shard_map/ppermute | solution.py:296
  40.4 0.5 %collective-permute-start.13 = (f32[32,128]{1,0:T(8,128)S(1)}, f32[32,128]{1,0:T(8,128)S(1)}, u32[]{:S(2)}, u32[]{:S(2)}) collective-permute-start(f32[32,128]{1,0:T(8,128)S(1)} %add.27.refs_0_), channel_id=1, source_target_pairs={{0,17},{1,16},{2,19},{3,18},{4,21},{5,20},{6,23},{7,22},{8,25},{9,... | collective-permute-start | bytes 49160 | tf_op jit(solution)/shard_map/ppermute | solution.py:296
  40.9 3.5 %collective-permute-done.13.refs_1_ = f32[32,128]{1,0:T(8,128)S(1)} collective-permute-done((f32[32,128]{1,0:T(8,128)S(1)}, f32[32,128]{1,0:T(8,128)S(1)}, u32[]{:S(2)}, u32[]{:S(2)}) %collective-permute-start.13) | collective-permute-done | bytes 16416 | tf_op jit(solution)/shard_map/ppermute | solution.py:296
  44.5 3.0 %orthonormal.1 = f32[64,512]{1,0:T(8,128)} custom-call(f32[32,128]{1,0:T(8,128)S(1)} %add.27.refs_0_, f32[32,128]{1,0:T(8,128)S(1)} %collective-permute-done.13.refs_1_, f32[64,512]{1,0:T(8,128)S(1)} %get-tuple-element.48.refs_2_), custom_call_target="tpu_custom_call" | custom-call | tf_op jit(solution)/shard_map/orthonormal/pallas_call | solution.py:280
  (20 shorter events, 2.0 us)
Async XLA Ops:
  0.0 1.9 %copy-start = (bf16[64,4096]{1,0:T(8,128)(2,1)S(1)}, bf16[64,4096]{1,0:T(8,128)(2,1)}, u32[]{:S(2)}) copy-start(bf16[64,4096]{1,0:T(8,128)(2,1)} %basis_ref.1) | copy-start | bytes 1572868
  1.9 0.7 %copy-start.1 = (s32[1,32]{1,0:T(1,128)S(1)}, s32[1,32]{1,0:T(1,128)}, u32[]{:S(2)}) copy-start(s32[1,32]{1,0:T(1,128)} %occ_ref.1) | copy-start | bytes 388
  3.5 1.4 %collective-permute-start = (f32[64,128]{1,0:T(8,128)S(1)}, f32[64,128]{1,0:T(8,128)S(1)}, u32[]{:S(2)}, u32[]{:S(2)}) collective-permute-start(f32[64,128]{1,0:T(8,128)S(1)} %get-tuple-element.29), channel_id=1, source_target_pairs={{0,1},{1,0},{2,3},{3,2},{4,5},{5,4},{6,7},{7,6},{8,9},{9,8},{10,11... | collective-permute-start | bytes 98312 | tf_op jit(solution)/shard_map/ppermute | solution.py:296
  4.8 4.2 %collective-permute-start.1 = (f32[64,128]{1,0:T(8,128)S(1)}, f32[64,128]{1,0:T(8,128)S(1)}, u32[]{:S(2)}, u32[]{:S(2)}) collective-permute-start(f32[64,128]{1,0:T(8,128)S(1)} %add.21.refs_0_), channel_id=1, source_target_pairs={{0,3},{1,2},{2,1},{3,0},{4,7},{5,6},{6,5},{7,4},{8,11},{9,10},{10,... | collective-permute-start | bytes 98312 | tf_op jit(solution)/shard_map/ppermute | solution.py:296
  9.5 6.7 %collective-permute-start.2 = (f32[264,128]{1,0:T(8,128)S(1)}, f32[264,128]{1,0:T(8,128)S(1)}, u32[]{:S(2)}, u32[]{:S(2)}) collective-permute-start(f32[264,128]{1,0:T(8,128)S(1)} %get-tuple-element.36), channel_id=1, source_target_pairs={{0,8},{1,9},{2,10},{3,11},{4,12},{5,13},{6,14},{7,15},{8,0},{9,1},... | collective-permute-start | bytes 405512 | tf_op jit(solution)/shard_map/ppermute | solution.py:296
  11.6 6.6 %collective-permute-start.3 = (f32[264,128]{1,0:T(8,128)S(1)}, f32[264,128]{1,0:T(8,128)S(1)}, u32[]{:S(2)}, u32[]{:S(2)}) collective-permute-start(f32[264,128]{1,0:T(8,128)S(1)} %get-tuple-element.39), channel_id=1, source_target_pairs={{0,4},{1,5},{2,6},{3,7},{4,0},{5,1},{6,2},{7,3},{8,12},{9,13},{10,... | collective-permute-start | bytes 405512 | tf_op jit(solution)/shard_map/ppermute | solution.py:296
  13.1 9.3 %collective-permute-start.5 = (f32[264,128]{1,0:T(8,128)S(1)}, f32[264,128]{1,0:T(8,128)S(1)}, u32[]{:S(2)}, u32[]{:S(2)}) collective-permute-start(f32[264,128]{1,0:T(8,128)S(1)} %get-tuple-element.43), channel_id=1, source_target_pairs={{0,28},{1,29},{2,30},{3,31},{4,24},{5,25},{6,26},{7,27},{8,20},{9,... | collective-permute-start | bytes 405512 | tf_op jit(solution)/shard_map/ppermute | solution.py:296
  16.1 11.3 %collective-permute-start.6 = (f32[264,128]{1,0:T(8,128)S(1)}, f32[264,128]{1,0:T(8,128)S(1)}, u32[]{:S(2)}, u32[]{:S(2)}) collective-permute-start(f32[264,128]{1,0:T(8,128)S(1)} %get-tuple-element.44), channel_id=1, source_target_pairs={{0,12},{1,13},{2,14},{3,15},{4,8},{5,9},{6,10},{7,11},{8,4},{9,5},... | collective-permute-start | bytes 405512 | tf_op jit(solution)/shard_map/ppermute | solution.py:296
  18.2 9.2 %collective-permute-start.4 = (f32[264,128]{1,0:T(8,128)S(1)}, f32[264,128]{1,0:T(8,128)S(1)}, u32[]{:S(2)}, u32[]{:S(2)}) collective-permute-start(f32[264,128]{1,0:T(8,128)S(1)} %add_add_fusion), channel_id=1, source_target_pairs={{0,16},{1,17},{2,18},{3,19},{4,20},{5,21},{6,22},{7,23},{8,24},{9,... | collective-permute-start | bytes 405512 | tf_op jit(solution)/shard_map/ppermute | solution.py:296
  20.9 8.4 %collective-permute-start.7 = (f32[264,128]{1,0:T(8,128)S(1)}, f32[264,128]{1,0:T(8,128)S(1)}, u32[]{:S(2)}, u32[]{:S(2)}) collective-permute-start(f32[264,128]{1,0:T(8,128)S(1)} %get-tuple-element.45), channel_id=1, source_target_pairs={{0,8},{1,9},{2,10},{3,11},{4,12},{5,13},{6,14},{7,15},{8,0},{9,1},... | collective-permute-start | bytes 405512 | tf_op jit(solution)/shard_map/ppermute | solution.py:296
  21.9 7.4 %collective-permute-start.8 = (f32[264,128]{1,0:T(8,128)S(1)}, f32[264,128]{1,0:T(8,128)S(1)}, u32[]{:S(2)}, u32[]{:S(2)}) collective-permute-start(f32[264,128]{1,0:T(8,128)S(1)} %get-tuple-element.46), channel_id=1, source_target_pairs={{0,4},{1,5},{2,6},{3,7},{4,0},{5,1},{6,2},{7,3},{8,12},{9,13},{10,... | collective-permute-start | bytes 405512 | tf_op jit(solution)/shard_map/ppermute | solution.py:296
  29.7 1.2 %collective-permute-start.9 = (f32[32,128]{1,0:T(8,128)S(1)}, f32[32,128]{1,0:T(8,128)S(1)}, u32[]{:S(2)}, u32[]{:S(2)}) collective-permute-start(f32[32,128]{1,0:T(8,128)S(1)} %get-tuple-element.47), channel_id=1, source_target_pairs={{0,1},{1,0},{2,3},{3,2},{4,5},{5,4},{6,7},{7,6},{8,9},{9,8},{10,11... | collective-permute-start | bytes 49160 | tf_op jit(solution)/shard_map/ppermute | solution.py:296
  30.9 3.2 %collective-permute-start.10 = (f32[32,128]{1,0:T(8,128)S(1)}, f32[32,128]{1,0:T(8,128)S(1)}, u32[]{:S(2)}, u32[]{:S(2)}) collective-permute-start(f32[32,128]{1,0:T(8,128)S(1)} %add.24), channel_id=1, source_target_pairs={{0,3},{1,2},{2,1},{3,0},{4,7},{5,6},{6,5},{7,4},{8,11},{9,10},{10,... | collective-permute-start | bytes 49160 | tf_op jit(solution)/shard_map/ppermute | solution.py:296
  34.1 3.2 %collective-permute-start.11 = (f32[32,128]{1,0:T(8,128)S(1)}, f32[32,128]{1,0:T(8,128)S(1)}, u32[]{:S(2)}, u32[]{:S(2)}) collective-permute-start(f32[32,128]{1,0:T(8,128)S(1)} %add.25), channel_id=1, source_target_pairs={{0,5},{1,4},{2,7},{3,6},{4,1},{5,0},{6,3},{7,2},{8,13},{9,12},{10,... | collective-permute-start | bytes 49160 | tf_op jit(solution)/shard_map/ppermute | solution.py:296
  37.2 3.2 %collective-permute-start.12 = (f32[32,128]{1,0:T(8,128)S(1)}, f32[32,128]{1,0:T(8,128)S(1)}, u32[]{:S(2)}, u32[]{:S(2)}) collective-permute-start(f32[32,128]{1,0:T(8,128)S(1)} %add.26), channel_id=1, source_target_pairs={{0,9},{1,8},{2,11},{3,10},{4,13},{5,12},{6,15},{7,14},{8,1},{9,0},... | collective-permute-start | bytes 49160 | tf_op jit(solution)/shard_map/ppermute | solution.py:296
  40.4 4.1 %collective-permute-start.13 = (f32[32,128]{1,0:T(8,128)S(1)}, f32[32,128]{1,0:T(8,128)S(1)}, u32[]{:S(2)}, u32[]{:S(2)}) collective-permute-start(f32[32,128]{1,0:T(8,128)S(1)} %add.27.refs_0_), channel_id=1, source_target_pairs={{0,17},{1,16},{2,19},{3,18},{4,21},{5,20},{6,23},{7,22},{8,25},{9,... | collective-permute-start | bytes 49160 | tf_op jit(solution)/shard_map/ppermute | solution.py:296

commit v2 on v1

--- a/solution.py
+++ b/solution.py
@@ -221,56 +221,87 @@
     return jnp.broadcast_to(x[at:at + 1, :], x.shape)
 
 
-def eliminate(groups, edge):
+def spread_column(rows, at):
+    return jnp.broadcast_to(rows[:, at:at + 1], rows.shape)
+
+
+def eliminate(groups, begin):
     groups = list(groups)
+    edge = groups[0].shape[0]
     below = lax.broadcasted_iota(jnp.int32, groups[0].shape, 0)
+    columns = [{c: spread_column(rows, begin + c) for c in range(edge)} for rows in groups]
     for at in range(len(groups)):
-        spread = [
-            [jnp.broadcast_to(rows[:, c:c + 1], rows.shape) for c in range(at * edge, (at + 1) * edge)]
-            for rows in groups[at:]
-        ]
-        for i in range(0, edge, 2):
-            cols = spread[0]
+        scale = jnp.zeros_like(groups[0])
+        later = (at + 1) * edge
+        for i in range(at * edge, later, 2):
+            if i == later - 4 and at + 1 < len(groups):
+                for rows, cols in zip(groups[at:], columns[at:]):
+                    cols.update({c: spread_column(rows, begin + c) for c in range(later, later + edge)})
+            row = i - at * edge
+            cols = columns[at]
             first, second = cols[i], cols[i + 1]
-            a, b, c = row_of(first, i), row_of(second, i), row_of(second, i + 1)
+            a, b, c = row_of(first, row), row_of(second, row), row_of(second, row + 1)
+            det = a * c - b * b
             inv_a = pl.reciprocal(a, approx=True)
-            inv_c = a * pl.reciprocal(a * c - b * b, approx=True)
+            inv_c = a * pl.reciprocal(det, approx=True)
             ratio = b * inv_a
+            scale = jnp.where(below == row, lax.rsqrt(a), jnp.where(below == row + 1, lax.rsqrt(det * inv_a), scale))
             factors = []
-            for k in range(i + 2, edge):
-                top = row_of(cols[k], i)
-                factors.append((k, top * inv_a, (row_of(cols[k], i + 1) - ratio * top) * inv_c))
+            for k in cols:
+                if k > i + 1:
+                    top = row_of(cols[k], row)
+                    factors.append((k, top * inv_a, (row_of(cols[k], row + 1) - ratio * top) * inv_c))
             rows = groups[at]
-            upper = row_of(rows, i) * inv_a
-            rows = rows - jnp.where(below > i, first, 0.0) * upper
-            lower = row_of(rows, i + 1) * inv_c
-            groups[at] = rows - jnp.where(below > i + 1, second - ratio * first, 0.0) * lower
-            for ahead, cols in enumerate(spread):
+            upper = row_of(rows, row) * inv_a
+            rows = rows - jnp.where(below > row, first, 0.0) * upper
+            lower = row_of(rows, row + 1) * inv_c
+            groups[at] = rows - jnp.where(below > row + 1, second - ratio * first, 0.0) * lower
+            for ahead in range(at, len(groups)):
+                cols = columns[ahead]
                 first = cols[i]
                 second = cols[i + 1] - ratio * first
                 for k, on_first, on_second in factors:
                     cols[k] = cols[k] - first * on_first - second * on_second
-                if ahead:
-                    groups[at + ahead] = groups[at + ahead] - first * upper - second * lower
+                if ahead > at:
+                    groups[ahead] = groups[ahead] - first * upper - second * lower
+                del cols[i], cols[i + 1]
+        groups[at] = groups[at] * scale
     return groups
 
 
-def basis_kernel(scale, *refs):
-    grams, (spread_ref, out_ref) = refs[:-2], refs[-2:]
-    gram = tree_sum([ref[...] for ref in grams])
-    comps = spread_ref.shape[0]
+def scale_kernel(gram_ref, times_ref, plus_ref):
+    gram = gram_ref[...]
+    half, comps = gram.shape[0], gram.shape[1] // 2
     gram = jnp.concatenate([gram[:, :comps], gram[:, comps:]], axis=0)
-    row_at = lax.broadcasted_iota(jnp.int32, (comps, comps), 0)
-    col_at = lax.broadcasted_iota(jnp.int32, (comps, comps), 1)
-    eye = row_at == col_at
+    eye = lax.broadcasted_iota(jnp.int32, gram.shape, 0) == lax.broadcasted_iota(jnp.int32, gram.shape, 1)
     diagonal = jnp.where(eye, gram, 0.0)
     row_scale = lax.rsqrt(jnp.sum(diagonal, axis=1, keepdims=True))
     col_scale = lax.rsqrt(jnp.sum(diagonal, axis=0, keepdims=True))
-    both = jnp.concatenate([gram * row_scale * col_scale, jnp.where(eye, col_scale, 0.0)], axis=1)
-    groups = eliminate([both[at:at + 8] for at in range(0, comps, 8)], 8)
-    both = jnp.concatenate(groups, axis=0)
-    pivots = jnp.sum(jnp.where(eye, both[:, :comps], 0.0), axis=1, keepdims=True)
-    inverse = both[:, comps:] * (scale * lax.rsqrt(pivots))
+    zeros = jnp.zeros_like(gram)
+    times_ref[...] = jnp.concatenate([zeros, row_scale * col_scale], axis=1)
+    plus_ref[...] = jnp.concatenate([jnp.where(eye, col_scale, 0.0), zeros], axis=1)
+
+
+def scales(gram):
+    half, lanes = gram.shape
+    return pl.pallas_call(
+        scale_kernel,
+        out_shape=[jax.ShapeDtypeStruct((2 * half, lanes), F32)] * 2,
+        in_specs=[WHOLE],
+        out_specs=[WHOLE, WHOLE],
+        compiler_params=PARAMS,
+        name="scales",
+    )(gram)
+
+
+def basis_kernel(scale, *refs):
+    grams, (times_ref, plus_ref, spread_ref, out_ref) = refs[:-4], refs[-4:]
+    gram = tree_sum([ref[...] for ref in grams])
+    comps = spread_ref.shape[0]
+    gram = jnp.concatenate([pltpu.roll(gram, comps, 1), gram], axis=0)
+    both = gram * times_ref[...] + plus_ref[...]
+    groups = eliminate([both[at:at + 8] for at in range(0, comps, 8)], comps)
+    inverse = jnp.concatenate(groups, axis=0)[:, :comps] * scale
     out_ref[...] = lax.dot_general(
         inverse, spread_ref[...], NN, precision=lax.Precision.HIGHEST, preferred_element_type=F32
     )
@@ -280,11 +311,11 @@
     return pl.pallas_call(
         functools.partial(basis_kernel, scale),
         out_shape=jax.ShapeDtypeStruct(spread.shape, F32),
-        in_specs=[WHOLE] * (len(grams) + 1),
+        in_specs=[WHOLE] * (len(grams) + 3),
         out_specs=WHOLE,
         compiler_params=PARAMS,
         name="orthonormal",
-    )(*grams, spread)
+    )(*grams, *scales(grams[0]), spread)
 
 
 def send(x, offset_cells, offset_genes):

time: 47.6 us -> 47.2 us (level)
  transfers between devices with their start and end apart: 14 -> 14, of which waited for: 9 -> 9; matrix products, arithmetic and copies ran while one was open for 0% -> 0% of each run, Pallas kernels for 1% -> 2%
where the time goes in v2:
time: 47.2 us; the launch traced here: 47 us
  waiting for transfers between devices  20.8 us (44%)
  starting transfers between devices  18.5 us (39%)
  Pallas kernels  6.96 us (15%)
  local copies, waits for them, and re-layouts  0.64 us (1%)
    ppermute x14, waiting for transfers between devices, send(): return lax.ppermute(x, ('cells', 'genes'), pairs)  20.8 us
    ppermute x14, starting transfers between devices, send(): return lax.ppermute(x, ('cells', 'genes'), pairs)  18.5 us
    pallas_call x1, Pallas kernels, orthonormal(): pl.pallas_call(functools.partial(basis_kernel, scale), out_shape=jax.Shap...  2.57 us
    pallas_call x1, Pallas kernels, log_terms(): pl.pallas_call(functools.partial(log_kernel, width), out_shape=(jax.Shape...  1.92 us
    pallas_call x2, Pallas kernels, spread_pieces(): pl.pallas_call(functools.partial(spread_kernel, len(scores), picks), out_...  0.98 us
  transfers between devices with their start and end apart: 14, of which 9 were waited for; matrix products, arithmetic and copies ran while one was open for 0% of the time, Pallas kernels for 2%

profile of v2, /device:TPU:0, one launch (start us, length us, event | category | flops | bytes accessed | tf_op | source)
XLA Modules:
  0.0 47.0 jit_solution(6820589723715938635)
XLA Ops:
  0.0 1.9 %log_terms.1 = (bf16[128,4096]{1,0:T(8,128)(2,1)S(1)}, bf16[128,4096]{1,0:T(8,128)(2,1)S(1)}, f32[1,4096]{1,0:T(1,128)S(1)}) custom-call(bf16[128,4096]{1,0:T(8,128)(2,1)} %counts_hbm.1), custom_call_target="tpu_custom_call" | custom-call | flops 10485760 | bytes 4194304 | tf_op jit(solution)/shard_map/log_terms/pallas_call | solution.py:65
  1.9 0.6 %copy-done.1 = s32[1,32]{1,0:T(1,128)S(1)} copy-done((s32[1,32]{1,0:T(1,128)S(1)}, s32[1,32]{1,0:T(1,128)}, u32[]{:S(2)}) %copy-start.1) | copy-done | bytes 152
  2.6 0.9 %scores.1 = (f32[64,128]{1,0:T(8,128)S(1)}, f32[1,4096]{1,0:T(1,128)S(1)}) custom-call(s32[1,32]{1,0:T(1,128)S(1)} %copy-done.1, bf16[64,4096]{1,0:T(8,128)(2,1)S(1)} %copy-done, bf16[128,4096]{1,0:T(8,128)(2,1)S(1)} %get-tuple-element.29.high_ref.refs_2_, bf16[128,4096]{1,0:T(8,128)(2,1)S(1)} %get-tuple-element.30.low_ref.refs_3_), custom_call_target="tpu_custom_call" | custom-call | tf_op jit(solution)/shard_map/scores/pallas_call | solution.py:102
  4.0 0.9 %collective-permute-done = f32[64,128]{1,0:T(8,128)S(1)} collective-permute-done((f32[64,128]{1,0:T(8,128)S(1)}, f32[64,128]{1,0:T(8,128)S(1)}, u32[]{:S(2)}, u32[]{:S(2)}) %collective-permute-start) | collective-permute-done | bytes 32800 | tf_op jit(solution)/shard_map/ppermute | solution.py:327
  4.8 2.6 %collective-permute-start.1 = (f32[64,128]{1,0:T(8,128)S(1)}, f32[64,128]{1,0:T(8,128)S(1)}, u32[]{:S(2)}, u32[]{:S(2)}) collective-permute-start(f32[64,128]{1,0:T(8,128)S(1)} %add.21.refs_0_), channel_id=1, source_target_pairs={{0,3},{1,2},{2,1},{3,0},{4,7},{5,6},{6,5},{7,4},{8,11},{9,10},{10,... | collective-permute-start | bytes 98312 | tf_op jit(solution)/shard_map/ppermute | solution.py:327
  7.5 1.6 %collective-permute-done.1.refs_1_ = f32[64,128]{1,0:T(8,128)S(1)} collective-permute-done((f32[64,128]{1,0:T(8,128)S(1)}, f32[64,128]{1,0:T(8,128)S(1)}, u32[]{:S(2)}, u32[]{:S(2)}) %collective-permute-start.1) | collective-permute-done | bytes 32800 | tf_op jit(solution)/shard_map/ppermute | solution.py:327
  9.5 2.1 %collective-permute-start.2 = (f32[264,128]{1,0:T(8,128)S(1)}, f32[264,128]{1,0:T(8,128)S(1)}, u32[]{:S(2)}, u32[]{:S(2)}) collective-permute-start(f32[264,128]{1,0:T(8,128)S(1)} %get-tuple-element.38), channel_id=1, source_target_pairs={{0,8},{1,9},{2,10},{3,11},{4,12},{5,13},{6,14},{7,15},{8,0},{9,1},... | collective-permute-start | bytes 405512 | tf_op jit(solution)/shard_map/ppermute | solution.py:327
  11.6 1.5 %collective-permute-start.3 = (f32[264,128]{1,0:T(8,128)S(1)}, f32[264,128]{1,0:T(8,128)S(1)}, u32[]{:S(2)}, u32[]{:S(2)}) collective-permute-start(f32[264,128]{1,0:T(8,128)S(1)} %get-tuple-element.41), channel_id=1, source_target_pairs={{0,4},{1,5},{2,6},{3,7},{4,0},{5,1},{6,2},{7,3},{8,12},{9,13},{10,... | collective-permute-start | bytes 405512 | tf_op jit(solution)/shard_map/ppermute | solution.py:327
  13.1 2.4 %collective-permute-start.5 = (f32[264,128]{1,0:T(8,128)S(1)}, f32[264,128]{1,0:T(8,128)S(1)}, u32[]{:S(2)}, u32[]{:S(2)}) collective-permute-start(f32[264,128]{1,0:T(8,128)S(1)} %get-tuple-element.45), channel_id=1, source_target_pairs={{0,28},{1,29},{2,30},{3,31},{4,24},{5,25},{6,26},{7,27},{8,20},{9,... | collective-permute-start | bytes 405512 | tf_op jit(solution)/shard_map/ppermute | solution.py:327
  15.5 0.6 %spread.3 = (f32[264,128]{1,0:T(8,128)S(1)}, f32[264,128]{1,0:T(8,128)S(1)}, f32[264,128]{1,0:T(8,128)S(1)}, f32[264,128]{1,0:T(8,128)S(1)}, f32[264,128]{1,0:T(8,128)S(1)}) custom-call(s32[1]{0:T(128)} %bitcast.me_ref, f32[64,128]{1,0:T(8,128)S(1)} %add.21.refs_0_, f32[64,128]{1,0:T(8,128)S(1)} %collective-permute-done.1.refs_1_, ...), custom_call_target="tpu_custom_call" | custom-call | flops 209715200 | bytes 2097152 | tf_op jit(solution)/shard_map/spread/pallas_call | solution.py:152
  16.1 2.1 %collective-permute-start.6 = (f32[264,128]{1,0:T(8,128)S(1)}, f32[264,128]{1,0:T(8,128)S(1)}, u32[]{:S(2)}, u32[]{:S(2)}) collective-permute-start(f32[264,128]{1,0:T(8,128)S(1)} %get-tuple-element.46), channel_id=1, source_target_pairs={{0,12},{1,13},{2,14},{3,15},{4,8},{5,9},{6,10},{7,11},{8,4},{9,5},... | collective-permute-start | bytes 405512 | tf_op jit(solution)/shard_map/ppermute | solution.py:327
  18.2 2.7 %collective-permute-start.4 = (f32[264,128]{1,0:T(8,128)S(1)}, f32[264,128]{1,0:T(8,128)S(1)}, u32[]{:S(2)}, u32[]{:S(2)}) collective-permute-start(f32[264,128]{1,0:T(8,128)S(1)} %add_add_fusion), channel_id=1, source_target_pairs={{0,16},{1,17},{2,18},{3,19},{4,20},{5,21},{6,22},{7,23},{8,24},{9,... | collective-permute-start | bytes 405512 | tf_op jit(solution)/shard_map/ppermute | solution.py:327
  20.9 1.0 %collective-permute-start.7 = (f32[264,128]{1,0:T(8,128)S(1)}, f32[264,128]{1,0:T(8,128)S(1)}, u32[]{:S(2)}, u32[]{:S(2)}) collective-permute-start(f32[264,128]{1,0:T(8,128)S(1)} %get-tuple-element.47), channel_id=1, source_target_pairs={{0,8},{1,9},{2,10},{3,11},{4,12},{5,13},{6,14},{7,15},{8,0},{9,1},... | collective-permute-start | bytes 405512 | tf_op jit(solution)/shard_map/ppermute | solution.py:327
  22.4 5.0 %collective-permute-done.6.refs_3_ = f32[264,128]{1,0:T(8,128)S(1)} collective-permute-done((f32[264,128]{1,0:T(8,128)S(1)}, f32[264,128]{1,0:T(8,128)S(1)}, u32[]{:S(2)}, u32[]{:S(2)}) %collective-permute-start.6) | collective-permute-done | bytes 135200 | tf_op jit(solution)/shard_map/ppermute | solution.py:327
  27.4 1.8 %collective-permute-done.7.refs_4_ = f32[264,128]{1,0:T(8,128)S(1)} collective-permute-done((f32[264,128]{1,0:T(8,128)S(1)}, f32[264,128]{1,0:T(8,128)S(1)}, u32[]{:S(2)}, u32[]{:S(2)}) %collective-permute-start.7) | collective-permute-done | bytes 135200 | tf_op jit(solution)/shard_map/ppermute | solution.py:327
  29.7 1.2 %collective-permute-done.9 = f32[32,128]{1,0:T(8,128)S(1)} collective-permute-done((f32[32,128]{1,0:T(8,128)S(1)}, f32[32,128]{1,0:T(8,128)S(1)}, u32[]{:S(2)}, u32[]{:S(2)}) %collective-permute-start.9) | collective-permute-done | bytes 16416 | tf_op jit(solution)/shard_map/ppermute | solution.py:327
  30.9 1.3 %collective-permute-start.10 = (f32[32,128]{1,0:T(8,128)S(1)}, f32[32,128]{1,0:T(8,128)S(1)}, u32[]{:S(2)}, u32[]{:S(2)}) collective-permute-start(f32[32,128]{1,0:T(8,128)S(1)} %add.24), channel_id=1, source_target_pairs={{0,3},{1,2},{2,1},{3,0},{4,7},{5,6},{6,5},{7,4},{8,11},{9,10},{10,... | collective-permute-start | bytes 49160 | tf_op jit(solution)/shard_map/ppermute | solution.py:327
  32.2 1.9 %collective-permute-done.10 = f32[32,128]{1,0:T(8,128)S(1)} collective-permute-done((f32[32,128]{1,0:T(8,128)S(1)}, f32[32,128]{1,0:T(8,128)S(1)}, u32[]{:S(2)}, u32[]{:S(2)}) %collective-permute-start.10) | collective-permute-done | bytes 16416 | tf_op jit(solution)/shard_map/ppermute | solution.py:327
  34.1 1.2 %collective-permute-start.11 = (f32[32,128]{1,0:T(8,128)S(1)}, f32[32,128]{1,0:T(8,128)S(1)}, u32[]{:S(2)}, u32[]{:S(2)}) collective-permute-start(f32[32,128]{1,0:T(8,128)S(1)} %add.25), channel_id=1, source_target_pairs={{0,5},{1,4},{2,7},{3,6},{4,1},{5,0},{6,3},{7,2},{8,13},{9,12},{10,... | collective-permute-start | bytes 49160 | tf_op jit(solution)/shard_map/ppermute | solution.py:327
  35.3 2.0 %collective-permute-done.11 = f32[32,128]{1,0:T(8,128)S(1)} collective-permute-done((f32[32,128]{1,0:T(8,128)S(1)}, f32[32,128]{1,0:T(8,128)S(1)}, u32[]{:S(2)}, u32[]{:S(2)}) %collective-permute-start.11) | collective-permute-done | bytes 16416 | tf_op jit(solution)/shard_map/ppermute | solution.py:327
  37.3 3.1 %collective-permute-done.12 = f32[32,128]{1,0:T(8,128)S(1)} collective-permute-done((f32[32,128]{1,0:T(8,128)S(1)}, f32[32,128]{1,0:T(8,128)S(1)}, u32[]{:S(2)}, u32[]{:S(2)}) %collective-permute-start.12) | collective-permute-done | bytes 16416 | tf_op jit(solution)/shard_map/ppermute | solution.py:327
  40.4 0.5 %collective-permute-start.13 = (f32[32,128]{1,0:T(8,128)S(1)}, f32[32,128]{1,0:T(8,128)S(1)}, u32[]{:S(2)}, u32[]{:S(2)}) collective-permute-start(f32[32,128]{1,0:T(8,128)S(1)} %add.27.gram_ref.refs_0_), channel_id=1, source_target_pairs={{0,17},{1,16},{2,19},{3,18},{4,21},{5,20},{6,23},{7,22},{8,25},{9,... | collective-permute-start | bytes 49160 | tf_op jit(solution)/shard_map/ppermute | solution.py:327
  41.1 3.3 %collective-permute-done.13.refs_1_ = f32[32,128]{1,0:T(8,128)S(1)} collective-permute-done((f32[32,128]{1,0:T(8,128)S(1)}, f32[32,128]{1,0:T(8,128)S(1)}, u32[]{:S(2)}, u32[]{:S(2)}) %collective-permute-start.13) | collective-permute-done | bytes 16416 | tf_op jit(solution)/shard_map/ppermute | solution.py:327
  44.5 2.6 %orthonormal.1 = f32[64,512]{1,0:T(8,128)} custom-call(f32[32,128]{1,0:T(8,128)S(1)} %add.27.gram_ref.refs_0_, f32[32,128]{1,0:T(8,128)S(1)} %collective-permute-done.13.refs_1_, f32[64,128]{1,0:T(8,128)S(1)} %get-tuple-element.50.refs_2_, f32[64,128]{1,0:T(8,128)S(1)} %get-tuple-element.51.refs_3_, f32[64,512]{1,0:T(8,128)S(1)} %get-tuple-element.52.refs_4_), custom_call_target="tpu_custom_call" | custom-call | tf_op jit(solution)/shard_map/orthonormal/pallas_call | solution.py:311
  (21 shorter events, 2.2 us)
Async XLA Ops:
  0.0 1.9 %copy-start = (bf16[64,4096]{1,0:T(8,128)(2,1)S(1)}, bf16[64,4096]{1,0:T(8,128)(2,1)}, u32[]{:S(2)}) copy-start(bf16[64,4096]{1,0:T(8,128)(2,1)} %basis_ref.1) | copy-start | bytes 1572868
  1.9 0.7 %copy-start.1 = (s32[1,32]{1,0:T(1,128)S(1)}, s32[1,32]{1,0:T(1,128)}, u32[]{:S(2)}) copy-start(s32[1,32]{1,0:T(1,128)} %occ_ref.1) | copy-start | bytes 388
  3.5 1.4 %collective-permute-start = (f32[64,128]{1,0:T(8,128)S(1)}, f32[64,128]{1,0:T(8,128)S(1)}, u32[]{:S(2)}, u32[]{:S(2)}) collective-permute-start(f32[64,128]{1,0:T(8,128)S(1)} %get-tuple-element.31), channel_id=1, source_target_pairs={{0,1},{1,0},{2,3},{3,2},{4,5},{5,4},{6,7},{7,6},{8,9},{9,8},{10,11... | collective-permute-start | bytes 98312 | tf_op jit(solution)/shard_map/ppermute | solution.py:327
  4.8 4.2 %collective-permute-start.1 = (f32[64,128]{1,0:T(8,128)S(1)}, f32[64,128]{1,0:T(8,128)S(1)}, u32[]{:S(2)}, u32[]{:S(2)}) collective-permute-start(f32[64,128]{1,0:T(8,128)S(1)} %add.21.refs_0_), channel_id=1, source_target_pairs={{0,3},{1,2},{2,1},{3,0},{4,7},{5,6},{6,5},{7,4},{8,11},{9,10},{10,... | collective-permute-start | bytes 98312 | tf_op jit(solution)/shard_map/ppermute | solution.py:327
  9.5 6.7 %collective-permute-start.2 = (f32[264,128]{1,0:T(8,128)S(1)}, f32[264,128]{1,0:T(8,128)S(1)}, u32[]{:S(2)}, u32[]{:S(2)}) collective-permute-start(f32[264,128]{1,0:T(8,128)S(1)} %get-tuple-element.38), channel_id=1, source_target_pairs={{0,8},{1,9},{2,10},{3,11},{4,12},{5,13},{6,14},{7,15},{8,0},{9,1},... | collective-permute-start | bytes 405512 | tf_op jit(solution)/shard_map/ppermute | solution.py:327
  11.6 6.6 %collective-permute-start.3 = (f32[264,128]{1,0:T(8,128)S(1)}, f32[264,128]{1,0:T(8,128)S(1)}, u32[]{:S(2)}, u32[]{:S(2)}) collective-permute-start(f32[264,128]{1,0:T(8,128)S(1)} %get-tuple-element.41), channel_id=1, source_target_pairs={{0,4},{1,5},{2,6},{3,7},{4,0},{5,1},{6,2},{7,3},{8,12},{9,13},{10,... | collective-permute-start | bytes 405512 | tf_op jit(solution)/shard_map/ppermute | solution.py:327
  13.1 9.3 %collective-permute-start.5 = (f32[264,128]{1,0:T(8,128)S(1)}, f32[264,128]{1,0:T(8,128)S(1)}, u32[]{:S(2)}, u32[]{:S(2)}) collective-permute-start(f32[264,128]{1,0:T(8,128)S(1)} %get-tuple-element.45), channel_id=1, source_target_pairs={{0,28},{1,29},{2,30},{3,31},{4,24},{5,25},{6,26},{7,27},{8,20},{9,... | collective-permute-start | bytes 405512 | tf_op jit(solution)/shard_map/ppermute | solution.py:327
  16.1 11.3 %collective-permute-start.6 = (f32[264,128]{1,0:T(8,128)S(1)}, f32[264,128]{1,0:T(8,128)S(1)}, u32[]{:S(2)}, u32[]{:S(2)}) collective-permute-start(f32[264,128]{1,0:T(8,128)S(1)} %get-tuple-element.46), channel_id=1, source_target_pairs={{0,12},{1,13},{2,14},{3,15},{4,8},{5,9},{6,10},{7,11},{8,4},{9,5},... | collective-permute-start | bytes 405512 | tf_op jit(solution)/shard_map/ppermute | solution.py:327
  18.2 9.2 %collective-permute-start.4 = (f32[264,128]{1,0:T(8,128)S(1)}, f32[264,128]{1,0:T(8,128)S(1)}, u32[]{:S(2)}, u32[]{:S(2)}) collective-permute-start(f32[264,128]{1,0:T(8,128)S(1)} %add_add_fusion), channel_id=1, source_target_pairs={{0,16},{1,17},{2,18},{3,19},{4,20},{5,21},{6,22},{7,23},{8,24},{9,... | collective-permute-start | bytes 405512 | tf_op jit(solution)/shard_map/ppermute | solution.py:327
  20.9 8.4 %collective-permute-start.7 = (f32[264,128]{1,0:T(8,128)S(1)}, f32[264,128]{1,0:T(8,128)S(1)}, u32[]{:S(2)}, u32[]{:S(2)}) collective-permute-start(f32[264,128]{1,0:T(8,128)S(1)} %get-tuple-element.47), channel_id=1, source_target_pairs={{0,8},{1,9},{2,10},{3,11},{4,12},{5,13},{6,14},{7,15},{8,0},{9,1},... | collective-permute-start | bytes 405512 | tf_op jit(solution)/shard_map/ppermute | solution.py:327
  21.9 7.4 %collective-permute-start.8 = (f32[264,128]{1,0:T(8,128)S(1)}, f32[264,128]{1,0:T(8,128)S(1)}, u32[]{:S(2)}, u32[]{:S(2)}) collective-permute-start(f32[264,128]{1,0:T(8,128)S(1)} %get-tuple-element.48), channel_id=1, source_target_pairs={{0,4},{1,5},{2,6},{3,7},{4,0},{5,1},{6,2},{7,3},{8,12},{9,13},{10,... | collective-permute-start | bytes 405512 | tf_op jit(solution)/shard_map/ppermute | solution.py:327
  29.7 1.2 %collective-permute-start.9 = (f32[32,128]{1,0:T(8,128)S(1)}, f32[32,128]{1,0:T(8,128)S(1)}, u32[]{:S(2)}, u32[]{:S(2)}) collective-permute-start(f32[32,128]{1,0:T(8,128)S(1)} %get-tuple-element.49), channel_id=1, source_target_pairs={{0,1},{1,0},{2,3},{3,2},{4,5},{5,4},{6,7},{7,6},{8,9},{9,8},{10,11... | collective-permute-start | bytes 49160 | tf_op jit(solution)/shard_map/ppermute | solution.py:327
  30.9 3.2 %collective-permute-start.10 = (f32[32,128]{1,0:T(8,128)S(1)}, f32[32,128]{1,0:T(8,128)S(1)}, u32[]{:S(2)}, u32[]{:S(2)}) collective-permute-start(f32[32,128]{1,0:T(8,128)S(1)} %add.24), channel_id=1, source_target_pairs={{0,3},{1,2},{2,1},{3,0},{4,7},{5,6},{6,5},{7,4},{8,11},{9,10},{10,... | collective-permute-start | bytes 49160 | tf_op jit(solution)/shard_map/ppermute | solution.py:327
  34.1 3.2 %collective-permute-start.11 = (f32[32,128]{1,0:T(8,128)S(1)}, f32[32,128]{1,0:T(8,128)S(1)}, u32[]{:S(2)}, u32[]{:S(2)}) collective-permute-start(f32[32,128]{1,0:T(8,128)S(1)} %add.25), channel_id=1, source_target_pairs={{0,5},{1,4},{2,7},{3,6},{4,1},{5,0},{6,3},{7,2},{8,13},{9,12},{10,... | collective-permute-start | bytes 49160 | tf_op jit(solution)/shard_map/ppermute | solution.py:327
  37.2 3.2 %collective-permute-start.12 = (f32[32,128]{1,0:T(8,128)S(1)}, f32[32,128]{1,0:T(8,128)S(1)}, u32[]{:S(2)}, u32[]{:S(2)}) collective-permute-start(f32[32,128]{1,0:T(8,128)S(1)} %add.26), channel_id=1, source_target_pairs={{0,9},{1,8},{2,11},{3,10},{4,13},{5,12},{6,15},{7,14},{8,1},{9,0},... | collective-permute-start | bytes 49160 | tf_op jit(solution)/shard_map/ppermute | solution.py:327
  40.4 4.1 %collective-permute-start.13 = (f32[32,128]{1,0:T(8,128)S(1)}, f32[32,128]{1,0:T(8,128)S(1)}, u32[]{:S(2)}, u32[]{:S(2)}) collective-permute-start(f32[32,128]{1,0:T(8,128)S(1)} %add.27.gram_ref.refs_0_), channel_id=1, source_target_pairs={{0,17},{1,16},{2,19},{3,18},{4,21},{5,20},{6,23},{7,22},{8,25},{9,... | collective-permute-start | bytes 49160 | tf_op jit(solution)/shard_map/ppermute | solution.py:327

commit v3 on v2

--- a/solution.py
+++ b/solution.py
@@ -128,17 +128,20 @@
     row_sums = jnp.sum(jnp.where(eye, jnp.sum(scores, axis=1, keepdims=True), 0.0), axis=0, keepdims=True)
     chunks = high_ref.shape[1] // (LANES * lax.axis_size("cells"))
     width = chunks * LANES
-    for pick, out in zip(picks, outs):
+    blocks = [(pick, out, at) for group, out in zip(picks, outs) for at, pick in enumerate(group)]
+    rows = block_rows(comps, chunks)
+    for pick, out, at_block in blocks:
+        base = at_block * rows
         start = pl.multiple_of((me_ref[0] ^ pick) * width, width)
         lanes = pl.ds(start, width)
         piece = spread_piece(terms, high_ref[:, lanes], low_ref[:, lanes]) * occ_ref[:, lanes]
         sums = sum_ref[:, lanes] * occ_ref[:, lanes]
         extra = [row_sums]
         for at in range(chunks):
-            out[at * comps:(at + 1) * comps] = piece[:, at * LANES:(at + 1) * LANES]
+            out[base + at * comps:base + (at + 1) * comps] = piece[:, at * LANES:(at + 1) * LANES]
             extra.append(sums[:, at * LANES:(at + 1) * LANES])
-        extra.append(jnp.zeros((out.shape[0] - chunks * comps - chunks - 1, LANES), F32))
-        out[chunks * comps:] = jnp.concatenate(extra, axis=0)
+        extra.append(jnp.zeros((rows - chunks * comps - chunks - 1, LANES), F32))
+        out[base + chunks * comps:base + rows] = jnp.concatenate(extra, axis=0)
 
 
 def block_rows(comps, chunks):
@@ -148,15 +151,16 @@
 def spread_pieces(me, scores, high, low, sums, occ, picks):
     comps = scores[0].shape[0]
     chunks = high.shape[1] // (LANES * lax.axis_size("cells"))
-    block = jax.ShapeDtypeStruct((block_rows(comps, chunks), LANES), F32)
+    rows = block_rows(comps, chunks)
+    count = sum(len(group) for group in picks)
     return pl.pallas_call(
         functools.partial(spread_kernel, len(scores), picks),
-        out_shape=[block] * len(picks),
+        out_shape=[jax.ShapeDtypeStruct((len(group) * rows, LANES), F32) for group in picks],
         in_specs=[SCALARS] + [WHOLE] * (len(scores) + 4),
         out_specs=[WHOLE] * len(picks),
         compiler_params=PARAMS,
         cost_estimate=pl.CostEstimate(
-            flops=10 * comps * len(picks) * chunks * LANES * high.shape[0], bytes_accessed=2**21, transcendentals=0
+            flops=10 * comps * count * chunks * LANES * high.shape[0], bytes_accessed=2**21, transcendentals=0
         ),
         name="spread",
     )(me, *scores, high, low, sums, occ)
@@ -165,7 +169,8 @@
 def gram_kernel(scale, chunks, *refs):
     pieces, (spread_ref, gram_ref) = refs[:-2], refs[-2:]
     comps = spread_ref.shape[0]
-    total = tree_sum([ref[...] for ref in pieces])
+    rows = block_rows(comps, chunks)
+    total = tree_sum([ref[ref.shape[0] - rows:] for ref in pieces])
     extra = total[chunks * comps:chunks * comps + chunks + 1]
     eye = lax.broadcasted_iota(jnp.int32, (comps, LANES), 0) == lax.broadcasted_iota(jnp.int32, (comps, LANES), 1)
     row_sums = jnp.sum(jnp.where(eye, extra[:1], 0.0), axis=1, keepdims=True) * scale
@@ -347,16 +352,16 @@
     comps = scores[0].shape[0]
     me = lax.axis_index("cells").astype(jnp.int32).reshape(1)
     make = functools.partial(spread_pieces, scores=scores, high=high, low=low, sums=sums, occ=occ)
-    first = list(make(me, picks=[6, 5, 7]))
-    first[0], me = lax.optimization_barrier((first[0], me))
-    came = [send(x, k - 4, 0) for k, x in zip((6, 5), first)]
-    straight = [send(first[2], 7, 0)]
-    far, own, *second = make(me, picks=[4, 0, 3, 2, 1])
-    came[0], second[0] = lax.optimization_barrier((came[0], second[0]))
-    far = tree_sum([far] + came)
-    far, second[1], second[2] = lax.optimization_barrier((far, second[1], second[2]))
-    straight += [send(x, k, 0) for k, x in zip((3, 2, 1), second)]
-    return centered_gram([own, send(far, 4, 0)] + straight, comps, cell_total)
+    pair, first, across = make(me, picks=[[6, 2], [5], [7]])
+    pair, me = lax.optimization_barrier((pair, me))
+    pair, first = send(pair, 2, 0), send(first, 1, 0)
+    across = send(across, 7, 0)
+    far, own, *second = make(me, picks=[[4], [0], [3], [1]])
+    first, second[0] = lax.optimization_barrier((first, second[0]))
+    far, second[1] = lax.optimization_barrier((tree_sum([far, pair[:far.shape[0]], first]), second[1]))
+    far = send(far, 4, 0)
+    straight = [send(x, k, 0) for k, x in zip((3, 1), second)]
+    return centered_gram([own, far, pair, across] + straight, comps, cell_total)
 
 
 def all_alike(counts, occupancy, start_basis):

time: 47.2 us -> 46.9 us (level)
  waiting for transfers between devices: 20.8 us -> 16.8 us
  starting transfers between devices: 18.5 us -> 22.2 us
    ppermute x14 -> x13, waiting for transfers between devices: 20.8 us -> 16.8 us  [send(): return lax.ppermute(x, ('cells', 'genes'), pairs)]
    ppermute x14 -> x13, starting transfers between devices: 18.5 us -> 22.2 us  [send(): return lax.ppermute(x, ('cells', 'genes'), pairs)]
  transfers between devices with their start and end apart: 14 -> 13, of which waited for: 9 -> 12; matrix products, arithmetic and copies ran while one was open for 0% -> 0% of each run, Pallas kernels for 2% -> 2%
where the time goes in v3:
time: 46.9 us; the launch traced here: 46.8 us
  starting transfers between devices  22.2 us (47%)
  waiting for transfers between devices  16.8 us (36%)
  Pallas kernels  6.98 us (15%)
  local copies, waits for them, and re-layouts  0.64 us (1%)
    ppermute x13, starting transfers between devices, send(): return lax.ppermute(x, ('cells', 'genes'), pairs)  22.2 us
    ppermute x13, waiting for transfers between devices, send(): return lax.ppermute(x, ('cells', 'genes'), pairs)  16.8 us
    pallas_call x1, Pallas kernels, orthonormal(): pl.pallas_call(functools.partial(basis_kernel, scale), out_shape=jax.Shap...  2.58 us
    pallas_call x1, Pallas kernels, log_terms(): pl.pallas_call(functools.partial(log_kernel, width), out_shape=(jax.Shape...  1.92 us
    pallas_call x2, Pallas kernels, spread_pieces(): pl.pallas_call(functools.partial(spread_kernel, len(scores), picks), out_...  0.98 us
  transfers between devices with their start and end apart: 13, of which 12 were waited for; matrix products, arithmetic and copies ran while one was open for 0% of the time, Pallas kernels for 2%

profile of v3, /device:TPU:0, one launch (start us, length us, event | category | flops | bytes accessed | tf_op | source)
XLA Modules:
  0.0 46.8 jit_solution(14157929214826717300)
XLA Ops:
  0.0 1.9 %log_terms.1 = (bf16[128,4096]{1,0:T(8,128)(2,1)S(1)}, bf16[128,4096]{1,0:T(8,128)(2,1)S(1)}, f32[1,4096]{1,0:T(1,128)S(1)}) custom-call(bf16[128,4096]{1,0:T(8,128)(2,1)} %counts_hbm.1), custom_call_target="tpu_custom_call" | custom-call | flops 10485760 | bytes 4194304 | tf_op jit(solution)/shard_map/log_terms/pallas_call | solution.py:65
  2.6 0.9 %scores.1 = (f32[64,128]{1,0:T(8,128)S(1)}, f32[1,4096]{1,0:T(1,128)S(1)}) custom-call(s32[1,32]{1,0:T(1,128)S(1)} %copy-done.1, bf16[64,4096]{1,0:T(8,128)(2,1)S(1)} %copy-done, bf16[128,4096]{1,0:T(8,128)(2,1)S(1)} %get-tuple-element.27.high_ref.refs_2_, bf16[128,4096]{1,0:T(8,128)(2,1)S(1)} %get-tuple-element.28.low_ref.refs_3_), custom_call_target="tpu_custom_call" | custom-call | tf_op jit(solution)/shard_map/scores/pallas_call | solution.py:102
  4.0 0.9 %collective-permute-done = f32[64,128]{1,0:T(8,128)S(1)} collective-permute-done((f32[64,128]{1,0:T(8,128)S(1)}, f32[64,128]{1,0:T(8,128)S(1)}, u32[]{:S(2)}, u32[]{:S(2)}) %collective-permute-start) | collective-permute-done | bytes 32800 | tf_op jit(solution)/shard_map/ppermute | solution.py:332
  4.8 2.6 %collective-permute-start.1 = (f32[64,128]{1,0:T(8,128)S(1)}, f32[64,128]{1,0:T(8,128)S(1)}, u32[]{:S(2)}, u32[]{:S(2)}) collective-permute-start(f32[64,128]{1,0:T(8,128)S(1)} %add.21.refs_0_), channel_id=1, source_target_pairs={{0,3},{1,2},{2,1},{3,0},{4,7},{5,6},{6,5},{7,4},{8,11},{9,10},{10,... | collective-permute-start | bytes 98312 | tf_op jit(solution)/shard_map/ppermute | solution.py:332
  7.5 1.6 %collective-permute-done.1.refs_1_ = f32[64,128]{1,0:T(8,128)S(1)} collective-permute-done((f32[64,128]{1,0:T(8,128)S(1)}, f32[64,128]{1,0:T(8,128)S(1)}, u32[]{:S(2)}, u32[]{:S(2)}) %collective-permute-start.1) | collective-permute-done | bytes 32800 | tf_op jit(solution)/shard_map/ppermute | solution.py:332
  9.5 2.1 %collective-permute-start.2 = (f32[528,128]{1,0:T(8,128)S(1)}, f32[528,128]{1,0:T(8,128)S(1)}, u32[]{:S(2)}, u32[]{:S(2)}) collective-permute-start(f32[528,128]{1,0:T(8,128)S(1)} %get-tuple-element.36), channel_id=1, source_target_pairs={{0,8},{1,9},{2,10},{3,11},{4,12},{5,13},{6,14},{7,15},{8,0},{9,1},... | collective-permute-start | bytes 811016 | tf_op jit(solution)/shard_map/ppermute | solution.py:332
  11.7 1.5 %collective-permute-start.3 = (f32[264,128]{1,0:T(8,128)S(1)}, f32[264,128]{1,0:T(8,128)S(1)}, u32[]{:S(2)}, u32[]{:S(2)}) collective-permute-start(f32[264,128]{1,0:T(8,128)S(1)} %get-tuple-element.37), channel_id=1, source_target_pairs={{0,4},{1,5},{2,6},{3,7},{4,0},{5,1},{6,2},{7,3},{8,12},{9,13},{10,... | collective-permute-start | bytes 405512 | tf_op jit(solution)/shard_map/ppermute | solution.py:332
  13.2 2.4 %collective-permute-start.5 = (f32[264,128]{1,0:T(8,128)S(1)}, f32[264,128]{1,0:T(8,128)S(1)}, u32[]{:S(2)}, u32[]{:S(2)}) collective-permute-start(f32[264,128]{1,0:T(8,128)S(1)} %get-tuple-element.42), channel_id=1, source_target_pairs={{0,28},{1,29},{2,30},{3,31},{4,24},{5,25},{6,26},{7,27},{8,20},{9,... | collective-permute-start | bytes 405512 | tf_op jit(solution)/shard_map/ppermute | solution.py:332
  16.1 0.9 %collective-permute-done.3 = f32[264,128]{1,0:T(8,128)S(1)} collective-permute-done((f32[264,128]{1,0:T(8,128)S(1)}, f32[264,128]{1,0:T(8,128)S(1)}, u32[]{:S(2)}, u32[]{:S(2)}) %collective-permute-start.3) | collective-permute-done | bytes 135200 | tf_op jit(solution)/shard_map/ppermute | solution.py:332
  17.1 4.3 %collective-permute-start.6 = (f32[264,128]{1,0:T(8,128)S(1)}, f32[264,128]{1,0:T(8,128)S(1)}, u32[]{:S(2)}, u32[]{:S(2)}) collective-permute-start(f32[264,128]{1,0:T(8,128)S(1)} %get-tuple-element.43), channel_id=1, source_target_pairs={{0,12},{1,13},{2,14},{3,15},{4,8},{5,9},{6,10},{7,11},{8,4},{9,5},... | collective-permute-start | bytes 405512 | tf_op jit(solution)/shard_map/ppermute | solution.py:332
  21.4 1.5 %collective-permute-start.4 = (f32[264,128]{1,0:T(8,128)S(1)}, f32[264,128]{1,0:T(8,128)S(1)}, u32[]{:S(2)}, u32[]{:S(2)}) collective-permute-start(f32[264,128]{1,0:T(8,128)S(1)} %fusion), channel_id=1, source_target_pairs={{0,16},{1,17},{2,18},{3,19},{4,20},{5,21},{6,22},{7,23},{8,24},{9,... | collective-permute-start | bytes 405512 | tf_op jit(solution)/shard_map/ppermute | solution.py:332
  22.9 1.3 %collective-permute-start.7 = (f32[264,128]{1,0:T(8,128)S(1)}, f32[264,128]{1,0:T(8,128)S(1)}, u32[]{:S(2)}, u32[]{:S(2)}) collective-permute-start(f32[264,128]{1,0:T(8,128)S(1)} %get-tuple-element.44), channel_id=1, source_target_pairs={{0,4},{1,5},{2,6},{3,7},{4,0},{5,1},{6,2},{7,3},{8,12},{9,13},{10,... | collective-permute-start | bytes 405512 | tf_op jit(solution)/shard_map/ppermute | solution.py:332
  24.2 1.2 %collective-permute-done.5.refs_3_ = f32[264,128]{1,0:T(8,128)S(1)} collective-permute-done((f32[264,128]{1,0:T(8,128)S(1)}, f32[264,128]{1,0:T(8,128)S(1)}, u32[]{:S(2)}, u32[]{:S(2)}) %collective-permute-start.5) | collective-permute-done | bytes 135200 | tf_op jit(solution)/shard_map/ppermute | solution.py:332
  25.4 2.9 %collective-permute-done.6.refs_4_ = f32[264,128]{1,0:T(8,128)S(1)} collective-permute-done((f32[264,128]{1,0:T(8,128)S(1)}, f32[264,128]{1,0:T(8,128)S(1)}, u32[]{:S(2)}, u32[]{:S(2)}) %collective-permute-start.6) | collective-permute-done | bytes 135200 | tf_op jit(solution)/shard_map/ppermute | solution.py:332
  29.4 1.2 %collective-permute-done.8 = f32[32,128]{1,0:T(8,128)S(1)} collective-permute-done((f32[32,128]{1,0:T(8,128)S(1)}, f32[32,128]{1,0:T(8,128)S(1)}, u32[]{:S(2)}, u32[]{:S(2)}) %collective-permute-start.8) | collective-permute-done | bytes 16416 | tf_op jit(solution)/shard_map/ppermute | solution.py:332
  30.6 1.3 %collective-permute-start.9 = (f32[32,128]{1,0:T(8,128)S(1)}, f32[32,128]{1,0:T(8,128)S(1)}, u32[]{:S(2)}, u32[]{:S(2)}) collective-permute-start(f32[32,128]{1,0:T(8,128)S(1)} %add.24), channel_id=1, source_target_pairs={{0,3},{1,2},{2,1},{3,0},{4,7},{5,6},{6,5},{7,4},{8,11},{9,10},{10,... | collective-permute-start | bytes 49160 | tf_op jit(solution)/shard_map/ppermute | solution.py:332
  31.8 1.9 %collective-permute-done.9 = f32[32,128]{1,0:T(8,128)S(1)} collective-permute-done((f32[32,128]{1,0:T(8,128)S(1)}, f32[32,128]{1,0:T(8,128)S(1)}, u32[]{:S(2)}, u32[]{:S(2)}) %collective-permute-start.9) | collective-permute-done | bytes 16416 | tf_op jit(solution)/shard_map/ppermute | solution.py:332
  33.7 1.0 %collective-permute-start.10 = (f32[32,128]{1,0:T(8,128)S(1)}, f32[32,128]{1,0:T(8,128)S(1)}, u32[]{:S(2)}, u32[]{:S(2)}) collective-permute-start(f32[32,128]{1,0:T(8,128)S(1)} %add.25), channel_id=1, source_target_pairs={{0,5},{1,4},{2,7},{3,6},{4,1},{5,0},{6,3},{7,2},{8,13},{9,12},{10,... | collective-permute-start | bytes 49160 | tf_op jit(solution)/shard_map/ppermute | solution.py:332
  34.7 2.2 %collective-permute-done.10 = f32[32,128]{1,0:T(8,128)S(1)} collective-permute-done((f32[32,128]{1,0:T(8,128)S(1)}, f32[32,128]{1,0:T(8,128)S(1)}, u32[]{:S(2)}, u32[]{:S(2)}) %collective-permute-start.10) | collective-permute-done | bytes 16416 | tf_op jit(solution)/shard_map/ppermute | solution.py:332
  36.9 1.8 %collective-permute-start.11 = (f32[32,128]{1,0:T(8,128)S(1)}, f32[32,128]{1,0:T(8,128)S(1)}, u32[]{:S(2)}, u32[]{:S(2)}) collective-permute-start(f32[32,128]{1,0:T(8,128)S(1)} %add.26), channel_id=1, source_target_pairs={{0,9},{1,8},{2,11},{3,10},{4,13},{5,12},{6,15},{7,14},{8,1},{9,0},... | collective-permute-start | bytes 49160 | tf_op jit(solution)/shard_map/ppermute | solution.py:332
  38.7 1.4 %collective-permute-done.11 = f32[32,128]{1,0:T(8,128)S(1)} collective-permute-done((f32[32,128]{1,0:T(8,128)S(1)}, f32[32,128]{1,0:T(8,128)S(1)}, u32[]{:S(2)}, u32[]{:S(2)}) %collective-permute-start.11) | collective-permute-done | bytes 16416 | tf_op jit(solution)/shard_map/ppermute | solution.py:332
  40.1 2.0 %collective-permute-start.12 = (f32[32,128]{1,0:T(8,128)S(1)}, f32[32,128]{1,0:T(8,128)S(1)}, u32[]{:S(2)}, u32[]{:S(2)}) collective-permute-start(f32[32,128]{1,0:T(8,128)S(1)} %add.27.gram_ref.refs_0_), channel_id=1, source_target_pairs={{0,17},{1,16},{2,19},{3,18},{4,21},{5,20},{6,23},{7,22},{8,25},{9,... | collective-permute-start | bytes 49160 | tf_op jit(solution)/shard_map/ppermute | solution.py:332
  42.3 1.9 %collective-permute-done.12.refs_1_ = f32[32,128]{1,0:T(8,128)S(1)} collective-permute-done((f32[32,128]{1,0:T(8,128)S(1)}, f32[32,128]{1,0:T(8,128)S(1)}, u32[]{:S(2)}, u32[]{:S(2)}) %collective-permute-start.12) | collective-permute-done | bytes 16416 | tf_op jit(solution)/shard_map/ppermute | solution.py:332
  44.2 2.6 %orthonormal.1 = f32[64,512]{1,0:T(8,128)} custom-call(f32[32,128]{1,0:T(8,128)S(1)} %add.27.gram_ref.refs_0_, f32[32,128]{1,0:T(8,128)S(1)} %collective-permute-done.12.refs_1_, f32[64,128]{1,0:T(8,128)S(1)} %get-tuple-element.46.refs_2_, f32[64,128]{1,0:T(8,128)S(1)} %get-tuple-element.47.refs_3_, f32[64,512]{1,0:T(8,128)S(1)} %get-tuple-element.48.refs_4_), custom_call_target="tpu_custom_call" | custom-call | tf_op jit(solution)/shard_map/orthonormal/pallas_call | solution.py:316
  (19 shorter events, 3.5 us)
Async XLA Ops:
  0.0 1.9 %copy-start = (bf16[64,4096]{1,0:T(8,128)(2,1)S(1)}, bf16[64,4096]{1,0:T(8,128)(2,1)}, u32[]{:S(2)}) copy-start(bf16[64,4096]{1,0:T(8,128)(2,1)} %basis_ref.1) | copy-start | bytes 1572868
  1.9 0.7 %copy-start.1 = (s32[1,32]{1,0:T(1,128)S(1)}, s32[1,32]{1,0:T(1,128)}, u32[]{:S(2)}) copy-start(s32[1,32]{1,0:T(1,128)} %occ_ref.1) | copy-start | bytes 388
  3.5 1.4 %collective-permute-start = (f32[64,128]{1,0:T(8,128)S(1)}, f32[64,128]{1,0:T(8,128)S(1)}, u32[]{:S(2)}, u32[]{:S(2)}) collective-permute-start(f32[64,128]{1,0:T(8,128)S(1)} %get-tuple-element.29), channel_id=1, source_target_pairs={{0,1},{1,0},{2,3},{3,2},{4,5},{5,4},{6,7},{7,6},{8,9},{9,8},{10,11... | collective-permute-start | bytes 98312 | tf_op jit(solution)/shard_map/ppermute | solution.py:332
  4.8 4.2 %collective-permute-start.1 = (f32[64,128]{1,0:T(8,128)S(1)}, f32[64,128]{1,0:T(8,128)S(1)}, u32[]{:S(2)}, u32[]{:S(2)}) collective-permute-start(f32[64,128]{1,0:T(8,128)S(1)} %add.21.refs_0_), channel_id=1, source_target_pairs={{0,3},{1,2},{2,1},{3,0},{4,7},{5,6},{6,5},{7,4},{8,11},{9,10},{10,... | collective-permute-start | bytes 98312 | tf_op jit(solution)/shard_map/ppermute | solution.py:332
  9.5 11.8 %collective-permute-start.2 = (f32[528,128]{1,0:T(8,128)S(1)}, f32[528,128]{1,0:T(8,128)S(1)}, u32[]{:S(2)}, u32[]{:S(2)}) collective-permute-start(f32[528,128]{1,0:T(8,128)S(1)} %get-tuple-element.36), channel_id=1, source_target_pairs={{0,8},{1,9},{2,10},{3,11},{4,12},{5,13},{6,14},{7,15},{8,0},{9,1},... | collective-permute-start | bytes 811016 | tf_op jit(solution)/shard_map/ppermute | solution.py:332
  11.7 5.4 %collective-permute-start.3 = (f32[264,128]{1,0:T(8,128)S(1)}, f32[264,128]{1,0:T(8,128)S(1)}, u32[]{:S(2)}, u32[]{:S(2)}) collective-permute-start(f32[264,128]{1,0:T(8,128)S(1)} %get-tuple-element.37), channel_id=1, source_target_pairs={{0,4},{1,5},{2,6},{3,7},{4,0},{5,1},{6,2},{7,3},{8,12},{9,13},{10,... | collective-permute-start | bytes 405512 | tf_op jit(solution)/shard_map/ppermute | solution.py:332
  13.2 12.2 %collective-permute-start.5 = (f32[264,128]{1,0:T(8,128)S(1)}, f32[264,128]{1,0:T(8,128)S(1)}, u32[]{:S(2)}, u32[]{:S(2)}) collective-permute-start(f32[264,128]{1,0:T(8,128)S(1)} %get-tuple-element.42), channel_id=1, source_target_pairs={{0,28},{1,29},{2,30},{3,31},{4,24},{5,25},{6,26},{7,27},{8,20},{9,... | collective-permute-start | bytes 405512 | tf_op jit(solution)/shard_map/ppermute | solution.py:332
  17.1 11.2 %collective-permute-start.6 = (f32[264,128]{1,0:T(8,128)S(1)}, f32[264,128]{1,0:T(8,128)S(1)}, u32[]{:S(2)}, u32[]{:S(2)}) collective-permute-start(f32[264,128]{1,0:T(8,128)S(1)} %get-tuple-element.43), channel_id=1, source_target_pairs={{0,12},{1,13},{2,14},{3,15},{4,8},{5,9},{6,10},{7,11},{8,4},{9,5},... | collective-permute-start | bytes 405512 | tf_op jit(solution)/shard_map/ppermute | solution.py:332
  21.4 7.4 %collective-permute-start.4 = (f32[264,128]{1,0:T(8,128)S(1)}, f32[264,128]{1,0:T(8,128)S(1)}, u32[]{:S(2)}, u32[]{:S(2)}) collective-permute-start(f32[264,128]{1,0:T(8,128)S(1)} %fusion), channel_id=1, source_target_pairs={{0,16},{1,17},{2,18},{3,19},{4,20},{5,21},{6,22},{7,23},{8,24},{9,... | collective-permute-start | bytes 405512 | tf_op jit(solution)/shard_map/ppermute | solution.py:332
  22.9 6.0 %collective-permute-start.7 = (f32[264,128]{1,0:T(8,128)S(1)}, f32[264,128]{1,0:T(8,128)S(1)}, u32[]{:S(2)}, u32[]{:S(2)}) collective-permute-start(f32[264,128]{1,0:T(8,128)S(1)} %get-tuple-element.44), channel_id=1, source_target_pairs={{0,4},{1,5},{2,6},{3,7},{4,0},{5,1},{6,2},{7,3},{8,12},{9,13},{10,... | collective-permute-start | bytes 405512 | tf_op jit(solution)/shard_map/ppermute | solution.py:332
  29.4 1.2 %collective-permute-start.8 = (f32[32,128]{1,0:T(8,128)S(1)}, f32[32,128]{1,0:T(8,128)S(1)}, u32[]{:S(2)}, u32[]{:S(2)}) collective-permute-start(f32[32,128]{1,0:T(8,128)S(1)} %get-tuple-element.45), channel_id=1, source_target_pairs={{0,1},{1,0},{2,3},{3,2},{4,5},{5,4},{6,7},{7,6},{8,9},{9,8},{10,11... | collective-permute-start | bytes 49160 | tf_op jit(solution)/shard_map/ppermute | solution.py:332
  30.6 3.2 %collective-permute-start.9 = (f32[32,128]{1,0:T(8,128)S(1)}, f32[32,128]{1,0:T(8,128)S(1)}, u32[]{:S(2)}, u32[]{:S(2)}) collective-permute-start(f32[32,128]{1,0:T(8,128)S(1)} %add.24), channel_id=1, source_target_pairs={{0,3},{1,2},{2,1},{3,0},{4,7},{5,6},{6,5},{7,4},{8,11},{9,10},{10,... | collective-permute-start | bytes 49160 | tf_op jit(solution)/shard_map/ppermute | solution.py:332
  33.7 3.2 %collective-permute-start.10 = (f32[32,128]{1,0:T(8,128)S(1)}, f32[32,128]{1,0:T(8,128)S(1)}, u32[]{:S(2)}, u32[]{:S(2)}) collective-permute-start(f32[32,128]{1,0:T(8,128)S(1)} %add.25), channel_id=1, source_target_pairs={{0,5},{1,4},{2,7},{3,6},{4,1},{5,0},{6,3},{7,2},{8,13},{9,12},{10,... | collective-permute-start | bytes 49160 | tf_op jit(solution)/shard_map/ppermute | solution.py:332
  36.9 3.2 %collective-permute-start.11 = (f32[32,128]{1,0:T(8,128)S(1)}, f32[32,128]{1,0:T(8,128)S(1)}, u32[]{:S(2)}, u32[]{:S(2)}) collective-permute-start(f32[32,128]{1,0:T(8,128)S(1)} %add.26), channel_id=1, source_target_pairs={{0,9},{1,8},{2,11},{3,10},{4,13},{5,12},{6,15},{7,14},{8,1},{9,0},... | collective-permute-start | bytes 49160 | tf_op jit(solution)/shard_map/ppermute | solution.py:332
  40.1 4.1 %collective-permute-start.12 = (f32[32,128]{1,0:T(8,128)S(1)}, f32[32,128]{1,0:T(8,128)S(1)}, u32[]{:S(2)}, u32[]{:S(2)}) collective-permute-start(f32[32,128]{1,0:T(8,128)S(1)} %add.27.gram_ref.refs_0_), channel_id=1, source_target_pairs={{0,17},{1,16},{2,19},{3,18},{4,21},{5,20},{6,23},{7,22},{8,25},{9,... | collective-permute-start | bytes 49160 | tf_op jit(solution)/shard_map/ppermute | solution.py:332

commit v4 on v3

--- a/solution.py
+++ b/solution.py
@@ -333,16 +333,15 @@
 
 
 def gene_terms(x):
-    terms = [x, send(x, 0, 1)]
-    for at in range(1, lax.axis_size("genes").bit_length() - 1):
-        x = tree_sum(terms)
-        terms = [x, send(x, 0, 1 << at | 1)]
-    return terms
-
-
-def cell_terms(x):
-    terms = [x]
-    for at in range(lax.axis_size("cells").bit_length() - 1):
+    x = x + send(x, 0, 1)
+    return [x, send(x, 0, 3)]
+
+
+def all_terms(x):
+    x = x + send(x, 0, 1)
+    across = [send(x, c, g) for c, g in ((1, 3), (1, 1), (0, 3))]
+    terms = [x + across[2], across[1] + across[0]]
+    for at in range(1, lax.axis_size("cells").bit_length() - 1):
         x = tree_sum(terms)
         terms = [x, send(x, 1 << at, 1)]
     return terms
@@ -384,7 +383,7 @@
     scores, occ = score_part(occupancy, start_basis, high, low)
     cell_total = counts.shape[0] * lax.axis_size("cells")
     spread, gram = scattered_spread(gene_terms(scores), high, low, sums, occ, cell_total)
-    return cell_terms(tree_sum(gene_terms(gram))), spread
+    return all_terms(gram), spread
 
 
 def on_device(counts, occupancy, start_basis):

time: 46.9 us -> 46.5 us (level)
  waiting for transfers between devices: 16.8 us -> 15.5 us
  starting transfers between devices: 22.2 us -> 23.1 us
    ppermute x13 -> x14, waiting for transfers between devices: 16.8 us -> 15.5 us  [send(): return lax.ppermute(x, ('cells', 'genes'), pairs)]
    ppermute x13 -> x14, starting transfers between devices: 22.2 us -> 23.1 us  [send(): return lax.ppermute(x, ('cells', 'genes'), pairs)]
  transfers between devices with their start and end apart: 13 -> 14, of which waited for: 12 -> 13; matrix products, arithmetic and copies ran while one was open for 0% -> 0% of each run, Pallas kernels for 2% -> 2%
where the time goes in v4:
time: 46.5 us; the launch traced here: 46.3 us
  starting transfers between devices  23.1 us (50%)
  waiting for transfers between devices  15.5 us (33%)
  Pallas kernels  6.98 us (15%)
  local copies, waits for them, and re-layouts  0.64 us (1%)
    ppermute x14, starting transfers between devices, send(): return lax.ppermute(x, ('cells', 'genes'), pairs)  23.1 us
    ppermute x14, waiting for transfers between devices, send(): return lax.ppermute(x, ('cells', 'genes'), pairs)  15.5 us
    pallas_call x1, Pallas kernels, orthonormal(): pl.pallas_call(functools.partial(basis_kernel, scale), out_shape=jax.Shap...  2.58 us
    pallas_call x1, Pallas kernels, log_terms(): pl.pallas_call(functools.partial(log_kernel, width), out_shape=(jax.Shape...  1.92 us
    pallas_call x2, Pallas kernels, spread_pieces(): pl.pallas_call(functools.partial(spread_kernel, len(scores), picks), out_...  0.98 us
  transfers between devices with their start and end apart: 14, of which 13 were waited for; matrix products, arithmetic and copies ran while one was open for 0% of the time, Pallas kernels for 2%

profile of v4, /device:TPU:0, one launch (start us, length us, event | category | flops | bytes accessed | tf_op | source)
XLA Modules:
  0.0 46.3 jit_solution(194691978858719043)
XLA Ops:
  0.0 1.9 %log_terms.1 = (bf16[128,4096]{1,0:T(8,128)(2,1)S(1)}, bf16[128,4096]{1,0:T(8,128)(2,1)S(1)}, f32[1,4096]{1,0:T(1,128)S(1)}) custom-call(bf16[128,4096]{1,0:T(8,128)(2,1)} %counts_hbm.1), custom_call_target="tpu_custom_call" | custom-call | flops 10485760 | bytes 4194304 | tf_op jit(solution)/shard_map/log_terms/pallas_call | solution.py:65
  2.6 0.9 %scores.1 = (f32[64,128]{1,0:T(8,128)S(1)}, f32[1,4096]{1,0:T(1,128)S(1)}) custom-call(s32[1,32]{1,0:T(1,128)S(1)} %copy-done.1, bf16[64,4096]{1,0:T(8,128)(2,1)S(1)} %copy-done, bf16[128,4096]{1,0:T(8,128)(2,1)S(1)} %get-tuple-element.27.high_ref.refs_2_, bf16[128,4096]{1,0:T(8,128)(2,1)S(1)} %get-tuple-element.28.low_ref.refs_3_), custom_call_target="tpu_custom_call" | custom-call | tf_op jit(solution)/shard_map/scores/pallas_call | solution.py:102
  4.0 0.9 %collective-permute-done = f32[64,128]{1,0:T(8,128)S(1)} collective-permute-done((f32[64,128]{1,0:T(8,128)S(1)}, f32[64,128]{1,0:T(8,128)S(1)}, u32[]{:S(2)}, u32[]{:S(2)}) %collective-permute-start) | collective-permute-done | bytes 32800 | tf_op jit(solution)/shard_map/ppermute | solution.py:332
  4.8 2.6 %collective-permute-start.1 = (f32[64,128]{1,0:T(8,128)S(1)}, f32[64,128]{1,0:T(8,128)S(1)}, u32[]{:S(2)}, u32[]{:S(2)}) collective-permute-start(f32[64,128]{1,0:T(8,128)S(1)} %add.24.refs_0_), channel_id=1, source_target_pairs={{0,3},{1,2},{2,1},{3,0},{4,7},{5,6},{6,5},{7,4},{8,11},{9,10},{10,... | collective-permute-start | bytes 98312 | tf_op jit(solution)/shard_map/ppermute | solution.py:332
  7.5 1.6 %collective-permute-done.1.refs_1_ = f32[64,128]{1,0:T(8,128)S(1)} collective-permute-done((f32[64,128]{1,0:T(8,128)S(1)}, f32[64,128]{1,0:T(8,128)S(1)}, u32[]{:S(2)}, u32[]{:S(2)}) %collective-permute-start.1) | collective-permute-done | bytes 32800 | tf_op jit(solution)/shard_map/ppermute | solution.py:332
  9.5 2.1 %collective-permute-start.2 = (f32[528,128]{1,0:T(8,128)S(1)}, f32[528,128]{1,0:T(8,128)S(1)}, u32[]{:S(2)}, u32[]{:S(2)}) collective-permute-start(f32[528,128]{1,0:T(8,128)S(1)} %get-tuple-element.36), channel_id=1, source_target_pairs={{0,8},{1,9},{2,10},{3,11},{4,12},{5,13},{6,14},{7,15},{8,0},{9,1},... | collective-permute-start | bytes 811016 | tf_op jit(solution)/shard_map/ppermute | solution.py:332
  11.7 1.5 %collective-permute-start.3 = (f32[264,128]{1,0:T(8,128)S(1)}, f32[264,128]{1,0:T(8,128)S(1)}, u32[]{:S(2)}, u32[]{:S(2)}) collective-permute-start(f32[264,128]{1,0:T(8,128)S(1)} %get-tuple-element.37), channel_id=1, source_target_pairs={{0,4},{1,5},{2,6},{3,7},{4,0},{5,1},{6,2},{7,3},{8,12},{9,13},{10,... | collective-permute-start | bytes 405512 | tf_op jit(solution)/shard_map/ppermute | solution.py:332
  13.2 2.4 %collective-permute-start.5 = (f32[264,128]{1,0:T(8,128)S(1)}, f32[264,128]{1,0:T(8,128)S(1)}, u32[]{:S(2)}, u32[]{:S(2)}) collective-permute-start(f32[264,128]{1,0:T(8,128)S(1)} %get-tuple-element.42), channel_id=1, source_target_pairs={{0,28},{1,29},{2,30},{3,31},{4,24},{5,25},{6,26},{7,27},{8,20},{9,... | collective-permute-start | bytes 405512 | tf_op jit(solution)/shard_map/ppermute | solution.py:332
  16.1 0.9 %collective-permute-done.3 = f32[264,128]{1,0:T(8,128)S(1)} collective-permute-done((f32[264,128]{1,0:T(8,128)S(1)}, f32[264,128]{1,0:T(8,128)S(1)}, u32[]{:S(2)}, u32[]{:S(2)}) %collective-permute-start.3) | collective-permute-done | bytes 135200 | tf_op jit(solution)/shard_map/ppermute | solution.py:332
  17.1 4.3 %collective-permute-start.6 = (f32[264,128]{1,0:T(8,128)S(1)}, f32[264,128]{1,0:T(8,128)S(1)}, u32[]{:S(2)}, u32[]{:S(2)}) collective-permute-start(f32[264,128]{1,0:T(8,128)S(1)} %get-tuple-element.43), channel_id=1, source_target_pairs={{0,12},{1,13},{2,14},{3,15},{4,8},{5,9},{6,10},{7,11},{8,4},{9,5},... | collective-permute-start | bytes 405512 | tf_op jit(solution)/shard_map/ppermute | solution.py:332
  21.4 1.5 %collective-permute-start.4 = (f32[264,128]{1,0:T(8,128)S(1)}, f32[264,128]{1,0:T(8,128)S(1)}, u32[]{:S(2)}, u32[]{:S(2)}) collective-permute-start(f32[264,128]{1,0:T(8,128)S(1)} %fusion), channel_id=1, source_target_pairs={{0,16},{1,17},{2,18},{3,19},{4,20},{5,21},{6,22},{7,23},{8,24},{9,... | collective-permute-start | bytes 405512 | tf_op jit(solution)/shard_map/ppermute | solution.py:332
  22.9 1.3 %collective-permute-start.7 = (f32[264,128]{1,0:T(8,128)S(1)}, f32[264,128]{1,0:T(8,128)S(1)}, u32[]{:S(2)}, u32[]{:S(2)}) collective-permute-start(f32[264,128]{1,0:T(8,128)S(1)} %get-tuple-element.44), channel_id=1, source_target_pairs={{0,4},{1,5},{2,6},{3,7},{4,0},{5,1},{6,2},{7,3},{8,12},{9,13},{10,... | collective-permute-start | bytes 405512 | tf_op jit(solution)/shard_map/ppermute | solution.py:332
  24.2 1.2 %collective-permute-done.5.refs_3_ = f32[264,128]{1,0:T(8,128)S(1)} collective-permute-done((f32[264,128]{1,0:T(8,128)S(1)}, f32[264,128]{1,0:T(8,128)S(1)}, u32[]{:S(2)}, u32[]{:S(2)}) %collective-permute-start.5) | collective-permute-done | bytes 135200 | tf_op jit(solution)/shard_map/ppermute | solution.py:332
  25.4 2.9 %collective-permute-done.6.refs_4_ = f32[264,128]{1,0:T(8,128)S(1)} collective-permute-done((f32[264,128]{1,0:T(8,128)S(1)}, f32[264,128]{1,0:T(8,128)S(1)}, u32[]{:S(2)}, u32[]{:S(2)}) %collective-permute-start.6) | collective-permute-done | bytes 135200 | tf_op jit(solution)/shard_map/ppermute | solution.py:332
  29.4 1.2 %collective-permute-done.8 = f32[32,128]{1,0:T(8,128)S(1)} collective-permute-done((f32[32,128]{1,0:T(8,128)S(1)}, f32[32,128]{1,0:T(8,128)S(1)}, u32[]{:S(2)}, u32[]{:S(2)}) %collective-permute-start.8) | collective-permute-done | bytes 16416 | tf_op jit(solution)/shard_map/ppermute | solution.py:332
  30.6 1.9 %collective-permute-start.11 = (f32[32,128]{1,0:T(8,128)S(1)}, f32[32,128]{1,0:T(8,128)S(1)}, u32[]{:S(2)}, u32[]{:S(2)}) collective-permute-start(f32[32,128]{1,0:T(8,128)S(1)} %add.27), channel_id=1, source_target_pairs={{0,7},{1,6},{2,5},{3,4},{4,3},{5,2},{6,1},{7,0},{8,15},{9,14},{10,... | collective-permute-start | bytes 49160 | tf_op jit(solution)/shard_map/ppermute | solution.py:332
  32.5 0.8 %collective-permute-start.10 = (f32[32,128]{1,0:T(8,128)S(1)}, f32[32,128]{1,0:T(8,128)S(1)}, u32[]{:S(2)}, u32[]{:S(2)}) collective-permute-start(f32[32,128]{1,0:T(8,128)S(1)} %add.27), channel_id=1, source_target_pairs={{0,5},{1,4},{2,7},{3,6},{4,1},{5,0},{6,3},{7,2},{8,13},{9,12},{10,... | collective-permute-start | bytes 49160 | tf_op jit(solution)/shard_map/ppermute | solution.py:332
  33.5 1.1 %collective-permute-done.11 = f32[32,128]{1,0:T(8,128)S(1)} collective-permute-done((f32[32,128]{1,0:T(8,128)S(1)}, f32[32,128]{1,0:T(8,128)S(1)}, u32[]{:S(2)}, u32[]{:S(2)}) %collective-permute-start.11) | collective-permute-done | bytes 16416 | tf_op jit(solution)/shard_map/ppermute | solution.py:332
  34.6 1.0 %collective-permute-done.10 = f32[32,128]{1,0:T(8,128)S(1)} collective-permute-done((f32[32,128]{1,0:T(8,128)S(1)}, f32[32,128]{1,0:T(8,128)S(1)}, u32[]{:S(2)}, u32[]{:S(2)}) %collective-permute-start.10) | collective-permute-done | bytes 16416 | tf_op jit(solution)/shard_map/ppermute | solution.py:332
  36.4 1.9 %collective-permute-start.12 = (f32[32,128]{1,0:T(8,128)S(1)}, f32[32,128]{1,0:T(8,128)S(1)}, u32[]{:S(2)}, u32[]{:S(2)}) collective-permute-start(f32[32,128]{1,0:T(8,128)S(1)} %add_add_fusion), channel_id=1, source_target_pairs={{0,9},{1,8},{2,11},{3,10},{4,13},{5,12},{6,15},{7,14},{8,1},{9,0},... | collective-permute-start | bytes 49160 | tf_op jit(solution)/shard_map/ppermute | solution.py:332
  38.3 1.4 %collective-permute-done.12 = f32[32,128]{1,0:T(8,128)S(1)} collective-permute-done((f32[32,128]{1,0:T(8,128)S(1)}, f32[32,128]{1,0:T(8,128)S(1)}, u32[]{:S(2)}, u32[]{:S(2)}) %collective-permute-start.12) | collective-permute-done | bytes 16416 | tf_op jit(solution)/shard_map/ppermute | solution.py:332
  39.7 2.0 %collective-permute-start.13 = (f32[32,128]{1,0:T(8,128)S(1)}, f32[32,128]{1,0:T(8,128)S(1)}, u32[]{:S(2)}, u32[]{:S(2)}) collective-permute-start(f32[32,128]{1,0:T(8,128)S(1)} %add.31.gram_ref.refs_0_), channel_id=1, source_target_pairs={{0,17},{1,16},{2,19},{3,18},{4,21},{5,20},{6,23},{7,22},{8,25},{9,... | collective-permute-start | bytes 49160 | tf_op jit(solution)/shard_map/ppermute | solution.py:332
  41.9 1.9 %collective-permute-done.13.refs_1_ = f32[32,128]{1,0:T(8,128)S(1)} collective-permute-done((f32[32,128]{1,0:T(8,128)S(1)}, f32[32,128]{1,0:T(8,128)S(1)}, u32[]{:S(2)}, u32[]{:S(2)}) %collective-permute-start.13) | collective-permute-done | bytes 16416 | tf_op jit(solution)/shard_map/ppermute | solution.py:332
  43.8 2.6 %orthonormal.1 = f32[64,512]{1,0:T(8,128)} custom-call(f32[32,128]{1,0:T(8,128)S(1)} %add.31.gram_ref.refs_0_, f32[32,128]{1,0:T(8,128)S(1)} %collective-permute-done.13.refs_1_, f32[64,128]{1,0:T(8,128)S(1)} %get-tuple-element.46.refs_2_, f32[64,128]{1,0:T(8,128)S(1)} %get-tuple-element.47.refs_3_, f32[64,512]{1,0:T(8,128)S(1)} %get-tuple-element.48.refs_4_), custom_call_target="tpu_custom_call" | custom-call | tf_op jit(solution)/shard_map/orthonormal/pallas_call | solution.py:316
  (20 shorter events, 4.6 us)
Async XLA Ops:
  0.0 1.9 %copy-start = (bf16[64,4096]{1,0:T(8,128)(2,1)S(1)}, bf16[64,4096]{1,0:T(8,128)(2,1)}, u32[]{:S(2)}) copy-start(bf16[64,4096]{1,0:T(8,128)(2,1)} %basis_ref.1) | copy-start | bytes 1572868
  1.9 0.7 %copy-start.1 = (s32[1,32]{1,0:T(1,128)S(1)}, s32[1,32]{1,0:T(1,128)}, u32[]{:S(2)}) copy-start(s32[1,32]{1,0:T(1,128)} %occ_ref.1) | copy-start | bytes 388
  3.5 1.4 %collective-permute-start = (f32[64,128]{1,0:T(8,128)S(1)}, f32[64,128]{1,0:T(8,128)S(1)}, u32[]{:S(2)}, u32[]{:S(2)}) collective-permute-start(f32[64,128]{1,0:T(8,128)S(1)} %get-tuple-element.29), channel_id=1, source_target_pairs={{0,1},{1,0},{2,3},{3,2},{4,5},{5,4},{6,7},{7,6},{8,9},{9,8},{10,11... | collective-permute-start | bytes 98312 | tf_op jit(solution)/shard_map/ppermute | solution.py:332
  4.8 4.2 %collective-permute-start.1 = (f32[64,128]{1,0:T(8,128)S(1)}, f32[64,128]{1,0:T(8,128)S(1)}, u32[]{:S(2)}, u32[]{:S(2)}) collective-permute-start(f32[64,128]{1,0:T(8,128)S(1)} %add.24.refs_0_), channel_id=1, source_target_pairs={{0,3},{1,2},{2,1},{3,0},{4,7},{5,6},{6,5},{7,4},{8,11},{9,10},{10,... | collective-permute-start | bytes 98312 | tf_op jit(solution)/shard_map/ppermute | solution.py:332
  9.5 11.8 %collective-permute-start.2 = (f32[528,128]{1,0:T(8,128)S(1)}, f32[528,128]{1,0:T(8,128)S(1)}, u32[]{:S(2)}, u32[]{:S(2)}) collective-permute-start(f32[528,128]{1,0:T(8,128)S(1)} %get-tuple-element.36), channel_id=1, source_target_pairs={{0,8},{1,9},{2,10},{3,11},{4,12},{5,13},{6,14},{7,15},{8,0},{9,1},... | collective-permute-start | bytes 811016 | tf_op jit(solution)/shard_map/ppermute | solution.py:332
  11.7 5.4 %collective-permute-start.3 = (f32[264,128]{1,0:T(8,128)S(1)}, f32[264,128]{1,0:T(8,128)S(1)}, u32[]{:S(2)}, u32[]{:S(2)}) collective-permute-start(f32[264,128]{1,0:T(8,128)S(1)} %get-tuple-element.37), channel_id=1, source_target_pairs={{0,4},{1,5},{2,6},{3,7},{4,0},{5,1},{6,2},{7,3},{8,12},{9,13},{10,... | collective-permute-start | bytes 405512 | tf_op jit(solution)/shard_map/ppermute | solution.py:332
  13.2 12.2 %collective-permute-start.5 = (f32[264,128]{1,0:T(8,128)S(1)}, f32[264,128]{1,0:T(8,128)S(1)}, u32[]{:S(2)}, u32[]{:S(2)}) collective-permute-start(f32[264,128]{1,0:T(8,128)S(1)} %get-tuple-element.42), channel_id=1, source_target_pairs={{0,28},{1,29},{2,30},{3,31},{4,24},{5,25},{6,26},{7,27},{8,20},{9,... | collective-permute-start | bytes 405512 | tf_op jit(solution)/shard_map/ppermute | solution.py:332
  17.1 11.2 %collective-permute-start.6 = (f32[264,128]{1,0:T(8,128)S(1)}, f32[264,128]{1,0:T(8,128)S(1)}, u32[]{:S(2)}, u32[]{:S(2)}) collective-permute-start(f32[264,128]{1,0:T(8,128)S(1)} %get-tuple-element.43), channel_id=1, source_target_pairs={{0,12},{1,13},{2,14},{3,15},{4,8},{5,9},{6,10},{7,11},{8,4},{9,5},... | collective-permute-start | bytes 405512 | tf_op jit(solution)/shard_map/ppermute | solution.py:332
  21.4 7.4 %collective-permute-start.4 = (f32[264,128]{1,0:T(8,128)S(1)}, f32[264,128]{1,0:T(8,128)S(1)}, u32[]{:S(2)}, u32[]{:S(2)}) collective-permute-start(f32[264,128]{1,0:T(8,128)S(1)} %fusion), channel_id=1, source_target_pairs={{0,16},{1,17},{2,18},{3,19},{4,20},{5,21},{6,22},{7,23},{8,24},{9,... | collective-permute-start | bytes 405512 | tf_op jit(solution)/shard_map/ppermute | solution.py:332
  22.9 6.0 %collective-permute-start.7 = (f32[264,128]{1,0:T(8,128)S(1)}, f32[264,128]{1,0:T(8,128)S(1)}, u32[]{:S(2)}, u32[]{:S(2)}) collective-permute-start(f32[264,128]{1,0:T(8,128)S(1)} %get-tuple-element.44), channel_id=1, source_target_pairs={{0,4},{1,5},{2,6},{3,7},{4,0},{5,1},{6,2},{7,3},{8,12},{9,13},{10,... | collective-permute-start | bytes 405512 | tf_op jit(solution)/shard_map/ppermute | solution.py:332
  29.4 1.2 %collective-permute-start.8 = (f32[32,128]{1,0:T(8,128)S(1)}, f32[32,128]{1,0:T(8,128)S(1)}, u32[]{:S(2)}, u32[]{:S(2)}) collective-permute-start(f32[32,128]{1,0:T(8,128)S(1)} %get-tuple-element.45), channel_id=1, source_target_pairs={{0,1},{1,0},{2,3},{3,2},{4,5},{5,4},{6,7},{7,6},{8,9},{9,8},{10,11... | collective-permute-start | bytes 49160 | tf_op jit(solution)/shard_map/ppermute | solution.py:332
  30.6 4.1 %collective-permute-start.11 = (f32[32,128]{1,0:T(8,128)S(1)}, f32[32,128]{1,0:T(8,128)S(1)}, u32[]{:S(2)}, u32[]{:S(2)}) collective-permute-start(f32[32,128]{1,0:T(8,128)S(1)} %add.27), channel_id=1, source_target_pairs={{0,7},{1,6},{2,5},{3,4},{4,3},{5,2},{6,1},{7,0},{8,15},{9,14},{10,... | collective-permute-start | bytes 49160 | tf_op jit(solution)/shard_map/ppermute | solution.py:332
  32.5 3.2 %collective-permute-start.10 = (f32[32,128]{1,0:T(8,128)S(1)}, f32[32,128]{1,0:T(8,128)S(1)}, u32[]{:S(2)}, u32[]{:S(2)}) collective-permute-start(f32[32,128]{1,0:T(8,128)S(1)} %add.27), channel_id=1, source_target_pairs={{0,5},{1,4},{2,7},{3,6},{4,1},{5,0},{6,3},{7,2},{8,13},{9,12},{10,... | collective-permute-start | bytes 49160 | tf_op jit(solution)/shard_map/ppermute | solution.py:332
  33.2 3.2 %collective-permute-start.9 = (f32[32,128]{1,0:T(8,128)S(1)}, f32[32,128]{1,0:T(8,128)S(1)}, u32[]{:S(2)}, u32[]{:S(2)}) collective-permute-start(f32[32,128]{1,0:T(8,128)S(1)} %add.27), channel_id=1, source_target_pairs={{0,3},{1,2},{2,1},{3,0},{4,7},{5,6},{6,5},{7,4},{8,11},{9,10},{10,... | collective-permute-start | bytes 49160 | tf_op jit(solution)/shard_map/ppermute | solution.py:332
  36.4 3.3 %collective-permute-start.12 = (f32[32,128]{1,0:T(8,128)S(1)}, f32[32,128]{1,0:T(8,128)S(1)}, u32[]{:S(2)}, u32[]{:S(2)}) collective-permute-start(f32[32,128]{1,0:T(8,128)S(1)} %add_add_fusion), channel_id=1, source_target_pairs={{0,9},{1,8},{2,11},{3,10},{4,13},{5,12},{6,15},{7,14},{8,1},{9,0},... | collective-permute-start | bytes 49160 | tf_op jit(solution)/shard_map/ppermute | solution.py:332
  39.7 4.1 %collective-permute-start.13 = (f32[32,128]{1,0:T(8,128)S(1)}, f32[32,128]{1,0:T(8,128)S(1)}, u32[]{:S(2)}, u32[]{:S(2)}) collective-permute-start(f32[32,128]{1,0:T(8,128)S(1)} %add.31.gram_ref.refs_0_), channel_id=1, source_target_pairs={{0,17},{1,16},{2,19},{3,18},{4,21},{5,20},{6,23},{7,22},{8,25},{9,... | collective-permute-start | bytes 49160 | tf_op jit(solution)/shard_map/ppermute | solution.py:332

commit v5 on v4

--- a/solution.py
+++ b/solution.py
@@ -91,9 +91,10 @@
             basis.append(basis_ref[:, pl.ds(at, edge)] * occ.astype(BF16))
         basis = jnp.concatenate(basis, axis=1)
         lanes = pl.ds(begin, width)
-        part = dot(basis, high_ref[:, lanes], NT) + dot(basis, low_ref[:, lanes], NT)
+        part = dot(basis, jnp.concatenate([high_ref[:, lanes], low_ref[:, lanes]], axis=0), NT)
         scores = part if scores is None else scores + part
-    score_ref[...] = scores
+    cells = score_ref.shape[1]
+    score_ref[...] = scores[:, :cells] + scores[:, cells:]
 
 
 def score_part(occupancy, basis, high, low):
@@ -109,13 +110,16 @@
     )(occupancy, basis, high, low)
 
 
+def term_product(left, right, dims):
+    rows = left[0].shape[0]
+    left = jnp.concatenate([jnp.concatenate([term] * len(right), axis=1) for term in left], axis=0)
+    out = dot(left, jnp.concatenate(right, axis=dims[0][1][0]), dims)
+    parts = [out[at:at + rows] for at in range(0, out.shape[0], rows)]
+    return functools.reduce(jnp.add, parts[::-1])
+
+
 def spread_piece(terms, high, low):
-    comps = terms[0].shape[0]
-    on_low = dot(jnp.concatenate(terms[:2], axis=0), low, NN)
-    on_high = dot(jnp.concatenate(terms, axis=0), high, NN)
-    small = on_low[comps:] + on_high[2 * comps:]
-    middle = on_low[:comps] + on_high[comps:2 * comps]
-    return (small + middle) + on_high[:comps]
+    return term_product(terms, [high, low], NN)
 
 
 def spread_kernel(count, picks, me_ref, *refs):
@@ -181,7 +185,8 @@
 
 
 def packed_gram(spread):
-    gram = lax.dot_general(spread, spread, NT, precision=lax.Precision.HIGHEST, preferred_element_type=F32)
+    terms = split_terms(spread, 3)
+    gram = term_product(terms, terms, NT)
     half = spread.shape[0] // 2
     return jnp.concatenate([gram[:half], gram[half:]], axis=1)
 
@@ -307,9 +312,7 @@
     both = gram * times_ref[...] + plus_ref[...]
     groups = eliminate([both[at:at + 8] for at in range(0, comps, 8)], comps)
     inverse = jnp.concatenate(groups, axis=0)[:, :comps] * scale
-    out_ref[...] = lax.dot_general(
-        inverse, spread_ref[...], NN, precision=lax.Precision.HIGHEST, preferred_element_type=F32
-    )
+    out_ref[...] = term_product(split_terms(inverse, 3), split_terms(spread_ref[...], 3), NN)
 
 
 def orthonormal(grams, spread, scale):

time: 46.5 us -> 46.3 us (level)
  transfers between devices with their start and end apart: 14 -> 14, of which waited for: 13 -> 13; matrix products, arithmetic and copies ran while one was open for 0% -> 0% of each run, Pallas kernels for 2% -> 1%
where the time goes in v5:
time: 46.3 us; the launch traced here: 46.2 us
  starting transfers between devices  23.1 us (50%)
  waiting for transfers between devices  15.6 us (34%)
  Pallas kernels  6.73 us (15%)
  local copies, waits for them, and re-layouts  0.64 us (1%)
    ppermute x14, starting transfers between devices, send(): return lax.ppermute(x, ('cells', 'genes'), pairs)  23.1 us
    ppermute x14, waiting for transfers between devices, send(): return lax.ppermute(x, ('cells', 'genes'), pairs)  15.6 us
    pallas_call x1, Pallas kernels, orthonormal(): pl.pallas_call(functools.partial(basis_kernel, scale), out_shape=jax.Shap...  2.6 us
    pallas_call x1, Pallas kernels, log_terms(): pl.pallas_call(functools.partial(log_kernel, width), out_shape=(jax.Shape...  1.92 us
  transfers between devices with their start and end apart: 14, of which 13 were waited for; matrix products, arithmetic and copies ran while one was open for 0% of the time, Pallas kernels for 1%

profile of v5, /device:TPU:0, one launch (start us, length us, event | category | flops | bytes accessed | tf_op | source)
XLA Modules:
  0.0 46.2 jit_solution(11165309820730976974)
XLA Ops:
  0.0 1.9 %log_terms.1 = (bf16[128,4096]{1,0:T(8,128)(2,1)S(1)}, bf16[128,4096]{1,0:T(8,128)(2,1)S(1)}, f32[1,4096]{1,0:T(1,128)S(1)}) custom-call(bf16[128,4096]{1,0:T(8,128)(2,1)} %counts_hbm.1), custom_call_target="tpu_custom_call" | custom-call | flops 10485760 | bytes 4194304 | tf_op jit(solution)/shard_map/log_terms/pallas_call | solution.py:65
  3.9 0.9 %collective-permute-done = f32[64,128]{1,0:T(8,128)S(1)} collective-permute-done((f32[64,128]{1,0:T(8,128)S(1)}, f32[64,128]{1,0:T(8,128)S(1)}, u32[]{:S(2)}, u32[]{:S(2)}) %collective-permute-start) | collective-permute-done | bytes 32800 | tf_op jit(solution)/shard_map/ppermute | solution.py:335
  4.7 2.6 %collective-permute-start.1 = (f32[64,128]{1,0:T(8,128)S(1)}, f32[64,128]{1,0:T(8,128)S(1)}, u32[]{:S(2)}, u32[]{:S(2)}) collective-permute-start(f32[64,128]{1,0:T(8,128)S(1)} %add.24.refs_0_), channel_id=1, source_target_pairs={{0,3},{1,2},{2,1},{3,0},{4,7},{5,6},{6,5},{7,4},{8,11},{9,10},{10,... | collective-permute-start | bytes 98312 | tf_op jit(solution)/shard_map/ppermute | solution.py:335
  7.3 1.6 %collective-permute-done.1.refs_1_ = f32[64,128]{1,0:T(8,128)S(1)} collective-permute-done((f32[64,128]{1,0:T(8,128)S(1)}, f32[64,128]{1,0:T(8,128)S(1)}, u32[]{:S(2)}, u32[]{:S(2)}) %collective-permute-start.1) | collective-permute-done | bytes 32800 | tf_op jit(solution)/shard_map/ppermute | solution.py:335
  9.3 2.1 %collective-permute-start.2 = (f32[528,128]{1,0:T(8,128)S(1)}, f32[528,128]{1,0:T(8,128)S(1)}, u32[]{:S(2)}, u32[]{:S(2)}) collective-permute-start(f32[528,128]{1,0:T(8,128)S(1)} %get-tuple-element.36), channel_id=1, source_target_pairs={{0,8},{1,9},{2,10},{3,11},{4,12},{5,13},{6,14},{7,15},{8,0},{9,1},... | collective-permute-start | bytes 811016 | tf_op jit(solution)/shard_map/ppermute | solution.py:335
  11.5 1.5 %collective-permute-start.3 = (f32[264,128]{1,0:T(8,128)S(1)}, f32[264,128]{1,0:T(8,128)S(1)}, u32[]{:S(2)}, u32[]{:S(2)}) collective-permute-start(f32[264,128]{1,0:T(8,128)S(1)} %get-tuple-element.37), channel_id=1, source_target_pairs={{0,4},{1,5},{2,6},{3,7},{4,0},{5,1},{6,2},{7,3},{8,12},{9,13},{10,... | collective-permute-start | bytes 405512 | tf_op jit(solution)/shard_map/ppermute | solution.py:335
  13.0 2.4 %collective-permute-start.5 = (f32[264,128]{1,0:T(8,128)S(1)}, f32[264,128]{1,0:T(8,128)S(1)}, u32[]{:S(2)}, u32[]{:S(2)}) collective-permute-start(f32[264,128]{1,0:T(8,128)S(1)} %get-tuple-element.42), channel_id=1, source_target_pairs={{0,28},{1,29},{2,30},{3,31},{4,24},{5,25},{6,26},{7,27},{8,20},{9,... | collective-permute-start | bytes 405512 | tf_op jit(solution)/shard_map/ppermute | solution.py:335
  15.8 1.1 %collective-permute-done.3 = f32[264,128]{1,0:T(8,128)S(1)} collective-permute-done((f32[264,128]{1,0:T(8,128)S(1)}, f32[264,128]{1,0:T(8,128)S(1)}, u32[]{:S(2)}, u32[]{:S(2)}) %collective-permute-start.3) | collective-permute-done | bytes 135200 | tf_op jit(solution)/shard_map/ppermute | solution.py:335
  16.8 4.3 %collective-permute-start.6 = (f32[264,128]{1,0:T(8,128)S(1)}, f32[264,128]{1,0:T(8,128)S(1)}, u32[]{:S(2)}, u32[]{:S(2)}) collective-permute-start(f32[264,128]{1,0:T(8,128)S(1)} %get-tuple-element.43), channel_id=1, source_target_pairs={{0,12},{1,13},{2,14},{3,15},{4,8},{5,9},{6,10},{7,11},{8,4},{9,5},... | collective-permute-start | bytes 405512 | tf_op jit(solution)/shard_map/ppermute | solution.py:335
  21.2 1.4 %collective-permute-start.4 = (f32[264,128]{1,0:T(8,128)S(1)}, f32[264,128]{1,0:T(8,128)S(1)}, u32[]{:S(2)}, u32[]{:S(2)}) collective-permute-start(f32[264,128]{1,0:T(8,128)S(1)} %fusion), channel_id=1, source_target_pairs={{0,16},{1,17},{2,18},{3,19},{4,20},{5,21},{6,22},{7,23},{8,24},{9,... | collective-permute-start | bytes 405512 | tf_op jit(solution)/shard_map/ppermute | solution.py:335
  22.6 1.3 %collective-permute-start.7 = (f32[264,128]{1,0:T(8,128)S(1)}, f32[264,128]{1,0:T(8,128)S(1)}, u32[]{:S(2)}, u32[]{:S(2)}) collective-permute-start(f32[264,128]{1,0:T(8,128)S(1)} %get-tuple-element.44), channel_id=1, source_target_pairs={{0,4},{1,5},{2,6},{3,7},{4,0},{5,1},{6,2},{7,3},{8,12},{9,13},{10,... | collective-permute-start | bytes 405512 | tf_op jit(solution)/shard_map/ppermute | solution.py:335
  23.9 1.2 %collective-permute-done.5.refs_3_ = f32[264,128]{1,0:T(8,128)S(1)} collective-permute-done((f32[264,128]{1,0:T(8,128)S(1)}, f32[264,128]{1,0:T(8,128)S(1)}, u32[]{:S(2)}, u32[]{:S(2)}) %collective-permute-start.5) | collective-permute-done | bytes 135200 | tf_op jit(solution)/shard_map/ppermute | solution.py:335
  25.2 2.9 %collective-permute-done.6.refs_4_ = f32[264,128]{1,0:T(8,128)S(1)} collective-permute-done((f32[264,128]{1,0:T(8,128)S(1)}, f32[264,128]{1,0:T(8,128)S(1)}, u32[]{:S(2)}, u32[]{:S(2)}) %collective-permute-start.6) | collective-permute-done | bytes 135200 | tf_op jit(solution)/shard_map/ppermute | solution.py:335
  29.2 1.2 %collective-permute-done.8 = f32[32,128]{1,0:T(8,128)S(1)} collective-permute-done((f32[32,128]{1,0:T(8,128)S(1)}, f32[32,128]{1,0:T(8,128)S(1)}, u32[]{:S(2)}, u32[]{:S(2)}) %collective-permute-start.8) | collective-permute-done | bytes 16416 | tf_op jit(solution)/shard_map/ppermute | solution.py:335
  30.4 1.9 %collective-permute-start.11 = (f32[32,128]{1,0:T(8,128)S(1)}, f32[32,128]{1,0:T(8,128)S(1)}, u32[]{:S(2)}, u32[]{:S(2)}) collective-permute-start(f32[32,128]{1,0:T(8,128)S(1)} %add.27), channel_id=1, source_target_pairs={{0,7},{1,6},{2,5},{3,4},{4,3},{5,2},{6,1},{7,0},{8,15},{9,14},{10,... | collective-permute-start | bytes 49160 | tf_op jit(solution)/shard_map/ppermute | solution.py:335
  32.3 0.8 %collective-permute-start.10 = (f32[32,128]{1,0:T(8,128)S(1)}, f32[32,128]{1,0:T(8,128)S(1)}, u32[]{:S(2)}, u32[]{:S(2)}) collective-permute-start(f32[32,128]{1,0:T(8,128)S(1)} %add.27), channel_id=1, source_target_pairs={{0,5},{1,4},{2,7},{3,6},{4,1},{5,0},{6,3},{7,2},{8,13},{9,12},{10,... | collective-permute-start | bytes 49160 | tf_op jit(solution)/shard_map/ppermute | solution.py:335
  33.4 1.1 %collective-permute-done.11 = f32[32,128]{1,0:T(8,128)S(1)} collective-permute-done((f32[32,128]{1,0:T(8,128)S(1)}, f32[32,128]{1,0:T(8,128)S(1)}, u32[]{:S(2)}, u32[]{:S(2)}) %collective-permute-start.11) | collective-permute-done | bytes 16416 | tf_op jit(solution)/shard_map/ppermute | solution.py:335
  34.4 1.0 %collective-permute-done.10 = f32[32,128]{1,0:T(8,128)S(1)} collective-permute-done((f32[32,128]{1,0:T(8,128)S(1)}, f32[32,128]{1,0:T(8,128)S(1)}, u32[]{:S(2)}, u32[]{:S(2)}) %collective-permute-start.10) | collective-permute-done | bytes 16416 | tf_op jit(solution)/shard_map/ppermute | solution.py:335
  35.4 0.8 %collective-permute-done.9 = f32[32,128]{1,0:T(8,128)S(1)} collective-permute-done((f32[32,128]{1,0:T(8,128)S(1)}, f32[32,128]{1,0:T(8,128)S(1)}, u32[]{:S(2)}, u32[]{:S(2)}) %collective-permute-start.9) | collective-permute-done | bytes 16416 | tf_op jit(solution)/shard_map/ppermute | solution.py:335
  36.2 1.8 %collective-permute-start.12 = (f32[32,128]{1,0:T(8,128)S(1)}, f32[32,128]{1,0:T(8,128)S(1)}, u32[]{:S(2)}, u32[]{:S(2)}) collective-permute-start(f32[32,128]{1,0:T(8,128)S(1)} %add_add_fusion), channel_id=1, source_target_pairs={{0,9},{1,8},{2,11},{3,10},{4,13},{5,12},{6,15},{7,14},{8,1},{9,0},... | collective-permute-start | bytes 49160 | tf_op jit(solution)/shard_map/ppermute | solution.py:335
  38.1 1.4 %collective-permute-done.12 = f32[32,128]{1,0:T(8,128)S(1)} collective-permute-done((f32[32,128]{1,0:T(8,128)S(1)}, f32[32,128]{1,0:T(8,128)S(1)}, u32[]{:S(2)}, u32[]{:S(2)}) %collective-permute-start.12) | collective-permute-done | bytes 16416 | tf_op jit(solution)/shard_map/ppermute | solution.py:335
  39.5 2.0 %collective-permute-start.13 = (f32[32,128]{1,0:T(8,128)S(1)}, f32[32,128]{1,0:T(8,128)S(1)}, u32[]{:S(2)}, u32[]{:S(2)}) collective-permute-start(f32[32,128]{1,0:T(8,128)S(1)} %add.31.gram_ref.refs_0_), channel_id=1, source_target_pairs={{0,17},{1,16},{2,19},{3,18},{4,21},{5,20},{6,23},{7,22},{8,25},{9,... | collective-permute-start | bytes 49160 | tf_op jit(solution)/shard_map/ppermute | solution.py:335
  41.7 1.9 %collective-permute-done.13.refs_1_ = f32[32,128]{1,0:T(8,128)S(1)} collective-permute-done((f32[32,128]{1,0:T(8,128)S(1)}, f32[32,128]{1,0:T(8,128)S(1)}, u32[]{:S(2)}, u32[]{:S(2)}) %collective-permute-start.13) | collective-permute-done | bytes 16416 | tf_op jit(solution)/shard_map/ppermute | solution.py:335
  43.6 2.6 %orthonormal.1 = f32[64,512]{1,0:T(8,128)} custom-call(f32[32,128]{1,0:T(8,128)S(1)} %add.31.gram_ref.refs_0_, f32[32,128]{1,0:T(8,128)S(1)} %collective-permute-done.13.refs_1_, f32[64,128]{1,0:T(8,128)S(1)} %get-tuple-element.46.refs_2_, f32[64,128]{1,0:T(8,128)S(1)} %get-tuple-element.47.refs_3_, f32[64,512]{1,0:T(8,128)S(1)} %get-tuple-element.48.refs_4_), custom_call_target="tpu_custom_call" | custom-call | tf_op jit(solution)/shard_map/orthonormal/pallas_call | solution.py:319
  (20 shorter events, 4.4 us)
Async XLA Ops:
  0.0 1.9 %copy-start = (bf16[64,4096]{1,0:T(8,128)(2,1)S(1)}, bf16[64,4096]{1,0:T(8,128)(2,1)}, u32[]{:S(2)}) copy-start(bf16[64,4096]{1,0:T(8,128)(2,1)} %basis_ref.1) | copy-start | bytes 1572868
  1.9 0.7 %copy-start.1 = (s32[1,32]{1,0:T(1,128)S(1)}, s32[1,32]{1,0:T(1,128)}, u32[]{:S(2)}) copy-start(s32[1,32]{1,0:T(1,128)} %occ_ref.1) | copy-start | bytes 388
  3.4 1.4 %collective-permute-start = (f32[64,128]{1,0:T(8,128)S(1)}, f32[64,128]{1,0:T(8,128)S(1)}, u32[]{:S(2)}, u32[]{:S(2)}) collective-permute-start(f32[64,128]{1,0:T(8,128)S(1)} %get-tuple-element.29), channel_id=1, source_target_pairs={{0,1},{1,0},{2,3},{3,2},{4,5},{5,4},{6,7},{7,6},{8,9},{9,8},{10,11... | collective-permute-start | bytes 98312 | tf_op jit(solution)/shard_map/ppermute | solution.py:335
  4.7 4.2 %collective-permute-start.1 = (f32[64,128]{1,0:T(8,128)S(1)}, f32[64,128]{1,0:T(8,128)S(1)}, u32[]{:S(2)}, u32[]{:S(2)}) collective-permute-start(f32[64,128]{1,0:T(8,128)S(1)} %add.24.refs_0_), channel_id=1, source_target_pairs={{0,3},{1,2},{2,1},{3,0},{4,7},{5,6},{6,5},{7,4},{8,11},{9,10},{10,... | collective-permute-start | bytes 98312 | tf_op jit(solution)/shard_map/ppermute | solution.py:335
  9.3 11.8 %collective-permute-start.2 = (f32[528,128]{1,0:T(8,128)S(1)}, f32[528,128]{1,0:T(8,128)S(1)}, u32[]{:S(2)}, u32[]{:S(2)}) collective-permute-start(f32[528,128]{1,0:T(8,128)S(1)} %get-tuple-element.36), channel_id=1, source_target_pairs={{0,8},{1,9},{2,10},{3,11},{4,12},{5,13},{6,14},{7,15},{8,0},{9,1},... | collective-permute-start | bytes 811016 | tf_op jit(solution)/shard_map/ppermute | solution.py:335
  11.5 5.4 %collective-permute-start.3 = (f32[264,128]{1,0:T(8,128)S(1)}, f32[264,128]{1,0:T(8,128)S(1)}, u32[]{:S(2)}, u32[]{:S(2)}) collective-permute-start(f32[264,128]{1,0:T(8,128)S(1)} %get-tuple-element.37), channel_id=1, source_target_pairs={{0,4},{1,5},{2,6},{3,7},{4,0},{5,1},{6,2},{7,3},{8,12},{9,13},{10,... | collective-permute-start | bytes 405512 | tf_op jit(solution)/shard_map/ppermute | solution.py:335
  13.0 12.2 %collective-permute-start.5 = (f32[264,128]{1,0:T(8,128)S(1)}, f32[264,128]{1,0:T(8,128)S(1)}, u32[]{:S(2)}, u32[]{:S(2)}) collective-permute-start(f32[264,128]{1,0:T(8,128)S(1)} %get-tuple-element.42), channel_id=1, source_target_pairs={{0,28},{1,29},{2,30},{3,31},{4,24},{5,25},{6,26},{7,27},{8,20},{9,... | collective-permute-start | bytes 405512 | tf_op jit(solution)/shard_map/ppermute | solution.py:335
  16.8 11.2 %collective-permute-start.6 = (f32[264,128]{1,0:T(8,128)S(1)}, f32[264,128]{1,0:T(8,128)S(1)}, u32[]{:S(2)}, u32[]{:S(2)}) collective-permute-start(f32[264,128]{1,0:T(8,128)S(1)} %get-tuple-element.43), channel_id=1, source_target_pairs={{0,12},{1,13},{2,14},{3,15},{4,8},{5,9},{6,10},{7,11},{8,4},{9,5},... | collective-permute-start | bytes 405512 | tf_op jit(solution)/shard_map/ppermute | solution.py:335
  21.2 7.4 %collective-permute-start.4 = (f32[264,128]{1,0:T(8,128)S(1)}, f32[264,128]{1,0:T(8,128)S(1)}, u32[]{:S(2)}, u32[]{:S(2)}) collective-permute-start(f32[264,128]{1,0:T(8,128)S(1)} %fusion), channel_id=1, source_target_pairs={{0,16},{1,17},{2,18},{3,19},{4,20},{5,21},{6,22},{7,23},{8,24},{9,... | collective-permute-start | bytes 405512 | tf_op jit(solution)/shard_map/ppermute | solution.py:335
  22.6 6.1 %collective-permute-start.7 = (f32[264,128]{1,0:T(8,128)S(1)}, f32[264,128]{1,0:T(8,128)S(1)}, u32[]{:S(2)}, u32[]{:S(2)}) collective-permute-start(f32[264,128]{1,0:T(8,128)S(1)} %get-tuple-element.44), channel_id=1, source_target_pairs={{0,4},{1,5},{2,6},{3,7},{4,0},{5,1},{6,2},{7,3},{8,12},{9,13},{10,... | collective-permute-start | bytes 405512 | tf_op jit(solution)/shard_map/ppermute | solution.py:335
  29.2 1.2 %collective-permute-start.8 = (f32[32,128]{1,0:T(8,128)S(1)}, f32[32,128]{1,0:T(8,128)S(1)}, u32[]{:S(2)}, u32[]{:S(2)}) collective-permute-start(f32[32,128]{1,0:T(8,128)S(1)} %get-tuple-element.45), channel_id=1, source_target_pairs={{0,1},{1,0},{2,3},{3,2},{4,5},{5,4},{6,7},{7,6},{8,9},{9,8},{10,11... | collective-permute-start | bytes 49160 | tf_op jit(solution)/shard_map/ppermute | solution.py:335
  30.4 4.1 %collective-permute-start.11 = (f32[32,128]{1,0:T(8,128)S(1)}, f32[32,128]{1,0:T(8,128)S(1)}, u32[]{:S(2)}, u32[]{:S(2)}) collective-permute-start(f32[32,128]{1,0:T(8,128)S(1)} %add.27), channel_id=1, source_target_pairs={{0,7},{1,6},{2,5},{3,4},{4,3},{5,2},{6,1},{7,0},{8,15},{9,14},{10,... | collective-permute-start | bytes 49160 | tf_op jit(solution)/shard_map/ppermute | solution.py:335
  32.3 3.2 %collective-permute-start.10 = (f32[32,128]{1,0:T(8,128)S(1)}, f32[32,128]{1,0:T(8,128)S(1)}, u32[]{:S(2)}, u32[]{:S(2)}) collective-permute-start(f32[32,128]{1,0:T(8,128)S(1)} %add.27), channel_id=1, source_target_pairs={{0,5},{1,4},{2,7},{3,6},{4,1},{5,0},{6,3},{7,2},{8,13},{9,12},{10,... | collective-permute-start | bytes 49160 | tf_op jit(solution)/shard_map/ppermute | solution.py:335
  33.1 3.2 %collective-permute-start.9 = (f32[32,128]{1,0:T(8,128)S(1)}, f32[32,128]{1,0:T(8,128)S(1)}, u32[]{:S(2)}, u32[]{:S(2)}) collective-permute-start(f32[32,128]{1,0:T(8,128)S(1)} %add.27), channel_id=1, source_target_pairs={{0,3},{1,2},{2,1},{3,0},{4,7},{5,6},{6,5},{7,4},{8,11},{9,10},{10,... | collective-permute-start | bytes 49160 | tf_op jit(solution)/shard_map/ppermute | solution.py:335
  36.2 3.3 %collective-permute-start.12 = (f32[32,128]{1,0:T(8,128)S(1)}, f32[32,128]{1,0:T(8,128)S(1)}, u32[]{:S(2)}, u32[]{:S(2)}) collective-permute-start(f32[32,128]{1,0:T(8,128)S(1)} %add_add_fusion), channel_id=1, source_target_pairs={{0,9},{1,8},{2,11},{3,10},{4,13},{5,12},{6,15},{7,14},{8,1},{9,0},... | collective-permute-start | bytes 49160 | tf_op jit(solution)/shard_map/ppermute | solution.py:335
  39.5 4.1 %collective-permute-start.13 = (f32[32,128]{1,0:T(8,128)S(1)}, f32[32,128]{1,0:T(8,128)S(1)}, u32[]{:S(2)}, u32[]{:S(2)}) collective-permute-start(f32[32,128]{1,0:T(8,128)S(1)} %add.31.gram_ref.refs_0_), channel_id=1, source_target_pairs={{0,17},{1,16},{2,19},{3,18},{4,21},{5,20},{6,23},{7,22},{8,25},{9,... | collective-permute-start | bytes 49160 | tf_op jit(solution)/shard_map/ppermute | solution.py:335

commit v6 on v5

--- a/solution.py
+++ b/solution.py
@@ -343,11 +343,9 @@
 def all_terms(x):
     x = x + send(x, 0, 1)
     across = [send(x, c, g) for c, g in ((1, 3), (1, 1), (0, 3))]
-    terms = [x + across[2], across[1] + across[0]]
-    for at in range(1, lax.axis_size("cells").bit_length() - 1):
-        x = tree_sum(terms)
-        terms = [x, send(x, 1 << at, 1)]
-    return terms
+    x = (x + across[2]) + (across[1] + across[0])
+    across = [send(x, c, 1) for c in (6, 4, 2)]
+    return [x, across[2], across[1], across[0]]
 
 
 def scattered_spread(scores, high, low, sums, occ, cell_total):

time: 46.3 us -> 46.4 us (level)
    ppermute x14 -> x15, starting transfers between devices: 23.1 us -> 23.2 us  [send(): return lax.ppermute(x, ('cells', 'genes'), pairs)]
    ppermute x14 -> x15, waiting for transfers between devices: 15.6 us -> 15.5 us  [send(): return lax.ppermute(x, ('cells', 'genes'), pairs)]
  transfers between devices with their start and end apart: 14 -> 15, of which waited for: 13 -> 13; matrix products, arithmetic and copies ran while one was open for 0% -> 0% of each run, Pallas kernels for 1% -> 1%
where the time goes in v6:
time: 46.4 us; the launch traced here: 46.2 us
  starting transfers between devices  23.2 us (50%)
  waiting for transfers between devices  15.5 us (33%)
  Pallas kernels  6.73 us (15%)
  local copies, waits for them, and re-layouts  0.64 us (1%)
    ppermute x15, starting transfers between devices, send(): return lax.ppermute(x, ('cells', 'genes'), pairs)  23.2 us
    ppermute x15, waiting for transfers between devices, send(): return lax.ppermute(x, ('cells', 'genes'), pairs)  15.5 us
    pallas_call x1, Pallas kernels, orthonormal(): pl.pallas_call(functools.partial(basis_kernel, scale), out_shape=jax.Shap...  2.6 us
    pallas_call x1, Pallas kernels, log_terms(): pl.pallas_call(functools.partial(log_kernel, width), out_shape=(jax.Shape...  1.92 us
  transfers between devices with their start and end apart: 15, of which 13 were waited for; matrix products, arithmetic and copies ran while one was open for 0% of the time, Pallas kernels for 1%

profile of v6, /device:TPU:0, one launch (start us, length us, event | category | flops | bytes accessed | tf_op | source)
XLA Modules:
  0.0 46.2 jit_solution(6028008652896254258)
XLA Ops:
  0.0 1.9 %log_terms.1 = (bf16[128,4096]{1,0:T(8,128)(2,1)S(1)}, bf16[128,4096]{1,0:T(8,128)(2,1)S(1)}, f32[1,4096]{1,0:T(1,128)S(1)}) custom-call(bf16[128,4096]{1,0:T(8,128)(2,1)} %counts_hbm.1), custom_call_target="tpu_custom_call" | custom-call | flops 10485760 | bytes 4194304 | tf_op jit(solution)/shard_map/log_terms/pallas_call | solution.py:65
  2.6 0.8 %scores.1 = (f32[64,128]{1,0:T(8,128)S(1)}, f32[1,4096]{1,0:T(1,128)S(1)}) custom-call(s32[1,32]{1,0:T(1,128)S(1)} %copy-done.1, bf16[64,4096]{1,0:T(8,128)(2,1)S(1)} %copy-done, bf16[128,4096]{1,0:T(8,128)(2,1)S(1)} %get-tuple-element.27.high_ref.refs_2_, bf16[128,4096]{1,0:T(8,128)(2,1)S(1)} %get-tuple-element.28.low_ref.refs_3_), custom_call_target="tpu_custom_call" | custom-call | tf_op jit(solution)/shard_map/scores/pallas_call | solution.py:103
  3.9 0.9 %collective-permute-done = f32[64,128]{1,0:T(8,128)S(1)} collective-permute-done((f32[64,128]{1,0:T(8,128)S(1)}, f32[64,128]{1,0:T(8,128)S(1)}, u32[]{:S(2)}, u32[]{:S(2)}) %collective-permute-start) | collective-permute-done | bytes 32800 | tf_op jit(solution)/shard_map/ppermute | solution.py:335
  4.7 2.6 %collective-permute-start.1 = (f32[64,128]{1,0:T(8,128)S(1)}, f32[64,128]{1,0:T(8,128)S(1)}, u32[]{:S(2)}, u32[]{:S(2)}) collective-permute-start(f32[64,128]{1,0:T(8,128)S(1)} %add.21.refs_0_), channel_id=1, source_target_pairs={{0,3},{1,2},{2,1},{3,0},{4,7},{5,6},{6,5},{7,4},{8,11},{9,10},{10,... | collective-permute-start | bytes 98312 | tf_op jit(solution)/shard_map/ppermute | solution.py:335
  7.3 1.6 %collective-permute-done.1.refs_1_ = f32[64,128]{1,0:T(8,128)S(1)} collective-permute-done((f32[64,128]{1,0:T(8,128)S(1)}, f32[64,128]{1,0:T(8,128)S(1)}, u32[]{:S(2)}, u32[]{:S(2)}) %collective-permute-start.1) | collective-permute-done | bytes 32800 | tf_op jit(solution)/shard_map/ppermute | solution.py:335
  9.3 2.1 %collective-permute-start.2 = (f32[528,128]{1,0:T(8,128)S(1)}, f32[528,128]{1,0:T(8,128)S(1)}, u32[]{:S(2)}, u32[]{:S(2)}) collective-permute-start(f32[528,128]{1,0:T(8,128)S(1)} %get-tuple-element.36), channel_id=1, source_target_pairs={{0,8},{1,9},{2,10},{3,11},{4,12},{5,13},{6,14},{7,15},{8,0},{9,1},... | collective-permute-start | bytes 811016 | tf_op jit(solution)/shard_map/ppermute | solution.py:335
  11.5 1.5 %collective-permute-start.3 = (f32[264,128]{1,0:T(8,128)S(1)}, f32[264,128]{1,0:T(8,128)S(1)}, u32[]{:S(2)}, u32[]{:S(2)}) collective-permute-start(f32[264,128]{1,0:T(8,128)S(1)} %get-tuple-element.37), channel_id=1, source_target_pairs={{0,4},{1,5},{2,6},{3,7},{4,0},{5,1},{6,2},{7,3},{8,12},{9,13},{10,... | collective-permute-start | bytes 405512 | tf_op jit(solution)/shard_map/ppermute | solution.py:335
  13.0 2.4 %collective-permute-start.5 = (f32[264,128]{1,0:T(8,128)S(1)}, f32[264,128]{1,0:T(8,128)S(1)}, u32[]{:S(2)}, u32[]{:S(2)}) collective-permute-start(f32[264,128]{1,0:T(8,128)S(1)} %get-tuple-element.42), channel_id=1, source_target_pairs={{0,28},{1,29},{2,30},{3,31},{4,24},{5,25},{6,26},{7,27},{8,20},{9,... | collective-permute-start | bytes 405512 | tf_op jit(solution)/shard_map/ppermute | solution.py:335
  15.8 1.1 %collective-permute-done.3 = f32[264,128]{1,0:T(8,128)S(1)} collective-permute-done((f32[264,128]{1,0:T(8,128)S(1)}, f32[264,128]{1,0:T(8,128)S(1)}, u32[]{:S(2)}, u32[]{:S(2)}) %collective-permute-start.3) | collective-permute-done | bytes 135200 | tf_op jit(solution)/shard_map/ppermute | solution.py:335
  16.8 4.3 %collective-permute-start.6 = (f32[264,128]{1,0:T(8,128)S(1)}, f32[264,128]{1,0:T(8,128)S(1)}, u32[]{:S(2)}, u32[]{:S(2)}) collective-permute-start(f32[264,128]{1,0:T(8,128)S(1)} %get-tuple-element.43), channel_id=1, source_target_pairs={{0,12},{1,13},{2,14},{3,15},{4,8},{5,9},{6,10},{7,11},{8,4},{9,5},... | collective-permute-start | bytes 405512 | tf_op jit(solution)/shard_map/ppermute | solution.py:335
  21.2 1.4 %collective-permute-start.4 = (f32[264,128]{1,0:T(8,128)S(1)}, f32[264,128]{1,0:T(8,128)S(1)}, u32[]{:S(2)}, u32[]{:S(2)}) collective-permute-start(f32[264,128]{1,0:T(8,128)S(1)} %fusion), channel_id=1, source_target_pairs={{0,16},{1,17},{2,18},{3,19},{4,20},{5,21},{6,22},{7,23},{8,24},{9,... | collective-permute-start | bytes 405512 | tf_op jit(solution)/shard_map/ppermute | solution.py:335
  22.6 1.3 %collective-permute-start.7 = (f32[264,128]{1,0:T(8,128)S(1)}, f32[264,128]{1,0:T(8,128)S(1)}, u32[]{:S(2)}, u32[]{:S(2)}) collective-permute-start(f32[264,128]{1,0:T(8,128)S(1)} %get-tuple-element.44), channel_id=1, source_target_pairs={{0,4},{1,5},{2,6},{3,7},{4,0},{5,1},{6,2},{7,3},{8,12},{9,13},{10,... | collective-permute-start | bytes 405512 | tf_op jit(solution)/shard_map/ppermute | solution.py:335
  23.9 1.2 %collective-permute-done.5.refs_3_ = f32[264,128]{1,0:T(8,128)S(1)} collective-permute-done((f32[264,128]{1,0:T(8,128)S(1)}, f32[264,128]{1,0:T(8,128)S(1)}, u32[]{:S(2)}, u32[]{:S(2)}) %collective-permute-start.5) | collective-permute-done | bytes 135200 | tf_op jit(solution)/shard_map/ppermute | solution.py:335
  25.2 2.9 %collective-permute-done.6.refs_4_ = f32[264,128]{1,0:T(8,128)S(1)} collective-permute-done((f32[264,128]{1,0:T(8,128)S(1)}, f32[264,128]{1,0:T(8,128)S(1)}, u32[]{:S(2)}, u32[]{:S(2)}) %collective-permute-start.6) | collective-permute-done | bytes 135200 | tf_op jit(solution)/shard_map/ppermute | solution.py:335
  29.2 1.2 %collective-permute-done.8 = f32[32,128]{1,0:T(8,128)S(1)} collective-permute-done((f32[32,128]{1,0:T(8,128)S(1)}, f32[32,128]{1,0:T(8,128)S(1)}, u32[]{:S(2)}, u32[]{:S(2)}) %collective-permute-start.8) | collective-permute-done | bytes 16416 | tf_op jit(solution)/shard_map/ppermute | solution.py:335
  30.4 1.9 %collective-permute-start.11 = (f32[32,128]{1,0:T(8,128)S(1)}, f32[32,128]{1,0:T(8,128)S(1)}, u32[]{:S(2)}, u32[]{:S(2)}) collective-permute-start(f32[32,128]{1,0:T(8,128)S(1)} %add.24), channel_id=1, source_target_pairs={{0,7},{1,6},{2,5},{3,4},{4,3},{5,2},{6,1},{7,0},{8,15},{9,14},{10,... | collective-permute-start | bytes 49160 | tf_op jit(solution)/shard_map/ppermute | solution.py:335
  32.3 0.8 %collective-permute-start.10 = (f32[32,128]{1,0:T(8,128)S(1)}, f32[32,128]{1,0:T(8,128)S(1)}, u32[]{:S(2)}, u32[]{:S(2)}) collective-permute-start(f32[32,128]{1,0:T(8,128)S(1)} %add.24), channel_id=1, source_target_pairs={{0,5},{1,4},{2,7},{3,6},{4,1},{5,0},{6,3},{7,2},{8,13},{9,12},{10,... | collective-permute-start | bytes 49160 | tf_op jit(solution)/shard_map/ppermute | solution.py:335
  33.4 1.1 %collective-permute-done.11 = f32[32,128]{1,0:T(8,128)S(1)} collective-permute-done((f32[32,128]{1,0:T(8,128)S(1)}, f32[32,128]{1,0:T(8,128)S(1)}, u32[]{:S(2)}, u32[]{:S(2)}) %collective-permute-start.11) | collective-permute-done | bytes 16416 | tf_op jit(solution)/shard_map/ppermute | solution.py:335
  34.4 1.0 %collective-permute-done.10 = f32[32,128]{1,0:T(8,128)S(1)} collective-permute-done((f32[32,128]{1,0:T(8,128)S(1)}, f32[32,128]{1,0:T(8,128)S(1)}, u32[]{:S(2)}, u32[]{:S(2)}) %collective-permute-start.10) | collective-permute-done | bytes 16416 | tf_op jit(solution)/shard_map/ppermute | solution.py:335
  35.4 0.8 %collective-permute-done.9 = f32[32,128]{1,0:T(8,128)S(1)} collective-permute-done((f32[32,128]{1,0:T(8,128)S(1)}, f32[32,128]{1,0:T(8,128)S(1)}, u32[]{:S(2)}, u32[]{:S(2)}) %collective-permute-start.9) | collective-permute-done | bytes 16416 | tf_op jit(solution)/shard_map/ppermute | solution.py:335
  36.2 3.3 %collective-permute-start.14 = (f32[32,128]{1,0:T(8,128)S(1)}, f32[32,128]{1,0:T(8,128)S(1)}, u32[]{:S(2)}, u32[]{:S(2)}) collective-permute-start(f32[32,128]{1,0:T(8,128)S(1)} %add_add_fusion.gram_ref.refs_0_), channel_id=1, source_target_pairs={{0,25},{1,24},{2,27},{3,26},{4,29},{5,28},{6,31},{7,30},{8,17},{9,... | collective-permute-start | bytes 49160 | tf_op jit(solution)/shard_map/ppermute | solution.py:335
  40.4 1.0 %collective-permute-done.14.refs_3_ = f32[32,128]{1,0:T(8,128)S(1)} collective-permute-done((f32[32,128]{1,0:T(8,128)S(1)}, f32[32,128]{1,0:T(8,128)S(1)}, u32[]{:S(2)}, u32[]{:S(2)}) %collective-permute-start.14) | collective-permute-done | bytes 16416 | tf_op jit(solution)/shard_map/ppermute | solution.py:335
  41.4 2.2 %collective-permute-done.13.refs_2_ = f32[32,128]{1,0:T(8,128)S(1)} collective-permute-done((f32[32,128]{1,0:T(8,128)S(1)}, f32[32,128]{1,0:T(8,128)S(1)}, u32[]{:S(2)}, u32[]{:S(2)}) %collective-permute-start.13) | collective-permute-done | bytes 16416 | tf_op jit(solution)/shard_map/ppermute | solution.py:335
  43.6 2.6 %orthonormal.1 = f32[64,512]{1,0:T(8,128)} custom-call(f32[32,128]{1,0:T(8,128)S(1)} %add_add_fusion.gram_ref.refs_0_, f32[32,128]{1,0:T(8,128)S(1)} %collective-permute-done.12.refs_1_, f32[32,128]{1,0:T(8,128)S(1)} %collective-permute-done.13.refs_2_, f32[32,128]{1,0:T(8,128)S(1)} %collective-permute-done.14.refs_3_, ...), custom_call_target="tpu_custom_call" | custom-call | tf_op jit(solution)/shard_map/orthonormal/pallas_call | solution.py:319
  (21 shorter events, 4.3 us)
Async XLA Ops:
  0.0 1.9 %copy-start = (bf16[64,4096]{1,0:T(8,128)(2,1)S(1)}, bf16[64,4096]{1,0:T(8,128)(2,1)}, u32[]{:S(2)}) copy-start(bf16[64,4096]{1,0:T(8,128)(2,1)} %basis_ref.1) | copy-start | bytes 1572868
  1.9 0.7 %copy-start.1 = (s32[1,32]{1,0:T(1,128)S(1)}, s32[1,32]{1,0:T(1,128)}, u32[]{:S(2)}) copy-start(s32[1,32]{1,0:T(1,128)} %occ_ref.1) | copy-start | bytes 388
  3.4 1.4 %collective-permute-start = (f32[64,128]{1,0:T(8,128)S(1)}, f32[64,128]{1,0:T(8,128)S(1)}, u32[]{:S(2)}, u32[]{:S(2)}) collective-permute-start(f32[64,128]{1,0:T(8,128)S(1)} %get-tuple-element.29), channel_id=1, source_target_pairs={{0,1},{1,0},{2,3},{3,2},{4,5},{5,4},{6,7},{7,6},{8,9},{9,8},{10,11... | collective-permute-start | bytes 98312 | tf_op jit(solution)/shard_map/ppermute | solution.py:335
  4.7 4.2 %collective-permute-start.1 = (f32[64,128]{1,0:T(8,128)S(1)}, f32[64,128]{1,0:T(8,128)S(1)}, u32[]{:S(2)}, u32[]{:S(2)}) collective-permute-start(f32[64,128]{1,0:T(8,128)S(1)} %add.21.refs_0_), channel_id=1, source_target_pairs={{0,3},{1,2},{2,1},{3,0},{4,7},{5,6},{6,5},{7,4},{8,11},{9,10},{10,... | collective-permute-start | bytes 98312 | tf_op jit(solution)/shard_map/ppermute | solution.py:335
  9.3 11.8 %collective-permute-start.2 = (f32[528,128]{1,0:T(8,128)S(1)}, f32[528,128]{1,0:T(8,128)S(1)}, u32[]{:S(2)}, u32[]{:S(2)}) collective-permute-start(f32[528,128]{1,0:T(8,128)S(1)} %get-tuple-element.36), channel_id=1, source_target_pairs={{0,8},{1,9},{2,10},{3,11},{4,12},{5,13},{6,14},{7,15},{8,0},{9,1},... | collective-permute-start | bytes 811016 | tf_op jit(solution)/shard_map/ppermute | solution.py:335
  11.5 5.4 %collective-permute-start.3 = (f32[264,128]{1,0:T(8,128)S(1)}, f32[264,128]{1,0:T(8,128)S(1)}, u32[]{:S(2)}, u32[]{:S(2)}) collective-permute-start(f32[264,128]{1,0:T(8,128)S(1)} %get-tuple-element.37), channel_id=1, source_target_pairs={{0,4},{1,5},{2,6},{3,7},{4,0},{5,1},{6,2},{7,3},{8,12},{9,13},{10,... | collective-permute-start | bytes 405512 | tf_op jit(solution)/shard_map/ppermute | solution.py:335
  13.0 12.2 %collective-permute-start.5 = (f32[264,128]{1,0:T(8,128)S(1)}, f32[264,128]{1,0:T(8,128)S(1)}, u32[]{:S(2)}, u32[]{:S(2)}) collective-permute-start(f32[264,128]{1,0:T(8,128)S(1)} %get-tuple-element.42), channel_id=1, source_target_pairs={{0,28},{1,29},{2,30},{3,31},{4,24},{5,25},{6,26},{7,27},{8,20},{9,... | collective-permute-start | bytes 405512 | tf_op jit(solution)/shard_map/ppermute | solution.py:335
  16.8 11.2 %collective-permute-start.6 = (f32[264,128]{1,0:T(8,128)S(1)}, f32[264,128]{1,0:T(8,128)S(1)}, u32[]{:S(2)}, u32[]{:S(2)}) collective-permute-start(f32[264,128]{1,0:T(8,128)S(1)} %get-tuple-element.43), channel_id=1, source_target_pairs={{0,12},{1,13},{2,14},{3,15},{4,8},{5,9},{6,10},{7,11},{8,4},{9,5},... | collective-permute-start | bytes 405512 | tf_op jit(solution)/shard_map/ppermute | solution.py:335
  21.2 7.4 %collective-permute-start.4 = (f32[264,128]{1,0:T(8,128)S(1)}, f32[264,128]{1,0:T(8,128)S(1)}, u32[]{:S(2)}, u32[]{:S(2)}) collective-permute-start(f32[264,128]{1,0:T(8,128)S(1)} %fusion), channel_id=1, source_target_pairs={{0,16},{1,17},{2,18},{3,19},{4,20},{5,21},{6,22},{7,23},{8,24},{9,... | collective-permute-start | bytes 405512 | tf_op jit(solution)/shard_map/ppermute | solution.py:335
  22.6 6.1 %collective-permute-start.7 = (f32[264,128]{1,0:T(8,128)S(1)}, f32[264,128]{1,0:T(8,128)S(1)}, u32[]{:S(2)}, u32[]{:S(2)}) collective-permute-start(f32[264,128]{1,0:T(8,128)S(1)} %get-tuple-element.44), channel_id=1, source_target_pairs={{0,4},{1,5},{2,6},{3,7},{4,0},{5,1},{6,2},{7,3},{8,12},{9,13},{10,... | collective-permute-start | bytes 405512 | tf_op jit(solution)/shard_map/ppermute | solution.py:335
  29.2 1.2 %collective-permute-start.8 = (f32[32,128]{1,0:T(8,128)S(1)}, f32[32,128]{1,0:T(8,128)S(1)}, u32[]{:S(2)}, u32[]{:S(2)}) collective-permute-start(f32[32,128]{1,0:T(8,128)S(1)} %get-tuple-element.45), channel_id=1, source_target_pairs={{0,1},{1,0},{2,3},{3,2},{4,5},{5,4},{6,7},{7,6},{8,9},{9,8},{10,11... | collective-permute-start | bytes 49160 | tf_op jit(solution)/shard_map/ppermute | solution.py:335
  30.4 4.1 %collective-permute-start.11 = (f32[32,128]{1,0:T(8,128)S(1)}, f32[32,128]{1,0:T(8,128)S(1)}, u32[]{:S(2)}, u32[]{:S(2)}) collective-permute-start(f32[32,128]{1,0:T(8,128)S(1)} %add.24), channel_id=1, source_target_pairs={{0,7},{1,6},{2,5},{3,4},{4,3},{5,2},{6,1},{7,0},{8,15},{9,14},{10,... | collective-permute-start | bytes 49160 | tf_op jit(solution)/shard_map/ppermute | solution.py:335
  32.3 3.2 %collective-permute-start.10 = (f32[32,128]{1,0:T(8,128)S(1)}, f32[32,128]{1,0:T(8,128)S(1)}, u32[]{:S(2)}, u32[]{:S(2)}) collective-permute-start(f32[32,128]{1,0:T(8,128)S(1)} %add.24), channel_id=1, source_target_pairs={{0,5},{1,4},{2,7},{3,6},{4,1},{5,0},{6,3},{7,2},{8,13},{9,12},{10,... | collective-permute-start | bytes 49160 | tf_op jit(solution)/shard_map/ppermute | solution.py:335
  33.1 3.2 %collective-permute-start.9 = (f32[32,128]{1,0:T(8,128)S(1)}, f32[32,128]{1,0:T(8,128)S(1)}, u32[]{:S(2)}, u32[]{:S(2)}) collective-permute-start(f32[32,128]{1,0:T(8,128)S(1)} %add.24), channel_id=1, source_target_pairs={{0,3},{1,2},{2,1},{3,0},{4,7},{5,6},{6,5},{7,4},{8,11},{9,10},{10,... | collective-permute-start | bytes 49160 | tf_op jit(solution)/shard_map/ppermute | solution.py:335
  36.2 5.1 %collective-permute-start.14 = (f32[32,128]{1,0:T(8,128)S(1)}, f32[32,128]{1,0:T(8,128)S(1)}, u32[]{:S(2)}, u32[]{:S(2)}) collective-permute-start(f32[32,128]{1,0:T(8,128)S(1)} %add_add_fusion.gram_ref.refs_0_), channel_id=1, source_target_pairs={{0,25},{1,24},{2,27},{3,26},{4,29},{5,28},{6,31},{7,30},{8,17},{9,... | collective-permute-start | bytes 49160 | tf_op jit(solution)/shard_map/ppermute | solution.py:335
  39.5 4.1 %collective-permute-start.13 = (f32[32,128]{1,0:T(8,128)S(1)}, f32[32,128]{1,0:T(8,128)S(1)}, u32[]{:S(2)}, u32[]{:S(2)}) collective-permute-start(f32[32,128]{1,0:T(8,128)S(1)} %add_add_fusion.gram_ref.refs_0_), channel_id=1, source_target_pairs={{0,17},{1,16},{2,19},{3,18},{4,21},{5,20},{6,23},{7,22},{8,25},{9,... | collective-permute-start | bytes 49160 | tf_op jit(solution)/shard_map/ppermute | solution.py:335
  39.5 4.1 %collective-permute-start.12 = (f32[32,128]{1,0:T(8,128)S(1)}, f32[32,128]{1,0:T(8,128)S(1)}, u32[]{:S(2)}, u32[]{:S(2)}) collective-permute-start(f32[32,128]{1,0:T(8,128)S(1)} %add_add_fusion.gram_ref.refs_0_), channel_id=1, source_target_pairs={{0,9},{1,8},{2,11},{3,10},{4,13},{5,12},{6,15},{7,14},{8,1},{9,0},... | collective-permute-start | bytes 49160 | tf_op jit(solution)/shard_map/ppermute | solution.py:335

commit v7 on v6

--- a/solution.py
+++ b/solution.py
@@ -38,7 +38,7 @@
     return parts[0]
 
 
-def log_kernel(width, counts_hbm, high_ref, low_ref, sum_ref, counts_ref, counts_sem):
+def log_kernel(width, counts_hbm, high_ref, low_ref, counts_ref, counts_sem):
     cells, genes = high_ref.shape
     fetches = [
         pltpu.make_async_copy(
@@ -56,7 +56,6 @@
             high = logged.astype(BF16)
             high_ref[:, lanes] = high
             low_ref[:, lanes] = (logged - high.astype(F32)).astype(BF16)
-            sum_ref[:, lanes] = jnp.sum(logged, axis=0, keepdims=True)
 
 
 def log_terms(counts):
@@ -67,10 +66,9 @@
         out_shape=(
             jax.ShapeDtypeStruct((cells, genes), BF16),
             jax.ShapeDtypeStruct((cells, genes), BF16),
-            jax.ShapeDtypeStruct((1, genes), F32),
         ),
         in_specs=[pl.BlockSpec(memory_space=pltpu.HBM)],
-        out_specs=(WHOLE, WHOLE, WHOLE),
+        out_specs=(WHOLE, WHOLE),
         scratch_shapes=[pltpu.VMEM(counts.shape, BF16), pltpu.SemaphoreType.DMA((genes // width,))],
         compiler_params=LOG_PARAMS,
         cost_estimate=pl.CostEstimate(flops=20 * cells * genes, bytes_accessed=8 * cells * genes, transcendentals=0),
@@ -118,16 +116,14 @@
     return functools.reduce(jnp.add, parts[::-1])
 
 
-def spread_piece(terms, high, low):
-    return term_product(terms, [high, low], NN)
-
-
 def spread_kernel(count, picks, me_ref, *refs):
-    score_refs, outs = refs[:count], refs[count + 4:]
-    high_ref, low_ref, sum_ref, occ_ref = refs[count:count + 4]
+    score_refs, outs = refs[:count], refs[count + 3:]
+    high_ref, low_ref, occ_ref = refs[count:count + 3]
     scores = tree_sum([ref[...] for ref in score_refs])
     comps = scores.shape[0]
-    terms = split_terms(scores, 3)
+    terms = split_terms(scores, 2)
+    scores = terms[0].astype(F32) + terms[1].astype(F32)
+    terms = terms + [jnp.ones_like(scores, BF16)[:8]]
     eye = lax.broadcasted_iota(jnp.int32, (comps, LANES), 0) == lax.broadcasted_iota(jnp.int32, (comps, LANES), 1)
     row_sums = jnp.sum(jnp.where(eye, jnp.sum(scores, axis=1, keepdims=True), 0.0), axis=0, keepdims=True)
     chunks = high_ref.shape[1] // (LANES * lax.axis_size("cells"))
@@ -138,8 +134,10 @@
         base = at_block * rows
         start = pl.multiple_of((me_ref[0] ^ pick) * width, width)
         lanes = pl.ds(start, width)
-        piece = spread_piece(terms, high_ref[:, lanes], low_ref[:, lanes]) * occ_ref[:, lanes]
-        sums = sum_ref[:, lanes] * occ_ref[:, lanes]
+        left = jnp.concatenate([jnp.concatenate([term, term], axis=1) for term in terms], axis=0)
+        out_all = dot(left, jnp.concatenate([high_ref[:, lanes], low_ref[:, lanes]], axis=0), NN) * occ_ref[:, lanes]
+        piece = out_all[comps:2 * comps] + out_all[:comps]
+        sums = out_all[2 * comps:2 * comps + 1]
         extra = [row_sums]
         for at in range(chunks):
             out[base + at * comps:base + (at + 1) * comps] = piece[:, at * LANES:(at + 1) * LANES]
@@ -152,7 +150,7 @@
     return comps * chunks + -(-(chunks + 1) // 8) * 8
 
 
-def spread_pieces(me, scores, high, low, sums, occ, picks):
+def spread_pieces(me, scores, high, low, occ, picks):
     comps = scores[0].shape[0]
     chunks = high.shape[1] // (LANES * lax.axis_size("cells"))
     rows = block_rows(comps, chunks)
@@ -160,14 +158,14 @@
     return pl.pallas_call(
         functools.partial(spread_kernel, len(scores), picks),
         out_shape=[jax.ShapeDtypeStruct((len(group) * rows, LANES), F32) for group in picks],
-        in_specs=[SCALARS] + [WHOLE] * (len(scores) + 4),
+        in_specs=[SCALARS] + [WHOLE] * (len(scores) + 3),
         out_specs=[WHOLE] * len(picks),
         compiler_params=PARAMS,
         cost_estimate=pl.CostEstimate(
             flops=10 * comps * count * chunks * LANES * high.shape[0], bytes_accessed=2**21, transcendentals=0
         ),
         name="spread",
-    )(me, *scores, high, low, sums, occ)
+    )(me, *scores, high, low, occ)
 
 
 def gram_kernel(scale, chunks, *refs):
@@ -348,10 +346,10 @@
     return [x, across[2], across[1], across[0]]
 
 
-def scattered_spread(scores, high, low, sums, occ, cell_total):
+def scattered_spread(scores, high, low, occ, cell_total):
     comps = scores[0].shape[0]
     me = lax.axis_index("cells").astype(jnp.int32).reshape(1)
-    make = functools.partial(spread_pieces, scores=scores, high=high, low=low, sums=sums, occ=occ)
+    make = functools.partial(spread_pieces, scores=scores, high=high, low=low, occ=occ)
     pair, first, across = make(me, picks=[[6, 2], [5], [7]])
     pair, me = lax.optimization_barrier((pair, me))
     pair, first = send(pair, 2, 0), send(first, 1, 0)
@@ -371,7 +369,7 @@
     logged = (logged * occupancy.astype(F32)[:, None, :, None]).reshape(counts.shape)
     high, low = split_terms(logged, 2)
     scores = lax.psum(dot(start_basis, high, NT) + dot(start_basis, low, NT), "genes")
-    spread = spread_piece(split_terms(scores, 3), high, low)
+    spread = term_product(split_terms(scores, 2), [high, low], NN)
     spread = lax.psum_scatter(spread, "cells", scatter_dimension=1, tiled=True)
     rows = lax.psum(jnp.sum(scores, axis=1, keepdims=True), "cells")
     sums = lax.psum_scatter(jnp.sum(logged, axis=0, keepdims=True), "cells", scatter_dimension=1, tiled=True)
@@ -380,10 +378,10 @@
 
 
 def in_steps(counts, occupancy, start_basis):
-    high, low, sums = log_terms(counts)
+    high, low = log_terms(counts)
     scores, occ = score_part(occupancy, start_basis, high, low)
     cell_total = counts.shape[0] * lax.axis_size("cells")
-    spread, gram = scattered_spread(gene_terms(scores), high, low, sums, occ, cell_total)
+    spread, gram = scattered_spread(gene_terms(scores), high, low, occ, cell_total)
     return all_terms(gram), spread
 
 

time: 46.4 us -> 46.2 us (level)
  no operation moved by 1% of the time
where the time goes in v7:
time: 46.2 us; the launch traced here: 46.1 us
  starting transfers between devices  23.2 us (50%)
  waiting for transfers between devices  15.6 us (34%)
  Pallas kernels  6.51 us (14%)
  local copies, waits for them, and re-layouts  0.64 us (1%)
    ppermute x15, starting transfers between devices, send(): return lax.ppermute(x, ('cells', 'genes'), pairs)  23.2 us
    ppermute x15, waiting for transfers between devices, send(): return lax.ppermute(x, ('cells', 'genes'), pairs)  15.6 us
    pallas_call x1, Pallas kernels, orthonormal(): pl.pallas_call(functools.partial(basis_kernel, scale), out_shape=jax.Shap...  2.6 us
    pallas_call x1, Pallas kernels, log_terms(): pl.pallas_call(functools.partial(log_kernel, width), out_shape=(jax.Shape...  1.81 us
  transfers between devices with their start and end apart: 15, of which 13 were waited for; matrix products, arithmetic and copies ran while one was open for 0% of the time, Pallas kernels for 1%

profile of v7, /device:TPU:0, one launch (start us, length us, event | category | flops | bytes accessed | tf_op | source)
XLA Modules:
  0.0 46.1 jit_solution(18369089335184253554)
XLA Ops:
  0.0 1.8 %log_terms.1 = (bf16[128,4096]{1,0:T(8,128)(2,1)S(1)}, bf16[128,4096]{1,0:T(8,128)(2,1)S(1)}) custom-call(bf16[128,4096]{1,0:T(8,128)(2,1)} %counts_hbm.1), custom_call_target="tpu_custom_call" | custom-call | flops 10485760 | bytes 4194304 | tf_op jit(solution)/shard_map/log_terms/pallas_call | solution.py:64
  2.5 0.8 %scores.1 = (f32[64,128]{1,0:T(8,128)S(1)}, f32[1,4096]{1,0:T(1,128)S(1)}) custom-call(s32[1,32]{1,0:T(1,128)S(1)} %copy-done.1, bf16[64,4096]{1,0:T(8,128)(2,1)S(1)} %copy-done, bf16[128,4096]{1,0:T(8,128)(2,1)S(1)} %get-tuple-element.26.high_ref.refs_2_, bf16[128,4096]{1,0:T(8,128)(2,1)S(1)} %get-tuple-element.27.low_ref.refs_3_), custom_call_target="tpu_custom_call" | custom-call | tf_op jit(solution)/shard_map/scores/pallas_call | solution.py:101
  3.8 0.9 %collective-permute-done = f32[64,128]{1,0:T(8,128)S(1)} collective-permute-done((f32[64,128]{1,0:T(8,128)S(1)}, f32[64,128]{1,0:T(8,128)S(1)}, u32[]{:S(2)}, u32[]{:S(2)}) %collective-permute-start) | collective-permute-done | bytes 32800 | tf_op jit(solution)/shard_map/ppermute | solution.py:333
  4.6 2.6 %collective-permute-start.1 = (f32[64,128]{1,0:T(8,128)S(1)}, f32[64,128]{1,0:T(8,128)S(1)}, u32[]{:S(2)}, u32[]{:S(2)}) collective-permute-start(f32[64,128]{1,0:T(8,128)S(1)} %add.21.refs_0_), channel_id=1, source_target_pairs={{0,3},{1,2},{2,1},{3,0},{4,7},{5,6},{6,5},{7,4},{8,11},{9,10},{10,... | collective-permute-start | bytes 98312 | tf_op jit(solution)/shard_map/ppermute | solution.py:333
  7.2 1.6 %collective-permute-done.1.refs_1_ = f32[64,128]{1,0:T(8,128)S(1)} collective-permute-done((f32[64,128]{1,0:T(8,128)S(1)}, f32[64,128]{1,0:T(8,128)S(1)}, u32[]{:S(2)}, u32[]{:S(2)}) %collective-permute-start.1) | collective-permute-done | bytes 32800 | tf_op jit(solution)/shard_map/ppermute | solution.py:333
  9.2 2.1 %collective-permute-start.2 = (f32[528,128]{1,0:T(8,128)S(1)}, f32[528,128]{1,0:T(8,128)S(1)}, u32[]{:S(2)}, u32[]{:S(2)}) collective-permute-start(f32[528,128]{1,0:T(8,128)S(1)} %get-tuple-element.34), channel_id=1, source_target_pairs={{0,8},{1,9},{2,10},{3,11},{4,12},{5,13},{6,14},{7,15},{8,0},{9,1},... | collective-permute-start | bytes 811016 | tf_op jit(solution)/shard_map/ppermute | solution.py:333
  11.3 1.5 %collective-permute-start.3 = (f32[264,128]{1,0:T(8,128)S(1)}, f32[264,128]{1,0:T(8,128)S(1)}, u32[]{:S(2)}, u32[]{:S(2)}) collective-permute-start(f32[264,128]{1,0:T(8,128)S(1)} %get-tuple-element.35), channel_id=1, source_target_pairs={{0,4},{1,5},{2,6},{3,7},{4,0},{5,1},{6,2},{7,3},{8,12},{9,13},{10,... | collective-permute-start | bytes 405512 | tf_op jit(solution)/shard_map/ppermute | solution.py:333
  12.8 2.4 %collective-permute-start.5 = (f32[264,128]{1,0:T(8,128)S(1)}, f32[264,128]{1,0:T(8,128)S(1)}, u32[]{:S(2)}, u32[]{:S(2)}) collective-permute-start(f32[264,128]{1,0:T(8,128)S(1)} %get-tuple-element.40), channel_id=1, source_target_pairs={{0,28},{1,29},{2,30},{3,31},{4,24},{5,25},{6,26},{7,27},{8,20},{9,... | collective-permute-start | bytes 405512 | tf_op jit(solution)/shard_map/ppermute | solution.py:333
  15.6 1.1 %collective-permute-done.3 = f32[264,128]{1,0:T(8,128)S(1)} collective-permute-done((f32[264,128]{1,0:T(8,128)S(1)}, f32[264,128]{1,0:T(8,128)S(1)}, u32[]{:S(2)}, u32[]{:S(2)}) %collective-permute-start.3) | collective-permute-done | bytes 135200 | tf_op jit(solution)/shard_map/ppermute | solution.py:333
  16.7 4.3 %collective-permute-start.6 = (f32[264,128]{1,0:T(8,128)S(1)}, f32[264,128]{1,0:T(8,128)S(1)}, u32[]{:S(2)}, u32[]{:S(2)}) collective-permute-start(f32[264,128]{1,0:T(8,128)S(1)} %get-tuple-element.41), channel_id=1, source_target_pairs={{0,12},{1,13},{2,14},{3,15},{4,8},{5,9},{6,10},{7,11},{8,4},{9,5},... | collective-permute-start | bytes 405512 | tf_op jit(solution)/shard_map/ppermute | solution.py:333
  21.0 1.5 %collective-permute-start.4 = (f32[264,128]{1,0:T(8,128)S(1)}, f32[264,128]{1,0:T(8,128)S(1)}, u32[]{:S(2)}, u32[]{:S(2)}) collective-permute-start(f32[264,128]{1,0:T(8,128)S(1)} %fusion), channel_id=1, source_target_pairs={{0,16},{1,17},{2,18},{3,19},{4,20},{5,21},{6,22},{7,23},{8,24},{9,... | collective-permute-start | bytes 405512 | tf_op jit(solution)/shard_map/ppermute | solution.py:333
  22.5 1.3 %collective-permute-start.7 = (f32[264,128]{1,0:T(8,128)S(1)}, f32[264,128]{1,0:T(8,128)S(1)}, u32[]{:S(2)}, u32[]{:S(2)}) collective-permute-start(f32[264,128]{1,0:T(8,128)S(1)} %get-tuple-element.42), channel_id=1, source_target_pairs={{0,4},{1,5},{2,6},{3,7},{4,0},{5,1},{6,2},{7,3},{8,12},{9,13},{10,... | collective-permute-start | bytes 405512 | tf_op jit(solution)/shard_map/ppermute | solution.py:333
  23.8 1.2 %collective-permute-done.5.refs_3_ = f32[264,128]{1,0:T(8,128)S(1)} collective-permute-done((f32[264,128]{1,0:T(8,128)S(1)}, f32[264,128]{1,0:T(8,128)S(1)}, u32[]{:S(2)}, u32[]{:S(2)}) %collective-permute-start.5) | collective-permute-done | bytes 135200 | tf_op jit(solution)/shard_map/ppermute | solution.py:333
  25.0 2.9 %collective-permute-done.6.refs_4_ = f32[264,128]{1,0:T(8,128)S(1)} collective-permute-done((f32[264,128]{1,0:T(8,128)S(1)}, f32[264,128]{1,0:T(8,128)S(1)}, u32[]{:S(2)}, u32[]{:S(2)}) %collective-permute-start.6) | collective-permute-done | bytes 135200 | tf_op jit(solution)/shard_map/ppermute | solution.py:333
  29.0 1.2 %collective-permute-done.8 = f32[32,128]{1,0:T(8,128)S(1)} collective-permute-done((f32[32,128]{1,0:T(8,128)S(1)}, f32[32,128]{1,0:T(8,128)S(1)}, u32[]{:S(2)}, u32[]{:S(2)}) %collective-permute-start.8) | collective-permute-done | bytes 16416 | tf_op jit(solution)/shard_map/ppermute | solution.py:333
  30.2 1.9 %collective-permute-start.11 = (f32[32,128]{1,0:T(8,128)S(1)}, f32[32,128]{1,0:T(8,128)S(1)}, u32[]{:S(2)}, u32[]{:S(2)}) collective-permute-start(f32[32,128]{1,0:T(8,128)S(1)} %add.24), channel_id=1, source_target_pairs={{0,7},{1,6},{2,5},{3,4},{4,3},{5,2},{6,1},{7,0},{8,15},{9,14},{10,... | collective-permute-start | bytes 49160 | tf_op jit(solution)/shard_map/ppermute | solution.py:333
  32.1 0.8 %collective-permute-start.10 = (f32[32,128]{1,0:T(8,128)S(1)}, f32[32,128]{1,0:T(8,128)S(1)}, u32[]{:S(2)}, u32[]{:S(2)}) collective-permute-start(f32[32,128]{1,0:T(8,128)S(1)} %add.24), channel_id=1, source_target_pairs={{0,5},{1,4},{2,7},{3,6},{4,1},{5,0},{6,3},{7,2},{8,13},{9,12},{10,... | collective-permute-start | bytes 49160 | tf_op jit(solution)/shard_map/ppermute | solution.py:333
  33.2 1.1 %collective-permute-done.11 = f32[32,128]{1,0:T(8,128)S(1)} collective-permute-done((f32[32,128]{1,0:T(8,128)S(1)}, f32[32,128]{1,0:T(8,128)S(1)}, u32[]{:S(2)}, u32[]{:S(2)}) %collective-permute-start.11) | collective-permute-done | bytes 16416 | tf_op jit(solution)/shard_map/ppermute | solution.py:333
  34.3 1.0 %collective-permute-done.10 = f32[32,128]{1,0:T(8,128)S(1)} collective-permute-done((f32[32,128]{1,0:T(8,128)S(1)}, f32[32,128]{1,0:T(8,128)S(1)}, u32[]{:S(2)}, u32[]{:S(2)}) %collective-permute-start.10) | collective-permute-done | bytes 16416 | tf_op jit(solution)/shard_map/ppermute | solution.py:333
  35.3 0.8 %collective-permute-done.9 = f32[32,128]{1,0:T(8,128)S(1)} collective-permute-done((f32[32,128]{1,0:T(8,128)S(1)}, f32[32,128]{1,0:T(8,128)S(1)}, u32[]{:S(2)}, u32[]{:S(2)}) %collective-permute-start.9) | collective-permute-done | bytes 16416 | tf_op jit(solution)/shard_map/ppermute | solution.py:333
  36.1 3.3 %collective-permute-start.14 = (f32[32,128]{1,0:T(8,128)S(1)}, f32[32,128]{1,0:T(8,128)S(1)}, u32[]{:S(2)}, u32[]{:S(2)}) collective-permute-start(f32[32,128]{1,0:T(8,128)S(1)} %add_add_fusion.gram_ref.refs_0_), channel_id=1, source_target_pairs={{0,25},{1,24},{2,27},{3,26},{4,29},{5,28},{6,31},{7,30},{8,17},{9,... | collective-permute-start | bytes 49160 | tf_op jit(solution)/shard_map/ppermute | solution.py:333
  40.2 1.0 %collective-permute-done.14.refs_3_ = f32[32,128]{1,0:T(8,128)S(1)} collective-permute-done((f32[32,128]{1,0:T(8,128)S(1)}, f32[32,128]{1,0:T(8,128)S(1)}, u32[]{:S(2)}, u32[]{:S(2)}) %collective-permute-start.14) | collective-permute-done | bytes 16416 | tf_op jit(solution)/shard_map/ppermute | solution.py:333
  41.2 2.2 %collective-permute-done.13.refs_2_ = f32[32,128]{1,0:T(8,128)S(1)} collective-permute-done((f32[32,128]{1,0:T(8,128)S(1)}, f32[32,128]{1,0:T(8,128)S(1)}, u32[]{:S(2)}, u32[]{:S(2)}) %collective-permute-start.13) | collective-permute-done | bytes 16416 | tf_op jit(solution)/shard_map/ppermute | solution.py:333
  43.4 2.6 %orthonormal.1 = f32[64,512]{1,0:T(8,128)} custom-call(f32[32,128]{1,0:T(8,128)S(1)} %add_add_fusion.gram_ref.refs_0_, f32[32,128]{1,0:T(8,128)S(1)} %collective-permute-done.12.refs_1_, f32[32,128]{1,0:T(8,128)S(1)} %collective-permute-done.13.refs_2_, f32[32,128]{1,0:T(8,128)S(1)} %collective-permute-done.14.refs_3_, ...), custom_call_target="tpu_custom_call" | custom-call | tf_op jit(solution)/shard_map/orthonormal/pallas_call | solution.py:317
  (21 shorter events, 4.2 us)
Async XLA Ops:
  0.0 1.8 %copy-start = (bf16[64,4096]{1,0:T(8,128)(2,1)S(1)}, bf16[64,4096]{1,0:T(8,128)(2,1)}, u32[]{:S(2)}) copy-start(bf16[64,4096]{1,0:T(8,128)(2,1)} %basis_ref.1) | copy-start | bytes 1572868
  1.8 0.7 %copy-start.1 = (s32[1,32]{1,0:T(1,128)S(1)}, s32[1,32]{1,0:T(1,128)}, u32[]{:S(2)}) copy-start(s32[1,32]{1,0:T(1,128)} %occ_ref.1) | copy-start | bytes 388
  3.2 1.4 %collective-permute-start = (f32[64,128]{1,0:T(8,128)S(1)}, f32[64,128]{1,0:T(8,128)S(1)}, u32[]{:S(2)}, u32[]{:S(2)}) collective-permute-start(f32[64,128]{1,0:T(8,128)S(1)} %get-tuple-element.28), channel_id=1, source_target_pairs={{0,1},{1,0},{2,3},{3,2},{4,5},{5,4},{6,7},{7,6},{8,9},{9,8},{10,11... | collective-permute-start | bytes 98312 | tf_op jit(solution)/shard_map/ppermute | solution.py:333
  4.6 4.2 %collective-permute-start.1 = (f32[64,128]{1,0:T(8,128)S(1)}, f32[64,128]{1,0:T(8,128)S(1)}, u32[]{:S(2)}, u32[]{:S(2)}) collective-permute-start(f32[64,128]{1,0:T(8,128)S(1)} %add.21.refs_0_), channel_id=1, source_target_pairs={{0,3},{1,2},{2,1},{3,0},{4,7},{5,6},{6,5},{7,4},{8,11},{9,10},{10,... | collective-permute-start | bytes 98312 | tf_op jit(solution)/shard_map/ppermute | solution.py:333
  9.2 11.8 %collective-permute-start.2 = (f32[528,128]{1,0:T(8,128)S(1)}, f32[528,128]{1,0:T(8,128)S(1)}, u32[]{:S(2)}, u32[]{:S(2)}) collective-permute-start(f32[528,128]{1,0:T(8,128)S(1)} %get-tuple-element.34), channel_id=1, source_target_pairs={{0,8},{1,9},{2,10},{3,11},{4,12},{5,13},{6,14},{7,15},{8,0},{9,1},... | collective-permute-start | bytes 811016 | tf_op jit(solution)/shard_map/ppermute | solution.py:333
  11.3 5.4 %collective-permute-start.3 = (f32[264,128]{1,0:T(8,128)S(1)}, f32[264,128]{1,0:T(8,128)S(1)}, u32[]{:S(2)}, u32[]{:S(2)}) collective-permute-start(f32[264,128]{1,0:T(8,128)S(1)} %get-tuple-element.35), channel_id=1, source_target_pairs={{0,4},{1,5},{2,6},{3,7},{4,0},{5,1},{6,2},{7,3},{8,12},{9,13},{10,... | collective-permute-start | bytes 405512 | tf_op jit(solution)/shard_map/ppermute | solution.py:333
  12.8 12.2 %collective-permute-start.5 = (f32[264,128]{1,0:T(8,128)S(1)}, f32[264,128]{1,0:T(8,128)S(1)}, u32[]{:S(2)}, u32[]{:S(2)}) collective-permute-start(f32[264,128]{1,0:T(8,128)S(1)} %get-tuple-element.40), channel_id=1, source_target_pairs={{0,28},{1,29},{2,30},{3,31},{4,24},{5,25},{6,26},{7,27},{8,20},{9,... | collective-permute-start | bytes 405512 | tf_op jit(solution)/shard_map/ppermute | solution.py:333
  16.7 11.2 %collective-permute-start.6 = (f32[264,128]{1,0:T(8,128)S(1)}, f32[264,128]{1,0:T(8,128)S(1)}, u32[]{:S(2)}, u32[]{:S(2)}) collective-permute-start(f32[264,128]{1,0:T(8,128)S(1)} %get-tuple-element.41), channel_id=1, source_target_pairs={{0,12},{1,13},{2,14},{3,15},{4,8},{5,9},{6,10},{7,11},{8,4},{9,5},... | collective-permute-start | bytes 405512 | tf_op jit(solution)/shard_map/ppermute | solution.py:333
  21.0 7.4 %collective-permute-start.4 = (f32[264,128]{1,0:T(8,128)S(1)}, f32[264,128]{1,0:T(8,128)S(1)}, u32[]{:S(2)}, u32[]{:S(2)}) collective-permute-start(f32[264,128]{1,0:T(8,128)S(1)} %fusion), channel_id=1, source_target_pairs={{0,16},{1,17},{2,18},{3,19},{4,20},{5,21},{6,22},{7,23},{8,24},{9,... | collective-permute-start | bytes 405512 | tf_op jit(solution)/shard_map/ppermute | solution.py:333
  22.5 6.1 %collective-permute-start.7 = (f32[264,128]{1,0:T(8,128)S(1)}, f32[264,128]{1,0:T(8,128)S(1)}, u32[]{:S(2)}, u32[]{:S(2)}) collective-permute-start(f32[264,128]{1,0:T(8,128)S(1)} %get-tuple-element.42), channel_id=1, source_target_pairs={{0,4},{1,5},{2,6},{3,7},{4,0},{5,1},{6,2},{7,3},{8,12},{9,13},{10,... | collective-permute-start | bytes 405512 | tf_op jit(solution)/shard_map/ppermute | solution.py:333
  29.0 1.2 %collective-permute-start.8 = (f32[32,128]{1,0:T(8,128)S(1)}, f32[32,128]{1,0:T(8,128)S(1)}, u32[]{:S(2)}, u32[]{:S(2)}) collective-permute-start(f32[32,128]{1,0:T(8,128)S(1)} %get-tuple-element.43), channel_id=1, source_target_pairs={{0,1},{1,0},{2,3},{3,2},{4,5},{5,4},{6,7},{7,6},{8,9},{9,8},{10,11... | collective-permute-start | bytes 49160 | tf_op jit(solution)/shard_map/ppermute | solution.py:333
  30.2 4.1 %collective-permute-start.11 = (f32[32,128]{1,0:T(8,128)S(1)}, f32[32,128]{1,0:T(8,128)S(1)}, u32[]{:S(2)}, u32[]{:S(2)}) collective-permute-start(f32[32,128]{1,0:T(8,128)S(1)} %add.24), channel_id=1, source_target_pairs={{0,7},{1,6},{2,5},{3,4},{4,3},{5,2},{6,1},{7,0},{8,15},{9,14},{10,... | collective-permute-start | bytes 49160 | tf_op jit(solution)/shard_map/ppermute | solution.py:333
  32.1 3.2 %collective-permute-start.10 = (f32[32,128]{1,0:T(8,128)S(1)}, f32[32,128]{1,0:T(8,128)S(1)}, u32[]{:S(2)}, u32[]{:S(2)}) collective-permute-start(f32[32,128]{1,0:T(8,128)S(1)} %add.24), channel_id=1, source_target_pairs={{0,5},{1,4},{2,7},{3,6},{4,1},{5,0},{6,3},{7,2},{8,13},{9,12},{10,... | collective-permute-start | bytes 49160 | tf_op jit(solution)/shard_map/ppermute | solution.py:333
  32.9 3.2 %collective-permute-start.9 = (f32[32,128]{1,0:T(8,128)S(1)}, f32[32,128]{1,0:T(8,128)S(1)}, u32[]{:S(2)}, u32[]{:S(2)}) collective-permute-start(f32[32,128]{1,0:T(8,128)S(1)} %add.24), channel_id=1, source_target_pairs={{0,3},{1,2},{2,1},{3,0},{4,7},{5,6},{6,5},{7,4},{8,11},{9,10},{10,... | collective-permute-start | bytes 49160 | tf_op jit(solution)/shard_map/ppermute | solution.py:333
  36.1 5.1 %collective-permute-start.14 = (f32[32,128]{1,0:T(8,128)S(1)}, f32[32,128]{1,0:T(8,128)S(1)}, u32[]{:S(2)}, u32[]{:S(2)}) collective-permute-start(f32[32,128]{1,0:T(8,128)S(1)} %add_add_fusion.gram_ref.refs_0_), channel_id=1, source_target_pairs={{0,25},{1,24},{2,27},{3,26},{4,29},{5,28},{6,31},{7,30},{8,17},{9,... | collective-permute-start | bytes 49160 | tf_op jit(solution)/shard_map/ppermute | solution.py:333
  39.4 4.1 %collective-permute-start.13 = (f32[32,128]{1,0:T(8,128)S(1)}, f32[32,128]{1,0:T(8,128)S(1)}, u32[]{:S(2)}, u32[]{:S(2)}) collective-permute-start(f32[32,128]{1,0:T(8,128)S(1)} %add_add_fusion.gram_ref.refs_0_), channel_id=1, source_target_pairs={{0,17},{1,16},{2,19},{3,18},{4,21},{5,20},{6,23},{7,22},{8,25},{9,... | collective-permute-start | bytes 49160 | tf_op jit(solution)/shard_map/ppermute | solution.py:333
  39.4 4.1 %collective-permute-start.12 = (f32[32,128]{1,0:T(8,128)S(1)}, f32[32,128]{1,0:T(8,128)S(1)}, u32[]{:S(2)}, u32[]{:S(2)}) collective-permute-start(f32[32,128]{1,0:T(8,128)S(1)} %add_add_fusion.gram_ref.refs_0_), channel_id=1, source_target_pairs={{0,9},{1,8},{2,11},{3,10},{4,13},{5,12},{6,15},{7,14},{8,1},{9,0},... | collective-permute-start | bytes 49160 | tf_op jit(solution)/shard_map/ppermute | solution.py:333

commit v8 on v7

--- a/solution.py
+++ b/solution.py
@@ -342,8 +342,8 @@
     x = x + send(x, 0, 1)
     across = [send(x, c, g) for c, g in ((1, 3), (1, 1), (0, 3))]
     x = (x + across[2]) + (across[1] + across[0])
-    across = [send(x, c, 1) for c in (6, 4, 2)]
-    return [x, across[2], across[1], across[0]]
+    far, both, near = [send(x, c, 1) for c in (4, 6, 2)]
+    return [x, near, far, both]
 
 
 def scattered_spread(scores, high, low, occ, cell_total):

time: 46.2 us -> 46.2 us (level)
  no operation moved by 1% of the time
where the time goes in v8:
time: 46.2 us; the launch traced here: 46.1 us
  starting transfers between devices  23.2 us (50%)
  waiting for transfers between devices  15.6 us (34%)
  Pallas kernels  6.51 us (14%)
  local copies, waits for them, and re-layouts  0.64 us (1%)
    ppermute x15, starting transfers between devices, send(): return lax.ppermute(x, ('cells', 'genes'), pairs)  23.2 us
    ppermute x15, waiting for transfers between devices, send(): return lax.ppermute(x, ('cells', 'genes'), pairs)  15.6 us
    pallas_call x1, Pallas kernels, orthonormal(): pl.pallas_call(functools.partial(basis_kernel, scale), out_shape=jax.Shap...  2.6 us
    pallas_call x1, Pallas kernels, log_terms(): pl.pallas_call(functools.partial(log_kernel, width), out_shape=(jax.Shape...  1.81 us
  transfers between devices with their start and end apart: 15, of which 13 were waited for; matrix products, arithmetic and copies ran while one was open for 0% of the time, Pallas kernels for 1%

profile of v8, /device:TPU:0, one launch (start us, length us, event | category | flops | bytes accessed | tf_op | source)
XLA Modules:
  0.0 46.1 jit_solution(18369089335184253554)
XLA Ops:
  0.0 1.8 %log_terms.1 = (bf16[128,4096]{1,0:T(8,128)(2,1)S(1)}, bf16[128,4096]{1,0:T(8,128)(2,1)S(1)}) custom-call(bf16[128,4096]{1,0:T(8,128)(2,1)} %counts_hbm.1), custom_call_target="tpu_custom_call" | custom-call | flops 10485760 | bytes 4194304 | tf_op jit(solution)/shard_map/log_terms/pallas_call | solution.py:64
  2.5 0.8 %scores.1 = (f32[64,128]{1,0:T(8,128)S(1)}, f32[1,4096]{1,0:T(1,128)S(1)}) custom-call(s32[1,32]{1,0:T(1,128)S(1)} %copy-done.1, bf16[64,4096]{1,0:T(8,128)(2,1)S(1)} %copy-done, bf16[128,4096]{1,0:T(8,128)(2,1)S(1)} %get-tuple-element.26.high_ref.refs_2_, bf16[128,4096]{1,0:T(8,128)(2,1)S(1)} %get-tuple-element.27.low_ref.refs_3_), custom_call_target="tpu_custom_call" | custom-call | tf_op jit(solution)/shard_map/scores/pallas_call | solution.py:101
  3.8 0.9 %collective-permute-done = f32[64,128]{1,0:T(8,128)S(1)} collective-permute-done((f32[64,128]{1,0:T(8,128)S(1)}, f32[64,128]{1,0:T(8,128)S(1)}, u32[]{:S(2)}, u32[]{:S(2)}) %collective-permute-start) | collective-permute-done | bytes 32800 | tf_op jit(solution)/shard_map/ppermute | solution.py:333
  4.6 2.6 %collective-permute-start.1 = (f32[64,128]{1,0:T(8,128)S(1)}, f32[64,128]{1,0:T(8,128)S(1)}, u32[]{:S(2)}, u32[]{:S(2)}) collective-permute-start(f32[64,128]{1,0:T(8,128)S(1)} %add.21.refs_0_), channel_id=1, source_target_pairs={{0,3},{1,2},{2,1},{3,0},{4,7},{5,6},{6,5},{7,4},{8,11},{9,10},{10,... | collective-permute-start | bytes 98312 | tf_op jit(solution)/shard_map/ppermute | solution.py:333
  7.2 1.6 %collective-permute-done.1.refs_1_ = f32[64,128]{1,0:T(8,128)S(1)} collective-permute-done((f32[64,128]{1,0:T(8,128)S(1)}, f32[64,128]{1,0:T(8,128)S(1)}, u32[]{:S(2)}, u32[]{:S(2)}) %collective-permute-start.1) | collective-permute-done | bytes 32800 | tf_op jit(solution)/shard_map/ppermute | solution.py:333
  9.2 2.1 %collective-permute-start.2 = (f32[528,128]{1,0:T(8,128)S(1)}, f32[528,128]{1,0:T(8,128)S(1)}, u32[]{:S(2)}, u32[]{:S(2)}) collective-permute-start(f32[528,128]{1,0:T(8,128)S(1)} %get-tuple-element.34), channel_id=1, source_target_pairs={{0,8},{1,9},{2,10},{3,11},{4,12},{5,13},{6,14},{7,15},{8,0},{9,1},... | collective-permute-start | bytes 811016 | tf_op jit(solution)/shard_map/ppermute | solution.py:333
  11.3 1.5 %collective-permute-start.3 = (f32[264,128]{1,0:T(8,128)S(1)}, f32[264,128]{1,0:T(8,128)S(1)}, u32[]{:S(2)}, u32[]{:S(2)}) collective-permute-start(f32[264,128]{1,0:T(8,128)S(1)} %get-tuple-element.35), channel_id=1, source_target_pairs={{0,4},{1,5},{2,6},{3,7},{4,0},{5,1},{6,2},{7,3},{8,12},{9,13},{10,... | collective-permute-start | bytes 405512 | tf_op jit(solution)/shard_map/ppermute | solution.py:333
  12.8 2.4 %collective-permute-start.5 = (f32[264,128]{1,0:T(8,128)S(1)}, f32[264,128]{1,0:T(8,128)S(1)}, u32[]{:S(2)}, u32[]{:S(2)}) collective-permute-start(f32[264,128]{1,0:T(8,128)S(1)} %get-tuple-element.40), channel_id=1, source_target_pairs={{0,28},{1,29},{2,30},{3,31},{4,24},{5,25},{6,26},{7,27},{8,20},{9,... | collective-permute-start | bytes 405512 | tf_op jit(solution)/shard_map/ppermute | solution.py:333
  15.6 1.1 %collective-permute-done.3 = f32[264,128]{1,0:T(8,128)S(1)} collective-permute-done((f32[264,128]{1,0:T(8,128)S(1)}, f32[264,128]{1,0:T(8,128)S(1)}, u32[]{:S(2)}, u32[]{:S(2)}) %collective-permute-start.3) | collective-permute-done | bytes 135200 | tf_op jit(solution)/shard_map/ppermute | solution.py:333
  16.7 4.3 %collective-permute-start.6 = (f32[264,128]{1,0:T(8,128)S(1)}, f32[264,128]{1,0:T(8,128)S(1)}, u32[]{:S(2)}, u32[]{:S(2)}) collective-permute-start(f32[264,128]{1,0:T(8,128)S(1)} %get-tuple-element.41), channel_id=1, source_target_pairs={{0,12},{1,13},{2,14},{3,15},{4,8},{5,9},{6,10},{7,11},{8,4},{9,5},... | collective-permute-start | bytes 405512 | tf_op jit(solution)/shard_map/ppermute | solution.py:333
  21.0 1.5 %collective-permute-start.4 = (f32[264,128]{1,0:T(8,128)S(1)}, f32[264,128]{1,0:T(8,128)S(1)}, u32[]{:S(2)}, u32[]{:S(2)}) collective-permute-start(f32[264,128]{1,0:T(8,128)S(1)} %fusion), channel_id=1, source_target_pairs={{0,16},{1,17},{2,18},{3,19},{4,20},{5,21},{6,22},{7,23},{8,24},{9,... | collective-permute-start | bytes 405512 | tf_op jit(solution)/shard_map/ppermute | solution.py:333
  22.5 1.3 %collective-permute-start.7 = (f32[264,128]{1,0:T(8,128)S(1)}, f32[264,128]{1,0:T(8,128)S(1)}, u32[]{:S(2)}, u32[]{:S(2)}) collective-permute-start(f32[264,128]{1,0:T(8,128)S(1)} %get-tuple-element.42), channel_id=1, source_target_pairs={{0,4},{1,5},{2,6},{3,7},{4,0},{5,1},{6,2},{7,3},{8,12},{9,13},{10,... | collective-permute-start | bytes 405512 | tf_op jit(solution)/shard_map/ppermute | solution.py:333
  23.8 1.2 %collective-permute-done.5.refs_3_ = f32[264,128]{1,0:T(8,128)S(1)} collective-permute-done((f32[264,128]{1,0:T(8,128)S(1)}, f32[264,128]{1,0:T(8,128)S(1)}, u32[]{:S(2)}, u32[]{:S(2)}) %collective-permute-start.5) | collective-permute-done | bytes 135200 | tf_op jit(solution)/shard_map/ppermute | solution.py:333
  25.0 2.9 %collective-permute-done.6.refs_4_ = f32[264,128]{1,0:T(8,128)S(1)} collective-permute-done((f32[264,128]{1,0:T(8,128)S(1)}, f32[264,128]{1,0:T(8,128)S(1)}, u32[]{:S(2)}, u32[]{:S(2)}) %collective-permute-start.6) | collective-permute-done | bytes 135200 | tf_op jit(solution)/shard_map/ppermute | solution.py:333
  29.0 1.2 %collective-permute-done.8 = f32[32,128]{1,0:T(8,128)S(1)} collective-permute-done((f32[32,128]{1,0:T(8,128)S(1)}, f32[32,128]{1,0:T(8,128)S(1)}, u32[]{:S(2)}, u32[]{:S(2)}) %collective-permute-start.8) | collective-permute-done | bytes 16416 | tf_op jit(solution)/shard_map/ppermute | solution.py:333
  30.2 1.9 %collective-permute-start.11 = (f32[32,128]{1,0:T(8,128)S(1)}, f32[32,128]{1,0:T(8,128)S(1)}, u32[]{:S(2)}, u32[]{:S(2)}) collective-permute-start(f32[32,128]{1,0:T(8,128)S(1)} %add.24), channel_id=1, source_target_pairs={{0,7},{1,6},{2,5},{3,4},{4,3},{5,2},{6,1},{7,0},{8,15},{9,14},{10,... | collective-permute-start | bytes 49160 | tf_op jit(solution)/shard_map/ppermute | solution.py:333
  32.1 0.8 %collective-permute-start.10 = (f32[32,128]{1,0:T(8,128)S(1)}, f32[32,128]{1,0:T(8,128)S(1)}, u32[]{:S(2)}, u32[]{:S(2)}) collective-permute-start(f32[32,128]{1,0:T(8,128)S(1)} %add.24), channel_id=1, source_target_pairs={{0,5},{1,4},{2,7},{3,6},{4,1},{5,0},{6,3},{7,2},{8,13},{9,12},{10,... | collective-permute-start | bytes 49160 | tf_op jit(solution)/shard_map/ppermute | solution.py:333
  33.2 1.1 %collective-permute-done.11 = f32[32,128]{1,0:T(8,128)S(1)} collective-permute-done((f32[32,128]{1,0:T(8,128)S(1)}, f32[32,128]{1,0:T(8,128)S(1)}, u32[]{:S(2)}, u32[]{:S(2)}) %collective-permute-start.11) | collective-permute-done | bytes 16416 | tf_op jit(solution)/shard_map/ppermute | solution.py:333
  34.3 1.0 %collective-permute-done.10 = f32[32,128]{1,0:T(8,128)S(1)} collective-permute-done((f32[32,128]{1,0:T(8,128)S(1)}, f32[32,128]{1,0:T(8,128)S(1)}, u32[]{:S(2)}, u32[]{:S(2)}) %collective-permute-start.10) | collective-permute-done | bytes 16416 | tf_op jit(solution)/shard_map/ppermute | solution.py:333
  35.3 0.8 %collective-permute-done.9 = f32[32,128]{1,0:T(8,128)S(1)} collective-permute-done((f32[32,128]{1,0:T(8,128)S(1)}, f32[32,128]{1,0:T(8,128)S(1)}, u32[]{:S(2)}, u32[]{:S(2)}) %collective-permute-start.9) | collective-permute-done | bytes 16416 | tf_op jit(solution)/shard_map/ppermute | solution.py:333
  36.1 3.3 %collective-permute-start.14 = (f32[32,128]{1,0:T(8,128)S(1)}, f32[32,128]{1,0:T(8,128)S(1)}, u32[]{:S(2)}, u32[]{:S(2)}) collective-permute-start(f32[32,128]{1,0:T(8,128)S(1)} %add_add_fusion.gram_ref.refs_0_), channel_id=1, source_target_pairs={{0,25},{1,24},{2,27},{3,26},{4,29},{5,28},{6,31},{7,30},{8,17},{9,... | collective-permute-start | bytes 49160 | tf_op jit(solution)/shard_map/ppermute | solution.py:333
  40.2 1.0 %collective-permute-done.14.refs_3_ = f32[32,128]{1,0:T(8,128)S(1)} collective-permute-done((f32[32,128]{1,0:T(8,128)S(1)}, f32[32,128]{1,0:T(8,128)S(1)}, u32[]{:S(2)}, u32[]{:S(2)}) %collective-permute-start.14) | collective-permute-done | bytes 16416 | tf_op jit(solution)/shard_map/ppermute | solution.py:333
  41.2 2.2 %collective-permute-done.13.refs_2_ = f32[32,128]{1,0:T(8,128)S(1)} collective-permute-done((f32[32,128]{1,0:T(8,128)S(1)}, f32[32,128]{1,0:T(8,128)S(1)}, u32[]{:S(2)}, u32[]{:S(2)}) %collective-permute-start.13) | collective-permute-done | bytes 16416 | tf_op jit(solution)/shard_map/ppermute | solution.py:333
  43.4 2.6 %orthonormal.1 = f32[64,512]{1,0:T(8,128)} custom-call(f32[32,128]{1,0:T(8,128)S(1)} %add_add_fusion.gram_ref.refs_0_, f32[32,128]{1,0:T(8,128)S(1)} %collective-permute-done.12.refs_1_, f32[32,128]{1,0:T(8,128)S(1)} %collective-permute-done.13.refs_2_, f32[32,128]{1,0:T(8,128)S(1)} %collective-permute-done.14.refs_3_, ...), custom_call_target="tpu_custom_call" | custom-call | tf_op jit(solution)/shard_map/orthonormal/pallas_call | solution.py:317
  (21 shorter events, 4.2 us)
Async XLA Ops:
  0.0 1.8 %copy-start = (bf16[64,4096]{1,0:T(8,128)(2,1)S(1)}, bf16[64,4096]{1,0:T(8,128)(2,1)}, u32[]{:S(2)}) copy-start(bf16[64,4096]{1,0:T(8,128)(2,1)} %basis_ref.1) | copy-start | bytes 1572868
  1.8 0.7 %copy-start.1 = (s32[1,32]{1,0:T(1,128)S(1)}, s32[1,32]{1,0:T(1,128)}, u32[]{:S(2)}) copy-start(s32[1,32]{1,0:T(1,128)} %occ_ref.1) | copy-start | bytes 388
  3.2 1.4 %collective-permute-start = (f32[64,128]{1,0:T(8,128)S(1)}, f32[64,128]{1,0:T(8,128)S(1)}, u32[]{:S(2)}, u32[]{:S(2)}) collective-permute-start(f32[64,128]{1,0:T(8,128)S(1)} %get-tuple-element.28), channel_id=1, source_target_pairs={{0,1},{1,0},{2,3},{3,2},{4,5},{5,4},{6,7},{7,6},{8,9},{9,8},{10,11... | collective-permute-start | bytes 98312 | tf_op jit(solution)/shard_map/ppermute | solution.py:333
  4.6 4.2 %collective-permute-start.1 = (f32[64,128]{1,0:T(8,128)S(1)}, f32[64,128]{1,0:T(8,128)S(1)}, u32[]{:S(2)}, u32[]{:S(2)}) collective-permute-start(f32[64,128]{1,0:T(8,128)S(1)} %add.21.refs_0_), channel_id=1, source_target_pairs={{0,3},{1,2},{2,1},{3,0},{4,7},{5,6},{6,5},{7,4},{8,11},{9,10},{10,... | collective-permute-start | bytes 98312 | tf_op jit(solution)/shard_map/ppermute | solution.py:333
  9.2 11.8 %collective-permute-start.2 = (f32[528,128]{1,0:T(8,128)S(1)}, f32[528,128]{1,0:T(8,128)S(1)}, u32[]{:S(2)}, u32[]{:S(2)}) collective-permute-start(f32[528,128]{1,0:T(8,128)S(1)} %get-tuple-element.34), channel_id=1, source_target_pairs={{0,8},{1,9},{2,10},{3,11},{4,12},{5,13},{6,14},{7,15},{8,0},{9,1},... | collective-permute-start | bytes 811016 | tf_op jit(solution)/shard_map/ppermute | solution.py:333
  11.3 5.4 %collective-permute-start.3 = (f32[264,128]{1,0:T(8,128)S(1)}, f32[264,128]{1,0:T(8,128)S(1)}, u32[]{:S(2)}, u32[]{:S(2)}) collective-permute-start(f32[264,128]{1,0:T(8,128)S(1)} %get-tuple-element.35), channel_id=1, source_target_pairs={{0,4},{1,5},{2,6},{3,7},{4,0},{5,1},{6,2},{7,3},{8,12},{9,13},{10,... | collective-permute-start | bytes 405512 | tf_op jit(solution)/shard_map/ppermute | solution.py:333
  12.8 12.2 %collective-permute-start.5 = (f32[264,128]{1,0:T(8,128)S(1)}, f32[264,128]{1,0:T(8,128)S(1)}, u32[]{:S(2)}, u32[]{:S(2)}) collective-permute-start(f32[264,128]{1,0:T(8,128)S(1)} %get-tuple-element.40), channel_id=1, source_target_pairs={{0,28},{1,29},{2,30},{3,31},{4,24},{5,25},{6,26},{7,27},{8,20},{9,... | collective-permute-start | bytes 405512 | tf_op jit(solution)/shard_map/ppermute | solution.py:333
  16.7 11.2 %collective-permute-start.6 = (f32[264,128]{1,0:T(8,128)S(1)}, f32[264,128]{1,0:T(8,128)S(1)}, u32[]{:S(2)}, u32[]{:S(2)}) collective-permute-start(f32[264,128]{1,0:T(8,128)S(1)} %get-tuple-element.41), channel_id=1, source_target_pairs={{0,12},{1,13},{2,14},{3,15},{4,8},{5,9},{6,10},{7,11},{8,4},{9,5},... | collective-permute-start | bytes 405512 | tf_op jit(solution)/shard_map/ppermute | solution.py:333
  21.0 7.4 %collective-permute-start.4 = (f32[264,128]{1,0:T(8,128)S(1)}, f32[264,128]{1,0:T(8,128)S(1)}, u32[]{:S(2)}, u32[]{:S(2)}) collective-permute-start(f32[264,128]{1,0:T(8,128)S(1)} %fusion), channel_id=1, source_target_pairs={{0,16},{1,17},{2,18},{3,19},{4,20},{5,21},{6,22},{7,23},{8,24},{9,... | collective-permute-start | bytes 405512 | tf_op jit(solution)/shard_map/ppermute | solution.py:333
  22.5 6.1 %collective-permute-start.7 = (f32[264,128]{1,0:T(8,128)S(1)}, f32[264,128]{1,0:T(8,128)S(1)}, u32[]{:S(2)}, u32[]{:S(2)}) collective-permute-start(f32[264,128]{1,0:T(8,128)S(1)} %get-tuple-element.42), channel_id=1, source_target_pairs={{0,4},{1,5},{2,6},{3,7},{4,0},{5,1},{6,2},{7,3},{8,12},{9,13},{10,... | collective-permute-start | bytes 405512 | tf_op jit(solution)/shard_map/ppermute | solution.py:333
  29.0 1.2 %collective-permute-start.8 = (f32[32,128]{1,0:T(8,128)S(1)}, f32[32,128]{1,0:T(8,128)S(1)}, u32[]{:S(2)}, u32[]{:S(2)}) collective-permute-start(f32[32,128]{1,0:T(8,128)S(1)} %get-tuple-element.43), channel_id=1, source_target_pairs={{0,1},{1,0},{2,3},{3,2},{4,5},{5,4},{6,7},{7,6},{8,9},{9,8},{10,11... | collective-permute-start | bytes 49160 | tf_op jit(solution)/shard_map/ppermute | solution.py:333
  30.2 4.1 %collective-permute-start.11 = (f32[32,128]{1,0:T(8,128)S(1)}, f32[32,128]{1,0:T(8,128)S(1)}, u32[]{:S(2)}, u32[]{:S(2)}) collective-permute-start(f32[32,128]{1,0:T(8,128)S(1)} %add.24), channel_id=1, source_target_pairs={{0,7},{1,6},{2,5},{3,4},{4,3},{5,2},{6,1},{7,0},{8,15},{9,14},{10,... | collective-permute-start | bytes 49160 | tf_op jit(solution)/shard_map/ppermute | solution.py:333
  32.1 3.2 %collective-permute-start.10 = (f32[32,128]{1,0:T(8,128)S(1)}, f32[32,128]{1,0:T(8,128)S(1)}, u32[]{:S(2)}, u32[]{:S(2)}) collective-permute-start(f32[32,128]{1,0:T(8,128)S(1)} %add.24), channel_id=1, source_target_pairs={{0,5},{1,4},{2,7},{3,6},{4,1},{5,0},{6,3},{7,2},{8,13},{9,12},{10,... | collective-permute-start | bytes 49160 | tf_op jit(solution)/shard_map/ppermute | solution.py:333
  32.9 3.2 %collective-permute-start.9 = (f32[32,128]{1,0:T(8,128)S(1)}, f32[32,128]{1,0:T(8,128)S(1)}, u32[]{:S(2)}, u32[]{:S(2)}) collective-permute-start(f32[32,128]{1,0:T(8,128)S(1)} %add.24), channel_id=1, source_target_pairs={{0,3},{1,2},{2,1},{3,0},{4,7},{5,6},{6,5},{7,4},{8,11},{9,10},{10,... | collective-permute-start | bytes 49160 | tf_op jit(solution)/shard_map/ppermute | solution.py:333
  36.1 5.1 %collective-permute-start.14 = (f32[32,128]{1,0:T(8,128)S(1)}, f32[32,128]{1,0:T(8,128)S(1)}, u32[]{:S(2)}, u32[]{:S(2)}) collective-permute-start(f32[32,128]{1,0:T(8,128)S(1)} %add_add_fusion.gram_ref.refs_0_), channel_id=1, source_target_pairs={{0,25},{1,24},{2,27},{3,26},{4,29},{5,28},{6,31},{7,30},{8,17},{9,... | collective-permute-start | bytes 49160 | tf_op jit(solution)/shard_map/ppermute | solution.py:333
  39.4 4.1 %collective-permute-start.13 = (f32[32,128]{1,0:T(8,128)S(1)}, f32[32,128]{1,0:T(8,128)S(1)}, u32[]{:S(2)}, u32[]{:S(2)}) collective-permute-start(f32[32,128]{1,0:T(8,128)S(1)} %add_add_fusion.gram_ref.refs_0_), channel_id=1, source_target_pairs={{0,17},{1,16},{2,19},{3,18},{4,21},{5,20},{6,23},{7,22},{8,25},{9,... | collective-permute-start | bytes 49160 | tf_op jit(solution)/shard_map/ppermute | solution.py:333
  39.4 4.1 %collective-permute-start.12 = (f32[32,128]{1,0:T(8,128)S(1)}, f32[32,128]{1,0:T(8,128)S(1)}, u32[]{:S(2)}, u32[]{:S(2)}) collective-permute-start(f32[32,128]{1,0:T(8,128)S(1)} %add_add_fusion.gram_ref.refs_0_), channel_id=1, source_target_pairs={{0,9},{1,8},{2,11},{3,10},{4,13},{5,12},{6,15},{7,14},{8,1},{9,0},... | collective-permute-start | bytes 49160 | tf_op jit(solution)/shard_map/ppermute | solution.py:333

commit v9 on v8

--- a/solution.py
+++ b/solution.py
@@ -343,7 +343,7 @@
     across = [send(x, c, g) for c, g in ((1, 3), (1, 1), (0, 3))]
     x = (x + across[2]) + (across[1] + across[0])
     far, both, near = [send(x, c, 1) for c in (4, 6, 2)]
-    return [x, near, far, both]
+    return [x, near, both, far]
 
 
 def scattered_spread(scores, high, low, occ, cell_total):

time: 46.2 us -> 46.1 us (level)
  no operation moved by 1% of the time
where the time goes in v9:
time: 46.1 us; the launch traced here: 46 us
  starting transfers between devices  23.4 us (51%)
  waiting for transfers between devices  15.3 us (33%)
  Pallas kernels  6.51 us (14%)
  local copies, waits for them, and re-layouts  0.64 us (1%)
    ppermute x15, starting transfers between devices, send(): return lax.ppermute(x, ('cells', 'genes'), pairs)  23.4 us
    ppermute x15, waiting for transfers between devices, send(): return lax.ppermute(x, ('cells', 'genes'), pairs)  15.3 us
    pallas_call x1, Pallas kernels, orthonormal(): pl.pallas_call(functools.partial(basis_kernel, scale), out_shape=jax.Shap...  2.6 us
    pallas_call x1, Pallas kernels, log_terms(): pl.pallas_call(functools.partial(log_kernel, width), out_shape=(jax.Shape...  1.81 us
  transfers between devices with their start and end apart: 15, of which 13 were waited for; matrix products, arithmetic and copies ran while one was open for 0% of the time, Pallas kernels for 1%

profile of v9, /device:TPU:0, one launch (start us, length us, event | category | flops | bytes accessed | tf_op | source)
XLA Modules:
  0.0 46.0 jit_solution(12591711995138729438)
XLA Ops:
  0.0 1.8 %log_terms.1 = (bf16[128,4096]{1,0:T(8,128)(2,1)S(1)}, bf16[128,4096]{1,0:T(8,128)(2,1)S(1)}) custom-call(bf16[128,4096]{1,0:T(8,128)(2,1)} %counts_hbm.1), custom_call_target="tpu_custom_call" | custom-call | flops 10485760 | bytes 4194304 | tf_op jit(solution)/shard_map/log_terms/pallas_call | solution.py:64
  3.8 0.9 %collective-permute-done = f32[64,128]{1,0:T(8,128)S(1)} collective-permute-done((f32[64,128]{1,0:T(8,128)S(1)}, f32[64,128]{1,0:T(8,128)S(1)}, u32[]{:S(2)}, u32[]{:S(2)}) %collective-permute-start) | collective-permute-done | bytes 32800 | tf_op jit(solution)/shard_map/ppermute | solution.py:333
  4.6 2.6 %collective-permute-start.1 = (f32[64,128]{1,0:T(8,128)S(1)}, f32[64,128]{1,0:T(8,128)S(1)}, u32[]{:S(2)}, u32[]{:S(2)}) collective-permute-start(f32[64,128]{1,0:T(8,128)S(1)} %add.21.refs_0_), channel_id=1, source_target_pairs={{0,3},{1,2},{2,1},{3,0},{4,7},{5,6},{6,5},{7,4},{8,11},{9,10},{10,... | collective-permute-start | bytes 98312 | tf_op jit(solution)/shard_map/ppermute | solution.py:333
  7.2 1.6 %collective-permute-done.1.refs_1_ = f32[64,128]{1,0:T(8,128)S(1)} collective-permute-done((f32[64,128]{1,0:T(8,128)S(1)}, f32[64,128]{1,0:T(8,128)S(1)}, u32[]{:S(2)}, u32[]{:S(2)}) %collective-permute-start.1) | collective-permute-done | bytes 32800 | tf_op jit(solution)/shard_map/ppermute | solution.py:333
  9.2 2.1 %collective-permute-start.2 = (f32[528,128]{1,0:T(8,128)S(1)}, f32[528,128]{1,0:T(8,128)S(1)}, u32[]{:S(2)}, u32[]{:S(2)}) collective-permute-start(f32[528,128]{1,0:T(8,128)S(1)} %get-tuple-element.34), channel_id=1, source_target_pairs={{0,8},{1,9},{2,10},{3,11},{4,12},{5,13},{6,14},{7,15},{8,0},{9,1},... | collective-permute-start | bytes 811016 | tf_op jit(solution)/shard_map/ppermute | solution.py:333
  11.3 1.5 %collective-permute-start.3 = (f32[264,128]{1,0:T(8,128)S(1)}, f32[264,128]{1,0:T(8,128)S(1)}, u32[]{:S(2)}, u32[]{:S(2)}) collective-permute-start(f32[264,128]{1,0:T(8,128)S(1)} %get-tuple-element.35), channel_id=1, source_target_pairs={{0,4},{1,5},{2,6},{3,7},{4,0},{5,1},{6,2},{7,3},{8,12},{9,13},{10,... | collective-permute-start | bytes 405512 | tf_op jit(solution)/shard_map/ppermute | solution.py:333
  12.8 2.4 %collective-permute-start.5 = (f32[264,128]{1,0:T(8,128)S(1)}, f32[264,128]{1,0:T(8,128)S(1)}, u32[]{:S(2)}, u32[]{:S(2)}) collective-permute-start(f32[264,128]{1,0:T(8,128)S(1)} %get-tuple-element.40), channel_id=1, source_target_pairs={{0,28},{1,29},{2,30},{3,31},{4,24},{5,25},{6,26},{7,27},{8,20},{9,... | collective-permute-start | bytes 405512 | tf_op jit(solution)/shard_map/ppermute | solution.py:333
  15.6 1.1 %collective-permute-done.3 = f32[264,128]{1,0:T(8,128)S(1)} collective-permute-done((f32[264,128]{1,0:T(8,128)S(1)}, f32[264,128]{1,0:T(8,128)S(1)}, u32[]{:S(2)}, u32[]{:S(2)}) %collective-permute-start.3) | collective-permute-done | bytes 135200 | tf_op jit(solution)/shard_map/ppermute | solution.py:333
  16.7 4.3 %collective-permute-start.6 = (f32[264,128]{1,0:T(8,128)S(1)}, f32[264,128]{1,0:T(8,128)S(1)}, u32[]{:S(2)}, u32[]{:S(2)}) collective-permute-start(f32[264,128]{1,0:T(8,128)S(1)} %get-tuple-element.41), channel_id=1, source_target_pairs={{0,12},{1,13},{2,14},{3,15},{4,8},{5,9},{6,10},{7,11},{8,4},{9,5},... | collective-permute-start | bytes 405512 | tf_op jit(solution)/shard_map/ppermute | solution.py:333
  21.0 1.5 %collective-permute-start.4 = (f32[264,128]{1,0:T(8,128)S(1)}, f32[264,128]{1,0:T(8,128)S(1)}, u32[]{:S(2)}, u32[]{:S(2)}) collective-permute-start(f32[264,128]{1,0:T(8,128)S(1)} %fusion), channel_id=1, source_target_pairs={{0,16},{1,17},{2,18},{3,19},{4,20},{5,21},{6,22},{7,23},{8,24},{9,... | collective-permute-start | bytes 405512 | tf_op jit(solution)/shard_map/ppermute | solution.py:333
  22.5 1.3 %collective-permute-start.7 = (f32[264,128]{1,0:T(8,128)S(1)}, f32[264,128]{1,0:T(8,128)S(1)}, u32[]{:S(2)}, u32[]{:S(2)}) collective-permute-start(f32[264,128]{1,0:T(8,128)S(1)} %get-tuple-element.42), channel_id=1, source_target_pairs={{0,4},{1,5},{2,6},{3,7},{4,0},{5,1},{6,2},{7,3},{8,12},{9,13},{10,... | collective-permute-start | bytes 405512 | tf_op jit(solution)/shard_map/ppermute | solution.py:333
  23.8 1.2 %collective-permute-done.5.refs_3_ = f32[264,128]{1,0:T(8,128)S(1)} collective-permute-done((f32[264,128]{1,0:T(8,128)S(1)}, f32[264,128]{1,0:T(8,128)S(1)}, u32[]{:S(2)}, u32[]{:S(2)}) %collective-permute-start.5) | collective-permute-done | bytes 135200 | tf_op jit(solution)/shard_map/ppermute | solution.py:333
  25.0 2.9 %collective-permute-done.6.refs_4_ = f32[264,128]{1,0:T(8,128)S(1)} collective-permute-done((f32[264,128]{1,0:T(8,128)S(1)}, f32[264,128]{1,0:T(8,128)S(1)}, u32[]{:S(2)}, u32[]{:S(2)}) %collective-permute-start.6) | collective-permute-done | bytes 135200 | tf_op jit(solution)/shard_map/ppermute | solution.py:333
  29.0 1.2 %collective-permute-done.8 = f32[32,128]{1,0:T(8,128)S(1)} collective-permute-done((f32[32,128]{1,0:T(8,128)S(1)}, f32[32,128]{1,0:T(8,128)S(1)}, u32[]{:S(2)}, u32[]{:S(2)}) %collective-permute-start.8) | collective-permute-done | bytes 16416 | tf_op jit(solution)/shard_map/ppermute | solution.py:333
  30.2 1.9 %collective-permute-start.11 = (f32[32,128]{1,0:T(8,128)S(1)}, f32[32,128]{1,0:T(8,128)S(1)}, u32[]{:S(2)}, u32[]{:S(2)}) collective-permute-start(f32[32,128]{1,0:T(8,128)S(1)} %add.24), channel_id=1, source_target_pairs={{0,7},{1,6},{2,5},{3,4},{4,3},{5,2},{6,1},{7,0},{8,15},{9,14},{10,... | collective-permute-start | bytes 49160 | tf_op jit(solution)/shard_map/ppermute | solution.py:333
  32.1 0.8 %collective-permute-start.10 = (f32[32,128]{1,0:T(8,128)S(1)}, f32[32,128]{1,0:T(8,128)S(1)}, u32[]{:S(2)}, u32[]{:S(2)}) collective-permute-start(f32[32,128]{1,0:T(8,128)S(1)} %add.24), channel_id=1, source_target_pairs={{0,5},{1,4},{2,7},{3,6},{4,1},{5,0},{6,3},{7,2},{8,13},{9,12},{10,... | collective-permute-start | bytes 49160 | tf_op jit(solution)/shard_map/ppermute | solution.py:333
  33.2 1.1 %collective-permute-done.11 = f32[32,128]{1,0:T(8,128)S(1)} collective-permute-done((f32[32,128]{1,0:T(8,128)S(1)}, f32[32,128]{1,0:T(8,128)S(1)}, u32[]{:S(2)}, u32[]{:S(2)}) %collective-permute-start.11) | collective-permute-done | bytes 16416 | tf_op jit(solution)/shard_map/ppermute | solution.py:333
  34.3 1.0 %collective-permute-done.10 = f32[32,128]{1,0:T(8,128)S(1)} collective-permute-done((f32[32,128]{1,0:T(8,128)S(1)}, f32[32,128]{1,0:T(8,128)S(1)}, u32[]{:S(2)}, u32[]{:S(2)}) %collective-permute-start.10) | collective-permute-done | bytes 16416 | tf_op jit(solution)/shard_map/ppermute | solution.py:333
  35.3 0.8 %collective-permute-done.9 = f32[32,128]{1,0:T(8,128)S(1)} collective-permute-done((f32[32,128]{1,0:T(8,128)S(1)}, f32[32,128]{1,0:T(8,128)S(1)}, u32[]{:S(2)}, u32[]{:S(2)}) %collective-permute-start.9) | collective-permute-done | bytes 16416 | tf_op jit(solution)/shard_map/ppermute | solution.py:333
  36.1 1.3 %collective-permute-start.14 = (f32[32,128]{1,0:T(8,128)S(1)}, f32[32,128]{1,0:T(8,128)S(1)}, u32[]{:S(2)}, u32[]{:S(2)}) collective-permute-start(f32[32,128]{1,0:T(8,128)S(1)} %add_add_fusion.gram_ref.refs_0_), channel_id=1, source_target_pairs={{0,17},{1,16},{2,19},{3,18},{4,21},{5,20},{6,23},{7,22},{8,25},{9,... | collective-permute-start | bytes 49160 | tf_op jit(solution)/shard_map/ppermute | solution.py:333
  37.4 2.9 %collective-permute-start.13 = (f32[32,128]{1,0:T(8,128)S(1)}, f32[32,128]{1,0:T(8,128)S(1)}, u32[]{:S(2)}, u32[]{:S(2)}) collective-permute-start(f32[32,128]{1,0:T(8,128)S(1)} %add_add_fusion.gram_ref.refs_0_), channel_id=1, source_target_pairs={{0,25},{1,24},{2,27},{3,26},{4,29},{5,28},{6,31},{7,30},{8,17},{9,... | collective-permute-start | bytes 49160 | tf_op jit(solution)/shard_map/ppermute | solution.py:333
  40.4 1.9 %collective-permute-done.13.refs_2_ = f32[32,128]{1,0:T(8,128)S(1)} collective-permute-done((f32[32,128]{1,0:T(8,128)S(1)}, f32[32,128]{1,0:T(8,128)S(1)}, u32[]{:S(2)}, u32[]{:S(2)}) %collective-permute-start.13) | collective-permute-done | bytes 16416 | tf_op jit(solution)/shard_map/ppermute | solution.py:333
  42.3 1.1 %collective-permute-done.12.refs_1_ = f32[32,128]{1,0:T(8,128)S(1)} collective-permute-done((f32[32,128]{1,0:T(8,128)S(1)}, f32[32,128]{1,0:T(8,128)S(1)}, u32[]{:S(2)}, u32[]{:S(2)}) %collective-permute-start.12) | collective-permute-done | bytes 16416 | tf_op jit(solution)/shard_map/ppermute | solution.py:333
  43.4 2.6 %orthonormal.1 = f32[64,512]{1,0:T(8,128)} custom-call(f32[32,128]{1,0:T(8,128)S(1)} %add_add_fusion.gram_ref.refs_0_, f32[32,128]{1,0:T(8,128)S(1)} %collective-permute-done.12.refs_1_, f32[32,128]{1,0:T(8,128)S(1)} %collective-permute-done.13.refs_2_, f32[32,128]{1,0:T(8,128)S(1)} %collective-permute-done.14.refs_3_, ...), custom_call_target="tpu_custom_call" | custom-call | tf_op jit(solution)/shard_map/orthonormal/pallas_call | solution.py:317
  (21 shorter events, 4.3 us)
Async XLA Ops:
  0.0 1.8 %copy-start = (bf16[64,4096]{1,0:T(8,128)(2,1)S(1)}, bf16[64,4096]{1,0:T(8,128)(2,1)}, u32[]{:S(2)}) copy-start(bf16[64,4096]{1,0:T(8,128)(2,1)} %basis_ref.1) | copy-start | bytes 1572868
  1.8 0.7 %copy-start.1 = (s32[1,32]{1,0:T(1,128)S(1)}, s32[1,32]{1,0:T(1,128)}, u32[]{:S(2)}) copy-start(s32[1,32]{1,0:T(1,128)} %occ_ref.1) | copy-start | bytes 388
  3.2 1.4 %collective-permute-start = (f32[64,128]{1,0:T(8,128)S(1)}, f32[64,128]{1,0:T(8,128)S(1)}, u32[]{:S(2)}, u32[]{:S(2)}) collective-permute-start(f32[64,128]{1,0:T(8,128)S(1)} %get-tuple-element.28), channel_id=1, source_target_pairs={{0,1},{1,0},{2,3},{3,2},{4,5},{5,4},{6,7},{7,6},{8,9},{9,8},{10,11... | collective-permute-start | bytes 98312 | tf_op jit(solution)/shard_map/ppermute | solution.py:333
  4.6 4.2 %collective-permute-start.1 = (f32[64,128]{1,0:T(8,128)S(1)}, f32[64,128]{1,0:T(8,128)S(1)}, u32[]{:S(2)}, u32[]{:S(2)}) collective-permute-start(f32[64,128]{1,0:T(8,128)S(1)} %add.21.refs_0_), channel_id=1, source_target_pairs={{0,3},{1,2},{2,1},{3,0},{4,7},{5,6},{6,5},{7,4},{8,11},{9,10},{10,... | collective-permute-start | bytes 98312 | tf_op jit(solution)/shard_map/ppermute | solution.py:333
  9.2 11.8 %collective-permute-start.2 = (f32[528,128]{1,0:T(8,128)S(1)}, f32[528,128]{1,0:T(8,128)S(1)}, u32[]{:S(2)}, u32[]{:S(2)}) collective-permute-start(f32[528,128]{1,0:T(8,128)S(1)} %get-tuple-element.34), channel_id=1, source_target_pairs={{0,8},{1,9},{2,10},{3,11},{4,12},{5,13},{6,14},{7,15},{8,0},{9,1},... | collective-permute-start | bytes 811016 | tf_op jit(solution)/shard_map/ppermute | solution.py:333
  11.3 5.4 %collective-permute-start.3 = (f32[264,128]{1,0:T(8,128)S(1)}, f32[264,128]{1,0:T(8,128)S(1)}, u32[]{:S(2)}, u32[]{:S(2)}) collective-permute-start(f32[264,128]{1,0:T(8,128)S(1)} %get-tuple-element.35), channel_id=1, source_target_pairs={{0,4},{1,5},{2,6},{3,7},{4,0},{5,1},{6,2},{7,3},{8,12},{9,13},{10,... | collective-permute-start | bytes 405512 | tf_op jit(solution)/shard_map/ppermute | solution.py:333
  12.8 12.2 %collective-permute-start.5 = (f32[264,128]{1,0:T(8,128)S(1)}, f32[264,128]{1,0:T(8,128)S(1)}, u32[]{:S(2)}, u32[]{:S(2)}) collective-permute-start(f32[264,128]{1,0:T(8,128)S(1)} %get-tuple-element.40), channel_id=1, source_target_pairs={{0,28},{1,29},{2,30},{3,31},{4,24},{5,25},{6,26},{7,27},{8,20},{9,... | collective-permute-start | bytes 405512 | tf_op jit(solution)/shard_map/ppermute | solution.py:333
  16.7 11.2 %collective-permute-start.6 = (f32[264,128]{1,0:T(8,128)S(1)}, f32[264,128]{1,0:T(8,128)S(1)}, u32[]{:S(2)}, u32[]{:S(2)}) collective-permute-start(f32[264,128]{1,0:T(8,128)S(1)} %get-tuple-element.41), channel_id=1, source_target_pairs={{0,12},{1,13},{2,14},{3,15},{4,8},{5,9},{6,10},{7,11},{8,4},{9,5},... | collective-permute-start | bytes 405512 | tf_op jit(solution)/shard_map/ppermute | solution.py:333
  21.0 7.4 %collective-permute-start.4 = (f32[264,128]{1,0:T(8,128)S(1)}, f32[264,128]{1,0:T(8,128)S(1)}, u32[]{:S(2)}, u32[]{:S(2)}) collective-permute-start(f32[264,128]{1,0:T(8,128)S(1)} %fusion), channel_id=1, source_target_pairs={{0,16},{1,17},{2,18},{3,19},{4,20},{5,21},{6,22},{7,23},{8,24},{9,... | collective-permute-start | bytes 405512 | tf_op jit(solution)/shard_map/ppermute | solution.py:333
  22.5 6.1 %collective-permute-start.7 = (f32[264,128]{1,0:T(8,128)S(1)}, f32[264,128]{1,0:T(8,128)S(1)}, u32[]{:S(2)}, u32[]{:S(2)}) collective-permute-start(f32[264,128]{1,0:T(8,128)S(1)} %get-tuple-element.42), channel_id=1, source_target_pairs={{0,4},{1,5},{2,6},{3,7},{4,0},{5,1},{6,2},{7,3},{8,12},{9,13},{10,... | collective-permute-start | bytes 405512 | tf_op jit(solution)/shard_map/ppermute | solution.py:333
  29.0 1.2 %collective-permute-start.8 = (f32[32,128]{1,0:T(8,128)S(1)}, f32[32,128]{1,0:T(8,128)S(1)}, u32[]{:S(2)}, u32[]{:S(2)}) collective-permute-start(f32[32,128]{1,0:T(8,128)S(1)} %get-tuple-element.43), channel_id=1, source_target_pairs={{0,1},{1,0},{2,3},{3,2},{4,5},{5,4},{6,7},{7,6},{8,9},{9,8},{10,11... | collective-permute-start | bytes 49160 | tf_op jit(solution)/shard_map/ppermute | solution.py:333
  30.2 4.1 %collective-permute-start.11 = (f32[32,128]{1,0:T(8,128)S(1)}, f32[32,128]{1,0:T(8,128)S(1)}, u32[]{:S(2)}, u32[]{:S(2)}) collective-permute-start(f32[32,128]{1,0:T(8,128)S(1)} %add.24), channel_id=1, source_target_pairs={{0,7},{1,6},{2,5},{3,4},{4,3},{5,2},{6,1},{7,0},{8,15},{9,14},{10,... | collective-permute-start | bytes 49160 | tf_op jit(solution)/shard_map/ppermute | solution.py:333
  32.1 3.2 %collective-permute-start.10 = (f32[32,128]{1,0:T(8,128)S(1)}, f32[32,128]{1,0:T(8,128)S(1)}, u32[]{:S(2)}, u32[]{:S(2)}) collective-permute-start(f32[32,128]{1,0:T(8,128)S(1)} %add.24), channel_id=1, source_target_pairs={{0,5},{1,4},{2,7},{3,6},{4,1},{5,0},{6,3},{7,2},{8,13},{9,12},{10,... | collective-permute-start | bytes 49160 | tf_op jit(solution)/shard_map/ppermute | solution.py:333
  32.9 3.2 %collective-permute-start.9 = (f32[32,128]{1,0:T(8,128)S(1)}, f32[32,128]{1,0:T(8,128)S(1)}, u32[]{:S(2)}, u32[]{:S(2)}) collective-permute-start(f32[32,128]{1,0:T(8,128)S(1)} %add.24), channel_id=1, source_target_pairs={{0,3},{1,2},{2,1},{3,0},{4,7},{5,6},{6,5},{7,4},{8,11},{9,10},{10,... | collective-permute-start | bytes 49160 | tf_op jit(solution)/shard_map/ppermute | solution.py:333
  36.1 4.4 %collective-permute-start.14 = (f32[32,128]{1,0:T(8,128)S(1)}, f32[32,128]{1,0:T(8,128)S(1)}, u32[]{:S(2)}, u32[]{:S(2)}) collective-permute-start(f32[32,128]{1,0:T(8,128)S(1)} %add_add_fusion.gram_ref.refs_0_), channel_id=1, source_target_pairs={{0,17},{1,16},{2,19},{3,18},{4,21},{5,20},{6,23},{7,22},{8,25},{9,... | collective-permute-start | bytes 49160 | tf_op jit(solution)/shard_map/ppermute | solution.py:333
  37.4 5.0 %collective-permute-start.13 = (f32[32,128]{1,0:T(8,128)S(1)}, f32[32,128]{1,0:T(8,128)S(1)}, u32[]{:S(2)}, u32[]{:S(2)}) collective-permute-start(f32[32,128]{1,0:T(8,128)S(1)} %add_add_fusion.gram_ref.refs_0_), channel_id=1, source_target_pairs={{0,25},{1,24},{2,27},{3,26},{4,29},{5,28},{6,31},{7,30},{8,17},{9,... | collective-permute-start | bytes 49160 | tf_op jit(solution)/shard_map/ppermute | solution.py:333
  40.2 3.2 %collective-permute-start.12 = (f32[32,128]{1,0:T(8,128)S(1)}, f32[32,128]{1,0:T(8,128)S(1)}, u32[]{:S(2)}, u32[]{:S(2)}) collective-permute-start(f32[32,128]{1,0:T(8,128)S(1)} %add_add_fusion.gram_ref.refs_0_), channel_id=1, source_target_pairs={{0,9},{1,8},{2,11},{3,10},{4,13},{5,12},{6,15},{7,14},{8,1},{9,0},... | collective-permute-start | bytes 49160 | tf_op jit(solution)/shard_map/ppermute | solution.py:333

commit v10 on v9

--- a/solution.py
+++ b/solution.py
@@ -340,8 +340,8 @@
 
 def all_terms(x):
     x = x + send(x, 0, 1)
-    across = [send(x, c, g) for c, g in ((1, 3), (1, 1), (0, 3))]
-    x = (x + across[2]) + (across[1] + across[0])
+    across = [send(x, c, g) for c, g in ((1, 1), (1, 3), (0, 3))]
+    x = (x + across[0]) + (across[1] + across[2])
     far, both, near = [send(x, c, 1) for c in (4, 6, 2)]
     return [x, near, both, far]
 

time: 46.1 us -> 45.8 us (level)
  no operation moved by 1% of the time
where the time goes in v10:
time: 45.8 us; the launch traced here: 45.7 us
  starting transfers between devices  23.4 us (51%)
  waiting for transfers between devices  15 us (33%)
  Pallas kernels  6.51 us (14%)
  local copies, waits for them, and re-layouts  0.64 us (1%)
    ppermute x15, starting transfers between devices, send(): return lax.ppermute(x, ('cells', 'genes'), pairs)  23.4 us
    ppermute x15, waiting for transfers between devices, send(): return lax.ppermute(x, ('cells', 'genes'), pairs)  15 us
    pallas_call x1, Pallas kernels, orthonormal(): pl.pallas_call(functools.partial(basis_kernel, scale), out_shape=jax.Shap...  2.6 us
    pallas_call x1, Pallas kernels, log_terms(): pl.pallas_call(functools.partial(log_kernel, width), out_shape=(jax.Shape...  1.81 us
  transfers between devices with their start and end apart: 15, of which 13 were waited for; matrix products, arithmetic and copies ran while one was open for 0% of the time, Pallas kernels for 1%

profile of v10, /device:TPU:0, one launch (start us, length us, event | category | flops | bytes accessed | tf_op | source)
XLA Modules:
  0.0 45.7 jit_solution(10829915661971266762)
XLA Ops:
  0.0 1.8 %log_terms.1 = (bf16[128,4096]{1,0:T(8,128)(2,1)S(1)}, bf16[128,4096]{1,0:T(8,128)(2,1)S(1)}) custom-call(bf16[128,4096]{1,0:T(8,128)(2,1)} %counts_hbm.1), custom_call_target="tpu_custom_call" | custom-call | flops 10485760 | bytes 4194304 | tf_op jit(solution)/shard_map/log_terms/pallas_call | solution.py:64
  1.8 0.6 %copy-done.1 = s32[1,32]{1,0:T(1,128)S(1)} copy-done((s32[1,32]{1,0:T(1,128)S(1)}, s32[1,32]{1,0:T(1,128)}, u32[]{:S(2)}) %copy-start.1) | copy-done | bytes 152
  2.5 0.8 %scores.1 = (f32[64,128]{1,0:T(8,128)S(1)}, f32[1,4096]{1,0:T(1,128)S(1)}) custom-call(s32[1,32]{1,0:T(1,128)S(1)} %copy-done.1, bf16[64,4096]{1,0:T(8,128)(2,1)S(1)} %copy-done, bf16[128,4096]{1,0:T(8,128)(2,1)S(1)} %get-tuple-element.26.high_ref.refs_2_, bf16[128,4096]{1,0:T(8,128)(2,1)S(1)} %get-tuple-element.27.low_ref.refs_3_), custom_call_target="tpu_custom_call" | custom-call | tf_op jit(solution)/shard_map/scores/pallas_call | solution.py:101
  3.8 0.9 %collective-permute-done = f32[64,128]{1,0:T(8,128)S(1)} collective-permute-done((f32[64,128]{1,0:T(8,128)S(1)}, f32[64,128]{1,0:T(8,128)S(1)}, u32[]{:S(2)}, u32[]{:S(2)}) %collective-permute-start) | collective-permute-done | bytes 32800 | tf_op jit(solution)/shard_map/ppermute | solution.py:333
  4.6 2.6 %collective-permute-start.1 = (f32[64,128]{1,0:T(8,128)S(1)}, f32[64,128]{1,0:T(8,128)S(1)}, u32[]{:S(2)}, u32[]{:S(2)}) collective-permute-start(f32[64,128]{1,0:T(8,128)S(1)} %add.21.refs_0_), channel_id=1, source_target_pairs={{0,3},{1,2},{2,1},{3,0},{4,7},{5,6},{6,5},{7,4},{8,11},{9,10},{10,... | collective-permute-start | bytes 98312 | tf_op jit(solution)/shard_map/ppermute | solution.py:333
  7.2 1.6 %collective-permute-done.1.refs_1_ = f32[64,128]{1,0:T(8,128)S(1)} collective-permute-done((f32[64,128]{1,0:T(8,128)S(1)}, f32[64,128]{1,0:T(8,128)S(1)}, u32[]{:S(2)}, u32[]{:S(2)}) %collective-permute-start.1) | collective-permute-done | bytes 32800 | tf_op jit(solution)/shard_map/ppermute | solution.py:333
  9.2 2.1 %collective-permute-start.2 = (f32[528,128]{1,0:T(8,128)S(1)}, f32[528,128]{1,0:T(8,128)S(1)}, u32[]{:S(2)}, u32[]{:S(2)}) collective-permute-start(f32[528,128]{1,0:T(8,128)S(1)} %get-tuple-element.34), channel_id=1, source_target_pairs={{0,8},{1,9},{2,10},{3,11},{4,12},{5,13},{6,14},{7,15},{8,0},{9,1},... | collective-permute-start | bytes 811016 | tf_op jit(solution)/shard_map/ppermute | solution.py:333
  11.3 1.5 %collective-permute-start.3 = (f32[264,128]{1,0:T(8,128)S(1)}, f32[264,128]{1,0:T(8,128)S(1)}, u32[]{:S(2)}, u32[]{:S(2)}) collective-permute-start(f32[264,128]{1,0:T(8,128)S(1)} %get-tuple-element.35), channel_id=1, source_target_pairs={{0,4},{1,5},{2,6},{3,7},{4,0},{5,1},{6,2},{7,3},{8,12},{9,13},{10,... | collective-permute-start | bytes 405512 | tf_op jit(solution)/shard_map/ppermute | solution.py:333
  12.8 2.4 %collective-permute-start.5 = (f32[264,128]{1,0:T(8,128)S(1)}, f32[264,128]{1,0:T(8,128)S(1)}, u32[]{:S(2)}, u32[]{:S(2)}) collective-permute-start(f32[264,128]{1,0:T(8,128)S(1)} %get-tuple-element.40), channel_id=1, source_target_pairs={{0,28},{1,29},{2,30},{3,31},{4,24},{5,25},{6,26},{7,27},{8,20},{9,... | collective-permute-start | bytes 405512 | tf_op jit(solution)/shard_map/ppermute | solution.py:333
  15.6 1.1 %collective-permute-done.3 = f32[264,128]{1,0:T(8,128)S(1)} collective-permute-done((f32[264,128]{1,0:T(8,128)S(1)}, f32[264,128]{1,0:T(8,128)S(1)}, u32[]{:S(2)}, u32[]{:S(2)}) %collective-permute-start.3) | collective-permute-done | bytes 135200 | tf_op jit(solution)/shard_map/ppermute | solution.py:333
  16.7 4.3 %collective-permute-start.6 = (f32[264,128]{1,0:T(8,128)S(1)}, f32[264,128]{1,0:T(8,128)S(1)}, u32[]{:S(2)}, u32[]{:S(2)}) collective-permute-start(f32[264,128]{1,0:T(8,128)S(1)} %get-tuple-element.41), channel_id=1, source_target_pairs={{0,12},{1,13},{2,14},{3,15},{4,8},{5,9},{6,10},{7,11},{8,4},{9,5},... | collective-permute-start | bytes 405512 | tf_op jit(solution)/shard_map/ppermute | solution.py:333
  21.0 1.5 %collective-permute-start.4 = (f32[264,128]{1,0:T(8,128)S(1)}, f32[264,128]{1,0:T(8,128)S(1)}, u32[]{:S(2)}, u32[]{:S(2)}) collective-permute-start(f32[264,128]{1,0:T(8,128)S(1)} %fusion), channel_id=1, source_target_pairs={{0,16},{1,17},{2,18},{3,19},{4,20},{5,21},{6,22},{7,23},{8,24},{9,... | collective-permute-start | bytes 405512 | tf_op jit(solution)/shard_map/ppermute | solution.py:333
  22.5 1.3 %collective-permute-start.7 = (f32[264,128]{1,0:T(8,128)S(1)}, f32[264,128]{1,0:T(8,128)S(1)}, u32[]{:S(2)}, u32[]{:S(2)}) collective-permute-start(f32[264,128]{1,0:T(8,128)S(1)} %get-tuple-element.42), channel_id=1, source_target_pairs={{0,4},{1,5},{2,6},{3,7},{4,0},{5,1},{6,2},{7,3},{8,12},{9,13},{10,... | collective-permute-start | bytes 405512 | tf_op jit(solution)/shard_map/ppermute | solution.py:333
  23.8 1.2 %collective-permute-done.5.refs_3_ = f32[264,128]{1,0:T(8,128)S(1)} collective-permute-done((f32[264,128]{1,0:T(8,128)S(1)}, f32[264,128]{1,0:T(8,128)S(1)}, u32[]{:S(2)}, u32[]{:S(2)}) %collective-permute-start.5) | collective-permute-done | bytes 135200 | tf_op jit(solution)/shard_map/ppermute | solution.py:333
  25.0 2.9 %collective-permute-done.6.refs_4_ = f32[264,128]{1,0:T(8,128)S(1)} collective-permute-done((f32[264,128]{1,0:T(8,128)S(1)}, f32[264,128]{1,0:T(8,128)S(1)}, u32[]{:S(2)}, u32[]{:S(2)}) %collective-permute-start.6) | collective-permute-done | bytes 135200 | tf_op jit(solution)/shard_map/ppermute | solution.py:333
  29.0 1.2 %collective-permute-done.8 = f32[32,128]{1,0:T(8,128)S(1)} collective-permute-done((f32[32,128]{1,0:T(8,128)S(1)}, f32[32,128]{1,0:T(8,128)S(1)}, u32[]{:S(2)}, u32[]{:S(2)}) %collective-permute-start.8) | collective-permute-done | bytes 16416 | tf_op jit(solution)/shard_map/ppermute | solution.py:333
  30.2 1.3 %collective-permute-start.11 = (f32[32,128]{1,0:T(8,128)S(1)}, f32[32,128]{1,0:T(8,128)S(1)}, u32[]{:S(2)}, u32[]{:S(2)}) collective-permute-start(f32[32,128]{1,0:T(8,128)S(1)} %add.24), channel_id=1, source_target_pairs={{0,3},{1,2},{2,1},{3,0},{4,7},{5,6},{6,5},{7,4},{8,11},{9,10},{10,... | collective-permute-start | bytes 49160 | tf_op jit(solution)/shard_map/ppermute | solution.py:333
  31.5 1.1 %collective-permute-start.10 = (f32[32,128]{1,0:T(8,128)S(1)}, f32[32,128]{1,0:T(8,128)S(1)}, u32[]{:S(2)}, u32[]{:S(2)}) collective-permute-start(f32[32,128]{1,0:T(8,128)S(1)} %add.24), channel_id=1, source_target_pairs={{0,7},{1,6},{2,5},{3,4},{4,3},{5,2},{6,1},{7,0},{8,15},{9,14},{10,... | collective-permute-start | bytes 49160 | tf_op jit(solution)/shard_map/ppermute | solution.py:333
  33.4 2.2 %collective-permute-done.10 = f32[32,128]{1,0:T(8,128)S(1)} collective-permute-done((f32[32,128]{1,0:T(8,128)S(1)}, f32[32,128]{1,0:T(8,128)S(1)}, u32[]{:S(2)}, u32[]{:S(2)}) %collective-permute-start.10) | collective-permute-done | bytes 16416 | tf_op jit(solution)/shard_map/ppermute | solution.py:333
  35.8 1.4 %collective-permute-start.14 = (f32[32,128]{1,0:T(8,128)S(1)}, f32[32,128]{1,0:T(8,128)S(1)}, u32[]{:S(2)}, u32[]{:S(2)}) collective-permute-start(f32[32,128]{1,0:T(8,128)S(1)} %add_add_fusion.gram_ref.refs_0_), channel_id=1, source_target_pairs={{0,17},{1,16},{2,19},{3,18},{4,21},{5,20},{6,23},{7,22},{8,25},{9,... | collective-permute-start | bytes 49160 | tf_op jit(solution)/shard_map/ppermute | solution.py:333
  37.2 2.7 %collective-permute-start.13 = (f32[32,128]{1,0:T(8,128)S(1)}, f32[32,128]{1,0:T(8,128)S(1)}, u32[]{:S(2)}, u32[]{:S(2)}) collective-permute-start(f32[32,128]{1,0:T(8,128)S(1)} %add_add_fusion.gram_ref.refs_0_), channel_id=1, source_target_pairs={{0,25},{1,24},{2,27},{3,26},{4,29},{5,28},{6,31},{7,30},{8,17},{9,... | collective-permute-start | bytes 49160 | tf_op jit(solution)/shard_map/ppermute | solution.py:333
  40.1 2.1 %collective-permute-done.13.refs_2_ = f32[32,128]{1,0:T(8,128)S(1)} collective-permute-done((f32[32,128]{1,0:T(8,128)S(1)}, f32[32,128]{1,0:T(8,128)S(1)}, u32[]{:S(2)}, u32[]{:S(2)}) %collective-permute-start.13) | collective-permute-done | bytes 16416 | tf_op jit(solution)/shard_map/ppermute | solution.py:333
  42.2 0.9 %collective-permute-done.12.refs_1_ = f32[32,128]{1,0:T(8,128)S(1)} collective-permute-done((f32[32,128]{1,0:T(8,128)S(1)}, f32[32,128]{1,0:T(8,128)S(1)}, u32[]{:S(2)}, u32[]{:S(2)}) %collective-permute-start.12) | collective-permute-done | bytes 16416 | tf_op jit(solution)/shard_map/ppermute | solution.py:333
  43.1 2.6 %orthonormal.1 = f32[64,512]{1,0:T(8,128)} custom-call(f32[32,128]{1,0:T(8,128)S(1)} %add_add_fusion.gram_ref.refs_0_, f32[32,128]{1,0:T(8,128)S(1)} %collective-permute-done.12.refs_1_, f32[32,128]{1,0:T(8,128)S(1)} %collective-permute-done.13.refs_2_, f32[32,128]{1,0:T(8,128)S(1)} %collective-permute-done.14.refs_3_, ...), custom_call_target="tpu_custom_call" | custom-call | tf_op jit(solution)/shard_map/orthonormal/pallas_call | solution.py:317
  (21 shorter events, 3.6 us)
Async XLA Ops:
  0.0 1.8 %copy-start = (bf16[64,4096]{1,0:T(8,128)(2,1)S(1)}, bf16[64,4096]{1,0:T(8,128)(2,1)}, u32[]{:S(2)}) copy-start(bf16[64,4096]{1,0:T(8,128)(2,1)} %basis_ref.1) | copy-start | bytes 1572868
  1.8 0.7 %copy-start.1 = (s32[1,32]{1,0:T(1,128)S(1)}, s32[1,32]{1,0:T(1,128)}, u32[]{:S(2)}) copy-start(s32[1,32]{1,0:T(1,128)} %occ_ref.1) | copy-start | bytes 388
  3.2 1.4 %collective-permute-start = (f32[64,128]{1,0:T(8,128)S(1)}, f32[64,128]{1,0:T(8,128)S(1)}, u32[]{:S(2)}, u32[]{:S(2)}) collective-permute-start(f32[64,128]{1,0:T(8,128)S(1)} %get-tuple-element.28), channel_id=1, source_target_pairs={{0,1},{1,0},{2,3},{3,2},{4,5},{5,4},{6,7},{7,6},{8,9},{9,8},{10,11... | collective-permute-start | bytes 98312 | tf_op jit(solution)/shard_map/ppermute | solution.py:333
  4.6 4.2 %collective-permute-start.1 = (f32[64,128]{1,0:T(8,128)S(1)}, f32[64,128]{1,0:T(8,128)S(1)}, u32[]{:S(2)}, u32[]{:S(2)}) collective-permute-start(f32[64,128]{1,0:T(8,128)S(1)} %add.21.refs_0_), channel_id=1, source_target_pairs={{0,3},{1,2},{2,1},{3,0},{4,7},{5,6},{6,5},{7,4},{8,11},{9,10},{10,... | collective-permute-start | bytes 98312 | tf_op jit(solution)/shard_map/ppermute | solution.py:333
  9.2 11.8 %collective-permute-start.2 = (f32[528,128]{1,0:T(8,128)S(1)}, f32[528,128]{1,0:T(8,128)S(1)}, u32[]{:S(2)}, u32[]{:S(2)}) collective-permute-start(f32[528,128]{1,0:T(8,128)S(1)} %get-tuple-element.34), channel_id=1, source_target_pairs={{0,8},{1,9},{2,10},{3,11},{4,12},{5,13},{6,14},{7,15},{8,0},{9,1},... | collective-permute-start | bytes 811016 | tf_op jit(solution)/shard_map/ppermute | solution.py:333
  11.3 5.4 %collective-permute-start.3 = (f32[264,128]{1,0:T(8,128)S(1)}, f32[264,128]{1,0:T(8,128)S(1)}, u32[]{:S(2)}, u32[]{:S(2)}) collective-permute-start(f32[264,128]{1,0:T(8,128)S(1)} %get-tuple-element.35), channel_id=1, source_target_pairs={{0,4},{1,5},{2,6},{3,7},{4,0},{5,1},{6,2},{7,3},{8,12},{9,13},{10,... | collective-permute-start | bytes 405512 | tf_op jit(solution)/shard_map/ppermute | solution.py:333
  12.8 12.2 %collective-permute-start.5 = (f32[264,128]{1,0:T(8,128)S(1)}, f32[264,128]{1,0:T(8,128)S(1)}, u32[]{:S(2)}, u32[]{:S(2)}) collective-permute-start(f32[264,128]{1,0:T(8,128)S(1)} %get-tuple-element.40), channel_id=1, source_target_pairs={{0,28},{1,29},{2,30},{3,31},{4,24},{5,25},{6,26},{7,27},{8,20},{9,... | collective-permute-start | bytes 405512 | tf_op jit(solution)/shard_map/ppermute | solution.py:333
  16.7 11.2 %collective-permute-start.6 = (f32[264,128]{1,0:T(8,128)S(1)}, f32[264,128]{1,0:T(8,128)S(1)}, u32[]{:S(2)}, u32[]{:S(2)}) collective-permute-start(f32[264,128]{1,0:T(8,128)S(1)} %get-tuple-element.41), channel_id=1, source_target_pairs={{0,12},{1,13},{2,14},{3,15},{4,8},{5,9},{6,10},{7,11},{8,4},{9,5},... | collective-permute-start | bytes 405512 | tf_op jit(solution)/shard_map/ppermute | solution.py:333
  21.0 7.4 %collective-permute-start.4 = (f32[264,128]{1,0:T(8,128)S(1)}, f32[264,128]{1,0:T(8,128)S(1)}, u32[]{:S(2)}, u32[]{:S(2)}) collective-permute-start(f32[264,128]{1,0:T(8,128)S(1)} %fusion), channel_id=1, source_target_pairs={{0,16},{1,17},{2,18},{3,19},{4,20},{5,21},{6,22},{7,23},{8,24},{9,... | collective-permute-start | bytes 405512 | tf_op jit(solution)/shard_map/ppermute | solution.py:333
  22.5 6.1 %collective-permute-start.7 = (f32[264,128]{1,0:T(8,128)S(1)}, f32[264,128]{1,0:T(8,128)S(1)}, u32[]{:S(2)}, u32[]{:S(2)}) collective-permute-start(f32[264,128]{1,0:T(8,128)S(1)} %get-tuple-element.42), channel_id=1, source_target_pairs={{0,4},{1,5},{2,6},{3,7},{4,0},{5,1},{6,2},{7,3},{8,12},{9,13},{10,... | collective-permute-start | bytes 405512 | tf_op jit(solution)/shard_map/ppermute | solution.py:333
  29.0 1.2 %collective-permute-start.8 = (f32[32,128]{1,0:T(8,128)S(1)}, f32[32,128]{1,0:T(8,128)S(1)}, u32[]{:S(2)}, u32[]{:S(2)}) collective-permute-start(f32[32,128]{1,0:T(8,128)S(1)} %get-tuple-element.43), channel_id=1, source_target_pairs={{0,1},{1,0},{2,3},{3,2},{4,5},{5,4},{6,7},{7,6},{8,9},{9,8},{10,11... | collective-permute-start | bytes 49160 | tf_op jit(solution)/shard_map/ppermute | solution.py:333
  30.2 3.2 %collective-permute-start.11 = (f32[32,128]{1,0:T(8,128)S(1)}, f32[32,128]{1,0:T(8,128)S(1)}, u32[]{:S(2)}, u32[]{:S(2)}) collective-permute-start(f32[32,128]{1,0:T(8,128)S(1)} %add.24), channel_id=1, source_target_pairs={{0,3},{1,2},{2,1},{3,0},{4,7},{5,6},{6,5},{7,4},{8,11},{9,10},{10,... | collective-permute-start | bytes 49160 | tf_op jit(solution)/shard_map/ppermute | solution.py:333
  31.5 4.1 %collective-permute-start.10 = (f32[32,128]{1,0:T(8,128)S(1)}, f32[32,128]{1,0:T(8,128)S(1)}, u32[]{:S(2)}, u32[]{:S(2)}) collective-permute-start(f32[32,128]{1,0:T(8,128)S(1)} %add.24), channel_id=1, source_target_pairs={{0,7},{1,6},{2,5},{3,4},{4,3},{5,2},{6,1},{7,0},{8,15},{9,14},{10,... | collective-permute-start | bytes 49160 | tf_op jit(solution)/shard_map/ppermute | solution.py:333
  32.6 3.2 %collective-permute-start.9 = (f32[32,128]{1,0:T(8,128)S(1)}, f32[32,128]{1,0:T(8,128)S(1)}, u32[]{:S(2)}, u32[]{:S(2)}) collective-permute-start(f32[32,128]{1,0:T(8,128)S(1)} %add.24), channel_id=1, source_target_pairs={{0,5},{1,4},{2,7},{3,6},{4,1},{5,0},{6,3},{7,2},{8,13},{9,12},{10,... | collective-permute-start | bytes 49160 | tf_op jit(solution)/shard_map/ppermute | solution.py:333
  35.8 4.3 %collective-permute-start.14 = (f32[32,128]{1,0:T(8,128)S(1)}, f32[32,128]{1,0:T(8,128)S(1)}, u32[]{:S(2)}, u32[]{:S(2)}) collective-permute-start(f32[32,128]{1,0:T(8,128)S(1)} %add_add_fusion.gram_ref.refs_0_), channel_id=1, source_target_pairs={{0,17},{1,16},{2,19},{3,18},{4,21},{5,20},{6,23},{7,22},{8,25},{9,... | collective-permute-start | bytes 49160 | tf_op jit(solution)/shard_map/ppermute | solution.py:333
  37.2 5.0 %collective-permute-start.13 = (f32[32,128]{1,0:T(8,128)S(1)}, f32[32,128]{1,0:T(8,128)S(1)}, u32[]{:S(2)}, u32[]{:S(2)}) collective-permute-start(f32[32,128]{1,0:T(8,128)S(1)} %add_add_fusion.gram_ref.refs_0_), channel_id=1, source_target_pairs={{0,25},{1,24},{2,27},{3,26},{4,29},{5,28},{6,31},{7,30},{8,17},{9,... | collective-permute-start | bytes 49160 | tf_op jit(solution)/shard_map/ppermute | solution.py:333
  39.9 3.2 %collective-permute-start.12 = (f32[32,128]{1,0:T(8,128)S(1)}, f32[32,128]{1,0:T(8,128)S(1)}, u32[]{:S(2)}, u32[]{:S(2)}) collective-permute-start(f32[32,128]{1,0:T(8,128)S(1)} %add_add_fusion.gram_ref.refs_0_), channel_id=1, source_target_pairs={{0,9},{1,8},{2,11},{3,10},{4,13},{5,12},{6,15},{7,14},{8,1},{9,0},... | collective-permute-start | bytes 49160 | tf_op jit(solution)/shard_map/ppermute | solution.py:333

commit v11 on v10

--- a/solution.py
+++ b/solution.py
@@ -340,7 +340,7 @@
 
 def all_terms(x):
     x = x + send(x, 0, 1)
-    across = [send(x, c, g) for c, g in ((1, 1), (1, 3), (0, 3))]
+    across = [send(x, c, g) for c, g in ((0, 3), (1, 3), (1, 1))]
     x = (x + across[0]) + (across[1] + across[2])
     far, both, near = [send(x, c, 1) for c in (4, 6, 2)]
     return [x, near, both, far]

time: 45.8 us -> 46.1 us (level)
  no operation moved by 1% of the time
where the time goes in v11:
time: 46.1 us; the launch traced here: 46 us
  starting transfers between devices  23.4 us (51%)
  waiting for transfers between devices  15.3 us (33%)
  Pallas kernels  6.51 us (14%)
  local copies, waits for them, and re-layouts  0.64 us (1%)
    ppermute x15, starting transfers between devices, send(): return lax.ppermute(x, ('cells', 'genes'), pairs)  23.4 us
    ppermute x15, waiting for transfers between devices, send(): return lax.ppermute(x, ('cells', 'genes'), pairs)  15.3 us
    pallas_call x1, Pallas kernels, orthonormal(): pl.pallas_call(functools.partial(basis_kernel, scale), out_shape=jax.Shap...  2.6 us
    pallas_call x1, Pallas kernels, log_terms(): pl.pallas_call(functools.partial(log_kernel, width), out_shape=(jax.Shape...  1.81 us
  transfers between devices with their start and end apart: 15, of which 13 were waited for; matrix products, arithmetic and copies ran while one was open for 0% of the time, Pallas kernels for 1%

profile of v11, /device:TPU:0, one launch (start us, length us, event | category | flops | bytes accessed | tf_op | source)
XLA Modules:
  0.0 46.0 jit_solution(13028853658067292803)
XLA Ops:
  0.0 1.8 %log_terms.1 = (bf16[128,4096]{1,0:T(8,128)(2,1)S(1)}, bf16[128,4096]{1,0:T(8,128)(2,1)S(1)}) custom-call(bf16[128,4096]{1,0:T(8,128)(2,1)} %counts_hbm.1), custom_call_target="tpu_custom_call" | custom-call | flops 10485760 | bytes 4194304 | tf_op jit(solution)/shard_map/log_terms/pallas_call | solution.py:64
  2.5 0.8 %scores.1 = (f32[64,128]{1,0:T(8,128)S(1)}, f32[1,4096]{1,0:T(1,128)S(1)}) custom-call(s32[1,32]{1,0:T(1,128)S(1)} %copy-done.1, bf16[64,4096]{1,0:T(8,128)(2,1)S(1)} %copy-done, bf16[128,4096]{1,0:T(8,128)(2,1)S(1)} %get-tuple-element.26.high_ref.refs_2_, bf16[128,4096]{1,0:T(8,128)(2,1)S(1)} %get-tuple-element.27.low_ref.refs_3_), custom_call_target="tpu_custom_call" | custom-call | tf_op jit(solution)/shard_map/scores/pallas_call | solution.py:101
  3.8 0.9 %collective-permute-done = f32[64,128]{1,0:T(8,128)S(1)} collective-permute-done((f32[64,128]{1,0:T(8,128)S(1)}, f32[64,128]{1,0:T(8,128)S(1)}, u32[]{:S(2)}, u32[]{:S(2)}) %collective-permute-start) | collective-permute-done | bytes 32800 | tf_op jit(solution)/shard_map/ppermute | solution.py:333
  4.6 2.6 %collective-permute-start.1 = (f32[64,128]{1,0:T(8,128)S(1)}, f32[64,128]{1,0:T(8,128)S(1)}, u32[]{:S(2)}, u32[]{:S(2)}) collective-permute-start(f32[64,128]{1,0:T(8,128)S(1)} %add.21.refs_0_), channel_id=1, source_target_pairs={{0,3},{1,2},{2,1},{3,0},{4,7},{5,6},{6,5},{7,4},{8,11},{9,10},{10,... | collective-permute-start | bytes 98312 | tf_op jit(solution)/shard_map/ppermute | solution.py:333
  7.2 1.6 %collective-permute-done.1.refs_1_ = f32[64,128]{1,0:T(8,128)S(1)} collective-permute-done((f32[64,128]{1,0:T(8,128)S(1)}, f32[64,128]{1,0:T(8,128)S(1)}, u32[]{:S(2)}, u32[]{:S(2)}) %collective-permute-start.1) | collective-permute-done | bytes 32800 | tf_op jit(solution)/shard_map/ppermute | solution.py:333
  9.2 2.1 %collective-permute-start.2 = (f32[528,128]{1,0:T(8,128)S(1)}, f32[528,128]{1,0:T(8,128)S(1)}, u32[]{:S(2)}, u32[]{:S(2)}) collective-permute-start(f32[528,128]{1,0:T(8,128)S(1)} %get-tuple-element.34), channel_id=1, source_target_pairs={{0,8},{1,9},{2,10},{3,11},{4,12},{5,13},{6,14},{7,15},{8,0},{9,1},... | collective-permute-start | bytes 811016 | tf_op jit(solution)/shard_map/ppermute | solution.py:333
  11.3 1.5 %collective-permute-start.3 = (f32[264,128]{1,0:T(8,128)S(1)}, f32[264,128]{1,0:T(8,128)S(1)}, u32[]{:S(2)}, u32[]{:S(2)}) collective-permute-start(f32[264,128]{1,0:T(8,128)S(1)} %get-tuple-element.35), channel_id=1, source_target_pairs={{0,4},{1,5},{2,6},{3,7},{4,0},{5,1},{6,2},{7,3},{8,12},{9,13},{10,... | collective-permute-start | bytes 405512 | tf_op jit(solution)/shard_map/ppermute | solution.py:333
  12.8 2.4 %collective-permute-start.5 = (f32[264,128]{1,0:T(8,128)S(1)}, f32[264,128]{1,0:T(8,128)S(1)}, u32[]{:S(2)}, u32[]{:S(2)}) collective-permute-start(f32[264,128]{1,0:T(8,128)S(1)} %get-tuple-element.40), channel_id=1, source_target_pairs={{0,28},{1,29},{2,30},{3,31},{4,24},{5,25},{6,26},{7,27},{8,20},{9,... | collective-permute-start | bytes 405512 | tf_op jit(solution)/shard_map/ppermute | solution.py:333
  15.6 1.1 %collective-permute-done.3 = f32[264,128]{1,0:T(8,128)S(1)} collective-permute-done((f32[264,128]{1,0:T(8,128)S(1)}, f32[264,128]{1,0:T(8,128)S(1)}, u32[]{:S(2)}, u32[]{:S(2)}) %collective-permute-start.3) | collective-permute-done | bytes 135200 | tf_op jit(solution)/shard_map/ppermute | solution.py:333
  16.7 4.3 %collective-permute-start.6 = (f32[264,128]{1,0:T(8,128)S(1)}, f32[264,128]{1,0:T(8,128)S(1)}, u32[]{:S(2)}, u32[]{:S(2)}) collective-permute-start(f32[264,128]{1,0:T(8,128)S(1)} %get-tuple-element.41), channel_id=1, source_target_pairs={{0,12},{1,13},{2,14},{3,15},{4,8},{5,9},{6,10},{7,11},{8,4},{9,5},... | collective-permute-start | bytes 405512 | tf_op jit(solution)/shard_map/ppermute | solution.py:333
  21.0 1.5 %collective-permute-start.4 = (f32[264,128]{1,0:T(8,128)S(1)}, f32[264,128]{1,0:T(8,128)S(1)}, u32[]{:S(2)}, u32[]{:S(2)}) collective-permute-start(f32[264,128]{1,0:T(8,128)S(1)} %fusion), channel_id=1, source_target_pairs={{0,16},{1,17},{2,18},{3,19},{4,20},{5,21},{6,22},{7,23},{8,24},{9,... | collective-permute-start | bytes 405512 | tf_op jit(solution)/shard_map/ppermute | solution.py:333
  22.5 1.3 %collective-permute-start.7 = (f32[264,128]{1,0:T(8,128)S(1)}, f32[264,128]{1,0:T(8,128)S(1)}, u32[]{:S(2)}, u32[]{:S(2)}) collective-permute-start(f32[264,128]{1,0:T(8,128)S(1)} %get-tuple-element.42), channel_id=1, source_target_pairs={{0,4},{1,5},{2,6},{3,7},{4,0},{5,1},{6,2},{7,3},{8,12},{9,13},{10,... | collective-permute-start | bytes 405512 | tf_op jit(solution)/shard_map/ppermute | solution.py:333
  23.8 1.2 %collective-permute-done.5.refs_3_ = f32[264,128]{1,0:T(8,128)S(1)} collective-permute-done((f32[264,128]{1,0:T(8,128)S(1)}, f32[264,128]{1,0:T(8,128)S(1)}, u32[]{:S(2)}, u32[]{:S(2)}) %collective-permute-start.5) | collective-permute-done | bytes 135200 | tf_op jit(solution)/shard_map/ppermute | solution.py:333
  25.0 2.9 %collective-permute-done.6.refs_4_ = f32[264,128]{1,0:T(8,128)S(1)} collective-permute-done((f32[264,128]{1,0:T(8,128)S(1)}, f32[264,128]{1,0:T(8,128)S(1)}, u32[]{:S(2)}, u32[]{:S(2)}) %collective-permute-start.6) | collective-permute-done | bytes 135200 | tf_op jit(solution)/shard_map/ppermute | solution.py:333
  29.0 1.2 %collective-permute-done.8 = f32[32,128]{1,0:T(8,128)S(1)} collective-permute-done((f32[32,128]{1,0:T(8,128)S(1)}, f32[32,128]{1,0:T(8,128)S(1)}, u32[]{:S(2)}, u32[]{:S(2)}) %collective-permute-start.8) | collective-permute-done | bytes 16416 | tf_op jit(solution)/shard_map/ppermute | solution.py:333
  30.2 1.0 %collective-permute-start.11 = (f32[32,128]{1,0:T(8,128)S(1)}, f32[32,128]{1,0:T(8,128)S(1)}, u32[]{:S(2)}, u32[]{:S(2)}) collective-permute-start(f32[32,128]{1,0:T(8,128)S(1)} %add.24), channel_id=1, source_target_pairs={{0,5},{1,4},{2,7},{3,6},{4,1},{5,0},{6,3},{7,2},{8,13},{9,12},{10,... | collective-permute-start | bytes 49160 | tf_op jit(solution)/shard_map/ppermute | solution.py:333
  31.2 1.7 %collective-permute-start.10 = (f32[32,128]{1,0:T(8,128)S(1)}, f32[32,128]{1,0:T(8,128)S(1)}, u32[]{:S(2)}, u32[]{:S(2)}) collective-permute-start(f32[32,128]{1,0:T(8,128)S(1)} %add.24), channel_id=1, source_target_pairs={{0,7},{1,6},{2,5},{3,4},{4,3},{5,2},{6,1},{7,0},{8,15},{9,14},{10,... | collective-permute-start | bytes 49160 | tf_op jit(solution)/shard_map/ppermute | solution.py:333
  33.4 1.9 %collective-permute-done.10 = f32[32,128]{1,0:T(8,128)S(1)} collective-permute-done((f32[32,128]{1,0:T(8,128)S(1)}, f32[32,128]{1,0:T(8,128)S(1)}, u32[]{:S(2)}, u32[]{:S(2)}) %collective-permute-start.10) | collective-permute-done | bytes 16416 | tf_op jit(solution)/shard_map/ppermute | solution.py:333
  35.3 0.8 %collective-permute-done.9 = f32[32,128]{1,0:T(8,128)S(1)} collective-permute-done((f32[32,128]{1,0:T(8,128)S(1)}, f32[32,128]{1,0:T(8,128)S(1)}, u32[]{:S(2)}, u32[]{:S(2)}) %collective-permute-start.9) | collective-permute-done | bytes 16416 | tf_op jit(solution)/shard_map/ppermute | solution.py:333
  36.1 1.3 %collective-permute-start.14 = (f32[32,128]{1,0:T(8,128)S(1)}, f32[32,128]{1,0:T(8,128)S(1)}, u32[]{:S(2)}, u32[]{:S(2)}) collective-permute-start(f32[32,128]{1,0:T(8,128)S(1)} %add_add_fusion.gram_ref.refs_0_), channel_id=1, source_target_pairs={{0,17},{1,16},{2,19},{3,18},{4,21},{5,20},{6,23},{7,22},{8,25},{9,... | collective-permute-start | bytes 49160 | tf_op jit(solution)/shard_map/ppermute | solution.py:333
  37.4 2.9 %collective-permute-start.13 = (f32[32,128]{1,0:T(8,128)S(1)}, f32[32,128]{1,0:T(8,128)S(1)}, u32[]{:S(2)}, u32[]{:S(2)}) collective-permute-start(f32[32,128]{1,0:T(8,128)S(1)} %add_add_fusion.gram_ref.refs_0_), channel_id=1, source_target_pairs={{0,25},{1,24},{2,27},{3,26},{4,29},{5,28},{6,31},{7,30},{8,17},{9,... | collective-permute-start | bytes 49160 | tf_op jit(solution)/shard_map/ppermute | solution.py:333
  40.4 1.9 %collective-permute-done.13.refs_2_ = f32[32,128]{1,0:T(8,128)S(1)} collective-permute-done((f32[32,128]{1,0:T(8,128)S(1)}, f32[32,128]{1,0:T(8,128)S(1)}, u32[]{:S(2)}, u32[]{:S(2)}) %collective-permute-start.13) | collective-permute-done | bytes 16416 | tf_op jit(solution)/shard_map/ppermute | solution.py:333
  42.3 1.1 %collective-permute-done.12.refs_1_ = f32[32,128]{1,0:T(8,128)S(1)} collective-permute-done((f32[32,128]{1,0:T(8,128)S(1)}, f32[32,128]{1,0:T(8,128)S(1)}, u32[]{:S(2)}, u32[]{:S(2)}) %collective-permute-start.12) | collective-permute-done | bytes 16416 | tf_op jit(solution)/shard_map/ppermute | solution.py:333
  43.4 2.6 %orthonormal.1 = f32[64,512]{1,0:T(8,128)} custom-call(f32[32,128]{1,0:T(8,128)S(1)} %add_add_fusion.gram_ref.refs_0_, f32[32,128]{1,0:T(8,128)S(1)} %collective-permute-done.12.refs_1_, f32[32,128]{1,0:T(8,128)S(1)} %collective-permute-done.13.refs_2_, f32[32,128]{1,0:T(8,128)S(1)} %collective-permute-done.14.refs_3_, ...), custom_call_target="tpu_custom_call" | custom-call | tf_op jit(solution)/shard_map/orthonormal/pallas_call | solution.py:317
  (21 shorter events, 3.7 us)
Async XLA Ops:
  0.0 1.8 %copy-start = (bf16[64,4096]{1,0:T(8,128)(2,1)S(1)}, bf16[64,4096]{1,0:T(8,128)(2,1)}, u32[]{:S(2)}) copy-start(bf16[64,4096]{1,0:T(8,128)(2,1)} %basis_ref.1) | copy-start | bytes 1572868
  1.8 0.7 %copy-start.1 = (s32[1,32]{1,0:T(1,128)S(1)}, s32[1,32]{1,0:T(1,128)}, u32[]{:S(2)}) copy-start(s32[1,32]{1,0:T(1,128)} %occ_ref.1) | copy-start | bytes 388
  3.2 1.4 %collective-permute-start = (f32[64,128]{1,0:T(8,128)S(1)}, f32[64,128]{1,0:T(8,128)S(1)}, u32[]{:S(2)}, u32[]{:S(2)}) collective-permute-start(f32[64,128]{1,0:T(8,128)S(1)} %get-tuple-element.28), channel_id=1, source_target_pairs={{0,1},{1,0},{2,3},{3,2},{4,5},{5,4},{6,7},{7,6},{8,9},{9,8},{10,11... | collective-permute-start | bytes 98312 | tf_op jit(solution)/shard_map/ppermute | solution.py:333
  4.6 4.2 %collective-permute-start.1 = (f32[64,128]{1,0:T(8,128)S(1)}, f32[64,128]{1,0:T(8,128)S(1)}, u32[]{:S(2)}, u32[]{:S(2)}) collective-permute-start(f32[64,128]{1,0:T(8,128)S(1)} %add.21.refs_0_), channel_id=1, source_target_pairs={{0,3},{1,2},{2,1},{3,0},{4,7},{5,6},{6,5},{7,4},{8,11},{9,10},{10,... | collective-permute-start | bytes 98312 | tf_op jit(solution)/shard_map/ppermute | solution.py:333
  9.2 11.8 %collective-permute-start.2 = (f32[528,128]{1,0:T(8,128)S(1)}, f32[528,128]{1,0:T(8,128)S(1)}, u32[]{:S(2)}, u32[]{:S(2)}) collective-permute-start(f32[528,128]{1,0:T(8,128)S(1)} %get-tuple-element.34), channel_id=1, source_target_pairs={{0,8},{1,9},{2,10},{3,11},{4,12},{5,13},{6,14},{7,15},{8,0},{9,1},... | collective-permute-start | bytes 811016 | tf_op jit(solution)/shard_map/ppermute | solution.py:333
  11.3 5.4 %collective-permute-start.3 = (f32[264,128]{1,0:T(8,128)S(1)}, f32[264,128]{1,0:T(8,128)S(1)}, u32[]{:S(2)}, u32[]{:S(2)}) collective-permute-start(f32[264,128]{1,0:T(8,128)S(1)} %get-tuple-element.35), channel_id=1, source_target_pairs={{0,4},{1,5},{2,6},{3,7},{4,0},{5,1},{6,2},{7,3},{8,12},{9,13},{10,... | collective-permute-start | bytes 405512 | tf_op jit(solution)/shard_map/ppermute | solution.py:333
  12.8 12.2 %collective-permute-start.5 = (f32[264,128]{1,0:T(8,128)S(1)}, f32[264,128]{1,0:T(8,128)S(1)}, u32[]{:S(2)}, u32[]{:S(2)}) collective-permute-start(f32[264,128]{1,0:T(8,128)S(1)} %get-tuple-element.40), channel_id=1, source_target_pairs={{0,28},{1,29},{2,30},{3,31},{4,24},{5,25},{6,26},{7,27},{8,20},{9,... | collective-permute-start | bytes 405512 | tf_op jit(solution)/shard_map/ppermute | solution.py:333
  16.7 11.2 %collective-permute-start.6 = (f32[264,128]{1,0:T(8,128)S(1)}, f32[264,128]{1,0:T(8,128)S(1)}, u32[]{:S(2)}, u32[]{:S(2)}) collective-permute-start(f32[264,128]{1,0:T(8,128)S(1)} %get-tuple-element.41), channel_id=1, source_target_pairs={{0,12},{1,13},{2,14},{3,15},{4,8},{5,9},{6,10},{7,11},{8,4},{9,5},... | collective-permute-start | bytes 405512 | tf_op jit(solution)/shard_map/ppermute | solution.py:333
  21.0 7.4 %collective-permute-start.4 = (f32[264,128]{1,0:T(8,128)S(1)}, f32[264,128]{1,0:T(8,128)S(1)}, u32[]{:S(2)}, u32[]{:S(2)}) collective-permute-start(f32[264,128]{1,0:T(8,128)S(1)} %fusion), channel_id=1, source_target_pairs={{0,16},{1,17},{2,18},{3,19},{4,20},{5,21},{6,22},{7,23},{8,24},{9,... | collective-permute-start | bytes 405512 | tf_op jit(solution)/shard_map/ppermute | solution.py:333
  22.5 6.1 %collective-permute-start.7 = (f32[264,128]{1,0:T(8,128)S(1)}, f32[264,128]{1,0:T(8,128)S(1)}, u32[]{:S(2)}, u32[]{:S(2)}) collective-permute-start(f32[264,128]{1,0:T(8,128)S(1)} %get-tuple-element.42), channel_id=1, source_target_pairs={{0,4},{1,5},{2,6},{3,7},{4,0},{5,1},{6,2},{7,3},{8,12},{9,13},{10,... | collective-permute-start | bytes 405512 | tf_op jit(solution)/shard_map/ppermute | solution.py:333
  29.0 1.2 %collective-permute-start.8 = (f32[32,128]{1,0:T(8,128)S(1)}, f32[32,128]{1,0:T(8,128)S(1)}, u32[]{:S(2)}, u32[]{:S(2)}) collective-permute-start(f32[32,128]{1,0:T(8,128)S(1)} %get-tuple-element.43), channel_id=1, source_target_pairs={{0,1},{1,0},{2,3},{3,2},{4,5},{5,4},{6,7},{7,6},{8,9},{9,8},{10,11... | collective-permute-start | bytes 49160 | tf_op jit(solution)/shard_map/ppermute | solution.py:333
  30.2 3.2 %collective-permute-start.11 = (f32[32,128]{1,0:T(8,128)S(1)}, f32[32,128]{1,0:T(8,128)S(1)}, u32[]{:S(2)}, u32[]{:S(2)}) collective-permute-start(f32[32,128]{1,0:T(8,128)S(1)} %add.24), channel_id=1, source_target_pairs={{0,5},{1,4},{2,7},{3,6},{4,1},{5,0},{6,3},{7,2},{8,13},{9,12},{10,... | collective-permute-start | bytes 49160 | tf_op jit(solution)/shard_map/ppermute | solution.py:333
  31.2 4.1 %collective-permute-start.10 = (f32[32,128]{1,0:T(8,128)S(1)}, f32[32,128]{1,0:T(8,128)S(1)}, u32[]{:S(2)}, u32[]{:S(2)}) collective-permute-start(f32[32,128]{1,0:T(8,128)S(1)} %add.24), channel_id=1, source_target_pairs={{0,7},{1,6},{2,5},{3,4},{4,3},{5,2},{6,1},{7,0},{8,15},{9,14},{10,... | collective-permute-start | bytes 49160 | tf_op jit(solution)/shard_map/ppermute | solution.py:333
  32.9 3.2 %collective-permute-start.9 = (f32[32,128]{1,0:T(8,128)S(1)}, f32[32,128]{1,0:T(8,128)S(1)}, u32[]{:S(2)}, u32[]{:S(2)}) collective-permute-start(f32[32,128]{1,0:T(8,128)S(1)} %add.24), channel_id=1, source_target_pairs={{0,3},{1,2},{2,1},{3,0},{4,7},{5,6},{6,5},{7,4},{8,11},{9,10},{10,... | collective-permute-start | bytes 49160 | tf_op jit(solution)/shard_map/ppermute | solution.py:333
  36.1 4.4 %collective-permute-start.14 = (f32[32,128]{1,0:T(8,128)S(1)}, f32[32,128]{1,0:T(8,128)S(1)}, u32[]{:S(2)}, u32[]{:S(2)}) collective-permute-start(f32[32,128]{1,0:T(8,128)S(1)} %add_add_fusion.gram_ref.refs_0_), channel_id=1, source_target_pairs={{0,17},{1,16},{2,19},{3,18},{4,21},{5,20},{6,23},{7,22},{8,25},{9,... | collective-permute-start | bytes 49160 | tf_op jit(solution)/shard_map/ppermute | solution.py:333
  37.4 5.0 %collective-permute-start.13 = (f32[32,128]{1,0:T(8,128)S(1)}, f32[32,128]{1,0:T(8,128)S(1)}, u32[]{:S(2)}, u32[]{:S(2)}) collective-permute-start(f32[32,128]{1,0:T(8,128)S(1)} %add_add_fusion.gram_ref.refs_0_), channel_id=1, source_target_pairs={{0,25},{1,24},{2,27},{3,26},{4,29},{5,28},{6,31},{7,30},{8,17},{9,... | collective-permute-start | bytes 49160 | tf_op jit(solution)/shard_map/ppermute | solution.py:333
  40.2 3.2 %collective-permute-start.12 = (f32[32,128]{1,0:T(8,128)S(1)}, f32[32,128]{1,0:T(8,128)S(1)}, u32[]{:S(2)}, u32[]{:S(2)}) collective-permute-start(f32[32,128]{1,0:T(8,128)S(1)} %add_add_fusion.gram_ref.refs_0_), channel_id=1, source_target_pairs={{0,9},{1,8},{2,11},{3,10},{4,13},{5,12},{6,15},{7,14},{8,1},{9,0},... | collective-permute-start | bytes 49160 | tf_op jit(solution)/shard_map/ppermute | solution.py:333
